TPU v7x, 32 devices: a whole 2x2x4 slice. The times are simulated.
32 devices in a mesh: grp: 2 (over y), tmpl: 4 (over z), slab: 2 (over x), sub: 2 (over core).
Axes of the slice: x: 2, y: 2, z: 4, core: 2. Of those that a mesh axis runs over, the one named last changes fastest.
Arguments:
- records: bfloat16 [256, 3, 1024], P(('grp', 'tmpl'), None, 'slab'), parts along dimension 0, may hold values from -6 to 6
- owner_slots: int32 [256], P(('grp', 'tmpl')), parts along dimension 0, may hold values from 0 to 127, each once
- gap_start: int32 [256, 4], P('grp'), parts along dimension 0, may hold values from 0 to 1023
- gap_len: int32 [256, 4], P('grp'), parts along dimension 0, may hold values from 1 to 127
- templates: bfloat16 [64, 20, 3, 300], P(('grp', 'tmpl', 'slab'), 'sub'), parts along dimension 0, may hold values from -6 to 6
- station_ids: int32 [64, 20], P(('grp', 'tmpl', 'slab'), 'sub'), parts along dimension 0, may hold values from 0 to 127, all different within a row
- offsets: int32 [64, 20], P(('grp', 'tmpl', 'slab'), 'sub'), parts along dimension 0, may hold values from 0 to 200
Outputs:
- stack: float32 [64, 1024], P(('grp', 'tmpl'), ('slab', 'sub')), parts along dimension 0
There are 2 independent parts, one for each index of `grp`. A program takes and returns all parts, laid end to end along the dimension named above; each array names one. Nothing has to cross between parts.
Inputs may be any that keep to these rules, and one draw needn't show every extreme that they name: `station_ids`: the 20 stations of one template are distinct. `owner_slots`: each station is held by exactly one slot.
All inputs are finite; a program needn't handle non-finite values.
Results may differ from a plain program's by a relative error of at most 0.0003.
Values may be sent and summed in bfloat16 or wider, within the bound.
No kernel may reach another device: no remote copies, remote signals or barrier semaphores. Data moves between devices by JAX's collectives and lax.ppermute only.
A program may use at most 192 MiB of HBM per device.

v0:
```python
import jax
import jax.numpy as jnp
from jax import lax
from jax.sharding import PartitionSpec as P

OFFMAX = 200


def shifted(block, axis, distance):
    devices = range(lax.axis_size(axis))
    route = [(i - distance, i) for i in devices if i - distance in devices]
    return lax.ppermute(block, axis, route)


def from_behind(value, axis, steps):
    count = lax.axis_size(axis)
    pairs = [(source, (source + steps) % count) for source in range(count)]
    return lax.ppermute(value, axis, pairs)


def correlate(data_ext, rms_data, slot_of, block, sids, offs, width):
    count, js, comps, taps = block.shape
    slots = slot_of[sids]

    def window(slot, off):
        start = (slot.astype(jnp.int32), jnp.zeros((), jnp.int32), off.astype(jnp.int32))
        seg = lax.dynamic_slice(data_ext, start, (1, comps, width + taps - 1))[0]
        scale = lax.dynamic_slice(rms_data, start, (1, comps, width))[0]
        return (seg, scale)

    segs, scales = jax.vmap(jax.vmap(window))(slots, offs)
    chans = count * js * comps
    num = lax.conv_general_dilated(
        segs.reshape(1, chans, width + taps - 1),
        block.reshape(chans, 1, taps),
        (1,),
        "VALID",
        dimension_numbers=("NCH", "OIH", "NCH"),
        feature_group_count=chans,
        preferred_element_type=jnp.float32,
    )
    wide = block.astype(jnp.float32)
    wrms = jnp.sqrt(jnp.mean(wide * wide, axis=-1) + 1e-06)
    ncc = num.reshape(count, js, comps, width) / (taps * wrms[..., None] * scales)
    return jnp.sum(ncc, axis=(1, 2))


def window_rms(data_ext, taps):
    wide = data_ext.astype(jnp.float32)
    sums = lax.reduce_window(
        wide * wide, jnp.array(0, wide.dtype), lax.add, (1, 1, taps), (1, 1, 1), "VALID"
    )
    return jnp.sqrt(sums / taps + 1e-06)


def on_device(records, owner_slots, gap_start, gap_len, templates, station_ids, offsets):
    width = records.shape[2]
    taps = templates.shape[3]
    rim = OFFMAX + taps - 1
    nstation = gap_start.shape[0]
    times = lax.axis_index("slab") * width + jnp.arange(width, dtype=jnp.int32)
    pick = owner_slots[:, None] == jnp.arange(nstation, dtype=jnp.int32)[None, :]
    starts = jnp.sum(jnp.where(pick[:, :, None], gap_start[None], 0), axis=1)
    ends = starts + jnp.sum(jnp.where(pick[:, :, None], gap_len[None], 0), axis=1)
    hit = (times[None, None, :] >= starts[:, :, None]) & (times[None, None, :] < ends[:, :, None])
    live = jnp.logical_not(jnp.any(hit, axis=1))
    masked = jnp.where(live[:, None, :], records, jnp.zeros((), records.dtype))
    gathered, slots_all = (
        lax.all_gather(masked, "tmpl", axis=0, tiled=True),
        lax.all_gather(owner_slots, "tmpl", axis=0, tiled=True),
    )
    ahead_rim = shifted(gathered[:, :, :rim], "slab", -1)
    data_ext = jnp.concatenate([gathered, ahead_rim], axis=2)
    rms_data = window_rms(data_ext, taps)
    slot_of = (
        jnp.zeros((nstation,), jnp.int32).at[slots_all].set(jnp.arange(nstation, dtype=jnp.int32))
    )
    count = templates.shape[0]
    here = lax.axis_index("slab")
    nslab = lax.axis_size("slab")
    steps_back = (here - jnp.arange(nslab, dtype=jnp.int32)) % nslab
    moving = (templates, station_ids, offsets)
    results = []
    for step in range(nslab):
        results.append(
            correlate(data_ext, rms_data, slot_of, moving[0], moving[1], moving[2], width)
        )
        if step + 1 < nslab:
            moving = from_behind((moving[0], moving[1], moving[2]), "slab", 1)
    stacked = jnp.stack(results)[steps_back]
    partial_sums = stacked.reshape(nslab * count, width)
    return lax.psum_scatter(partial_sums, "sub", scatter_dimension=1, tiled=True)


def solution(mesh):
    in_specs = (
        P(("grp", "tmpl"), None, "slab"),
        P(("grp", "tmpl")),
        P("grp", None),
        P("grp", None),
        P(("grp", "tmpl", "slab"), "sub", None, None),
        P(("grp", "tmpl", "slab"), "sub"),
        P(("grp", "tmpl", "slab"), "sub"),
    )
    out_specs = P(("grp", "tmpl"), ("slab", "sub"))
    return jax.shard_map(
        on_device, mesh=mesh, in_specs=in_specs, out_specs=out_specs, check_vma=False
    )
```

profile of v0, /device:TPU:0, one launch (start us, length us, event | category | flops | bytes accessed | tf_op | source)
XLA Modules:
  0.0 365.7 jit_solution(5863924489339995438)
XLA Ops:
  6.6 3.0 collective-permute-start.1
  9.7 1.9 collective-permute-start.3
  11.6 0.7 iota_compare_fusion
  12.3 0.9 select_reduce_fusion
  13.3 0.1 and_reduce_fusion
  13.4 0.9 broadcast_select_fusion
  14.3 14.5 %all_gather.6 = bf16[128,3,512]{2,0,1:T(8,128)(2,1)S(1)} all-gather(bf16[32,3,512]{2,0,1:T(8,128)(2,1)S(1)} %broadcast_select_fusion), channel_id=1, replica_groups=mesh['grp'=2,'tmpl'=4,'slab'=2,'sub'=2] {'tmpl'}, dimensions={0}, use_global_device_ids=true | all-gather | bytes 491520 | tf_op jit(solution)/shard_map/all_gather | solution.py:69
  28.8 0.2 copy.111
  29.1 1.3 collective-permute-start
  30.4 0.1 multiply_reduce_fusion.1
  30.6 0.2 copy.112
  30.9 0.6 dynamic-slice
  32.1 0.2 dynamic-update-slice
  32.4 8.2 %all-reduce = s32[128]{0:T(128)S(1)} all-reduce(s32[128]{0:T(128)S(1)} %dynamic-update-slice), channel_id=1, replica_groups=mesh['grp'=2,'tmpl'=4,'slab'=2,'sub'=2] {'tmpl'}, use_global_device_ids=true, to_apply=%add | all-reduce | flops 128 | bytes 1024
  40.7 1.5 scatter_custom_fusion
  42.2 0.8 gather_fusion
  43.0 0.1 gather.26
  43.3 0.1 copy.119
  43.4 0.1 copy.120
  43.6 0.2 copy.117
  43.9 0.8 gather_fusion.3
  44.9 0.1 multiply_reduce_fusion
  45.1 0.1 copy.131
  45.2 0.1 copy.132
  45.5 0.2 copy.129
  45.7 0.1 convert_multiply_fusion
  45.8 29.3 %add_sqrt_fusion = f32[128,3,712]{0,1,2:T(4,128)S(1)} fusion(f32[128,3,1011]{0,2,1:T(8,128)S(1)} %convert_multiply_fusion), kind=kOutput, calls=%fused_computation.11 | output fusion | flops 82295808 | bytes 2646528 | tf_op jit(solution)/shard_map/reduce_window | solution.py:50
  75.1 22.2 %copy.113 = bf16[128,3,1011]{1,0,2:T(8,128)(2,1)} copy(bf16[128,3,1011]{0,2,1:T(8,128)(2,1)S(1)} %pad_maximum_fusion) | data formatting | bytes 1552896 | tf_op jit(solution)/shard_map/concatenate | solution.py:73
  97.3 39.4 %gather_fusion.4 = bf16[40,3,811]{1,0,2:T(8,128)(2,1)} fusion(bf16[128,3,1011]{1,0,2:T(8,128)(2,1)} %copy.113, s32[40]{0:T(128)S(1)} %reshape.192), kind=kCustom, calls=%fused_computation.4 | custom fusion | bytes 389760 | tf_op jit(solution)/shard_map/vmap(vmap())/gather | solution.py:27
  136.7 39.6 %gather_fusion.1 = bf16[40,3,811]{1,0,2:T(8,128)(2,1)} fusion(bf16[128,3,1011]{1,0,2:T(8,128)(2,1)} %copy.113, s32[40]{0:T(128)S(1)} %reshape.170), kind=kCustom, calls=%fused_computation.1 | custom fusion | bytes 389760 | tf_op jit(solution)/shard_map/vmap(vmap())/gather | solution.py:27
  176.4 10.2 %reshape.263 = bf16[1,120,811]{1,0,2:T(2,128)(2,1)S(1)} reshape(bf16[40,3,811]{1,0,2:T(8,128)(2,1)} %gather_fusion.1) | data formatting | bytes 389280 | tf_op jit(solution)/shard_map/reshape;vmap(vmap())/squeeze | solution.py:34
  186.6 10.0 %reshape.264 = bf16[1,120,811]{1,0,2:T(2,128)(2,1)S(1)} reshape(bf16[40,3,811]{1,0,2:T(8,128)(2,1)} %gather_fusion.4) | data formatting | bytes 389280 | tf_op jit(solution)/shard_map/reshape;vmap(vmap())/squeeze | solution.py:34
  196.6 33.7 %fusion.30 = f32[1,120,512]{1,0,2:T(1,128)S(1)} fusion(bf16[1,120,811]{1,0,2:T(2,128)(2,1)S(1)} %reshape.263, bf16[120,1,300]{0,1,2:T(2,128)(2,1)S(1)} %copy.117), kind=kOutput, calls=%fused_computation.68 | convolution fusion | flops 36864000 | bytes 512400 | tf_op jit(solution)/shard_map/conv_general_dilated | solution.py:33
  230.3 0.1 copy.118
  230.5 31.5 %fusion.31 = f32[1,120,512]{1,0,2:T(1,128)S(1)} fusion(bf16[1,120,811]{1,0,2:T(2,128)(2,1)S(1)} %reshape.264, bf16[120,1,300]{0,1,2:T(2,128)(2,1)S(1)} %copy.129), kind=kOutput, calls=%fused_computation.69 | convolution fusion | flops 36864000 | bytes 512400 | tf_op jit(solution)/shard_map/conv_general_dilated | solution.py:33
  262.0 0.1 copy.130
  262.1 0.1 reshape.159
  262.2 0.1 reshape.157
  262.4 21.0 %copy.122 = f32[128,3,712]{1,0,2:T(8,128)} copy(f32[128,3,712]{0,1,2:T(4,128)S(1)} %add_sqrt_fusion) | data formatting | bytes 2187264 | tf_op jit(solution)/shard_map/sqrt | solution.py:53
  283.4 26.4 %gather_fusion.5 = f32[40,3,512]{1,0,2:T(8,128)} fusion(f32[128,3,712]{1,0,2:T(8,128)} %copy.122, s32[40]{0:T(128)S(1)} %reshape.199), kind=kCustom, calls=%fused_computation.5 | custom fusion | bytes 492000 | tf_op jit(solution)/shard_map/vmap(vmap())/gather | solution.py:28
  309.8 26.7 %gather_fusion.2 = f32[40,3,512]{1,0,2:T(8,128)} fusion(f32[128,3,712]{1,0,2:T(8,128)} %copy.122, s32[40]{0:T(128)S(1)} %reshape.177), kind=kCustom, calls=%fused_computation.2 | custom fusion | bytes 492000 | tf_op jit(solution)/shard_map/vmap(vmap())/gather | solution.py:28
  336.5 6.0 %copy.138 = f32[40,3,512]{2,1,0:T(4,128)S(1)} copy(f32[40,3,512]{1,0,2:T(8,128)} %gather_fusion.2) | data formatting | bytes 491520 | tf_op jit(solution)/shard_map/vmap(vmap())/squeeze | solution.py:28
  342.5 6.0 %copy.141 = f32[40,3,512]{2,1,0:T(4,128)S(1)} copy(f32[40,3,512]{1,0,2:T(8,128)} %gather_fusion.5) | data formatting | bytes 491520 | tf_op jit(solution)/shard_map/vmap(vmap())/squeeze | solution.py:28
  348.6 0.2 fusion.3
  348.8 0.2 fusion.2
  349.0 0.6 gather_fusion.6
  349.6 0.6 reshape.160
  350.2 8.4 %reduce-scatter.2.cloned.1.call-done = f32[8,256]{1,0:T(8,128)} async-done(((f32[8,512]{1,0:T(8,128)}), f32[8,256]{1,0:T(8,128)}) %reduce-scatter.2.cloned.1.call-update) | async-done | bytes 8208 | tf_op jit(solution)/shard_map/reduce_scatter | solution.py:92
  (46 shorter events, 1.2 us)
Async XLA Ops:
  6.5 24.3 %copy-start.4 = (u32[32]{0:T(128)S(1)}, u32[32]{0:T(128)}, u32[]{:S(2)}) copy-start(u32[32]{0:T(128)} %constant.144) | copy-start | bytes 388
  6.5 23.9 %copy-start.1 = (s32[4,10]{1,0:T(4,128)S(1)}, s32[4,10]{1,0:T(4,128)}, u32[]{:S(2)}) copy-start(s32[4,10]{1,0:T(4,128)} %param.12) | copy-start | bytes 484
  6.5 23.9 %copy-start = (bf16[4,10,3,300]{3,0,2,1:T(4,128)(2,1)S(1)}, bf16[4,10,3,300]{3,0,2,1:T(4,128)(2,1)}, u32[]{:S(2)}) copy-start(bf16[4,10,3,300]{3,0,2,1:T(4,128)(2,1)} %param.11) | copy-start | bytes 216004
  6.5 25.6 %copy-start.3 = (s32[32]{0:T(128)S(1)}, s32[32]{0:T(128)}, u32[]{:S(2)}) copy-start(s32[32]{0:T(128)} %param.8) | copy-start | bytes 388
  6.5 352.1 %reduce-scatter.2.cloned.1.call-start = ((), (), s32[]{:S(2)}) async-start(), calls=%async_computation.1 | async-start | bytes 24576 | tf_op jit(solution)/shard_map/reduce_scatter | solution.py:92
  6.6 37.2 %collective-permute-start.1 = (s32[4,10]{1,0:T(4,128)}, s32[4,10]{1,0:T(4,128)S(1)}, u32[]{:S(2)}, u32[]{:S(2)}) collective-permute-start(s32[4,10]{1,0:T(4,128)} %param.12), channel_id=1, source_target_pairs={{0,2},{2,0},{1,3},{3,1},{4,6},{6,4},{5,7},{7,5},{8,10},{10,8},{9,1... | collective-permute-start | bytes 488 | tf_op jit(solution)/shard_map/ppermute | solution.py:18
  9.6 35.2 %collective-permute-start.2 = (s32[4,10]{1,0:T(4,128)}, s32[4,10]{1,0:T(4,128)S(1)}, u32[]{:S(2)}, u32[]{:S(2)}) collective-permute-start(s32[4,10]{1,0:T(4,128)} %param.13), channel_id=1, source_target_pairs={{0,2},{2,0},{1,3},{3,1},{4,6},{6,4},{5,7},{7,5},{8,10},{10,8},{9,1... | collective-permute-start | bytes 488 | tf_op jit(solution)/shard_map/ppermute | solution.py:18
  9.7 35.3 %collective-permute-start.3 = (bf16[4,10,3,300]{3,0,2,1:T(4,128)(2,1)}, bf16[4,10,3,300]{3,0,2,1:T(4,128)(2,1)S(1)}, u32[]{:S(2)}, u32[]{:S(2)}) collective-permute-start(bf16[4,10,3,300]{3,0,2,1:T(4,128)(2,1)} %param.11), channel_id=1, source_target_pairs={{0,2},{2,0},{1,3},{3,1},{4,6},{6,4},{5,7},{7,5},{8,10},{10,8},{9,1... | collective-permute-start | bytes 216008 | tf_op jit(solution)/shard_map/ppermute | solution.py:18
  29.1 16.6 %collective-permute-start = (bf16[128,3,499]{0,2,1:T(8,128)(2,1)S(1)}, bf16[128,3,499]{0,2,1:T(8,128)(2,1)S(1)}, u32[]{:S(2)}, u32[]{:S(2)}) collective-permute-start(bf16[128,3,499]{0,2,1:T(8,128)(2,1)S(1)} %copy.111), channel_id=1, source_target_pairs={{2,0},{3,1},{6,4},{7,5},{10,8},{11,9},{14,12},{15,13},{18,16},{19,... | collective-permute-start | bytes 1149704 | tf_op jit(solution)/shard_map/ppermute | solution.py:12
  30.6 12.5 %copy-start.2 = (s32[4,10]{1,0:T(4,128)S(1)}, s32[4,10]{1,0:T(4,128)}, u32[]{:S(2)}) copy-start(s32[4,10]{1,0:T(4,128)} %param.13) | copy-start | bytes 484
Sparse Core Ops, SparseCore 0:
  350.3 8.2 reduce-scatter.1
where the time goes:
time: 369 us; the launch traced here: 366 us
  local copies, waits for them, and re-layouts  215 us (58%)
  matrix products  65.2 us (18%)
  other arithmetic  32.9 us (9%)
  blocking collectives  22.7 us (6%)
  between operations  14.6 us (4%)
  waiting for transfers between devices  8.42 us (2%)
  starting transfers between devices  6.35 us (2%)
    gather x2, local copies, waits for them, and re-layouts, window(): seg = lax.dynamic_slice(data_ext, start, (1, comps, width + taps - 1))[0]  79.1 us
    conv_general_dilated x2, matrix products, correlate(): lax.conv_general_dilated(segs.reshape(1, chans, width + taps - 1), block....  65.2 us
    gather x2, local copies, waits for them, and re-layouts, window(): scale = lax.dynamic_slice(rms_data, start, (1, comps, width))[0]  53.1 us
    another operation x1, other arithmetic, window_rms(): lax.reduce_window(wide * wide, jnp.array(0, wide.dtype), lax.add, (1, 1,...  29.3 us
    concatenate x1, local copies, waits for them, and re-layouts, on_device(): data_ext = jnp.concatenate([gathered, ahead_rim], axis=2)  22.2 us
    sqrt x1, local copies, waits for them, and re-layouts, window_rms(): return jnp.sqrt(sums / taps + 1e-06)  21 us
    squeeze x2, local copies, waits for them, and re-layouts, correlate(): segs.reshape(1, chans, width + taps - 1)  20.3 us
    all_gather x1, blocking collectives, on_device(): lax.all_gather(masked, 'tmpl', axis=0, tiled=True)  14.5 us
  transfers between devices with their start and end apart: 5, of which 1 were waited for; matrix products, arithmetic and copies ran while one was open for 2% of the time, Pallas kernels for 0%

commit v1 on v0

v1 whole, which is shorter than its diff:
```python
import jax
import jax.numpy as jnp
from jax import lax
from jax.experimental import pallas as pl
from jax.experimental.pallas import tpu as pltpu
from jax.sharding import PartitionSpec as P

LANES = 128
SPAN = 64
EXTRA = 16


def round_up(value, step):
    return -(-value // step) * step


def prepare_kernel(sids, offs, gap_start, gap_len, templates, filters, scale, sid_col, off_col, mask, band):
    count, js = sids.shape
    refs = count * js
    comps, taps = templates.shape[1:]
    nstation = gap_start.shape[0]
    depth = filters.shape[2]
    for k in range(count):
        for j in range(js):
            row = k * js + j
            sid_col[row, :] = jnp.full((LANES,), sids[k, j], jnp.int32)
            off_col[row, :] = jnp.full((LANES,), offs[k, j], jnp.int32)

    def one_ref(r, carry):
        wave = templates[r].astype(jnp.float32)
        wave = jnp.concatenate([wave, jnp.zeros((comps, depth - taps), jnp.float32)], axis=1)
        power = jnp.sum(wave * wave, axis=1, keepdims=True) / taps
        factor = 1.0 / (taps * jnp.sqrt(power + 1e-06))
        for c in range(comps):
            scale[pl.ds(c * refs + r, 1), :] = jnp.broadcast_to(factor[c : c + 1], (1, LANES))
            rows = jnp.broadcast_to(wave[c : c + 1], (SPAN, depth))
            rows = pltpu.roll(rows, 0, 1, stride=1, stride_axis=0)
            filters[c * refs + r] = rows.astype(jnp.bfloat16)
        return carry

    lax.fori_loop(0, refs, one_ref, 0, unroll=4)
    own = lax.broadcasted_iota(jnp.int32, (refs, nstation), 1) == sid_col[:, :nstation]
    own = jnp.where(own, 1.0, 0.0)
    starts = gap_start[...]
    ends = starts + gap_len[...]
    live = jnp.ones(mask.shape, jnp.float32)
    times = lax.broadcasted_iota(jnp.int32, mask.shape, 1).astype(jnp.float32)
    first = jnp.dot(own, starts.astype(jnp.float32), precision=lax.Precision.HIGHEST)
    last = jnp.dot(own, ends.astype(jnp.float32), precision=lax.Precision.HIGHEST)
    for g in range(starts.shape[1]):
        inside = (times >= first[:, g : g + 1] - 0.5) & (times < last[:, g : g + 1] - 0.5)
        live = jnp.where(inside, 0.0, live)
    mask[...] = live
    lead = lax.broadcasted_iota(jnp.int32, band.shape, 0) - lax.broadcasted_iota(jnp.int32, band.shape, 1)
    band[...] = jnp.where((lead >= 0) & (lead < taps), 1.0, 0.0).astype(jnp.bfloat16)


def correlate_kernel(comps, rows_slab, nslab, taps, *args):
    nsub = len(args) - 6 - 6
    blocks = args[:nsub]
    filters, scale, sid_col, off_col, mask, band = args[nsub : nsub + 6]
    out, segs, low, high, norm, total = args[nsub + 6 :]
    refs, time = mask.shape
    width = blocks[0].shape[2]
    chunks = time // LANES
    per = width // LANES
    chans = comps * refs
    count = out.shape[1]
    js = refs // count
    tall = low.shape[1]
    pieces = [(part, z) for part in blocks for z in range(part.shape[0])]
    depth = len(pieces) * rows_slab
    owner = []
    lines = round_up(depth, width) // width
    for q in range(lines):
        lane = lax.broadcasted_iota(jnp.int32, (1, width), 1) + q * width
        line = jnp.full((1, width), -1.0, jnp.float32)
        for b, (part, z) in enumerate(pieces):
            tail = part[z, nslab * rows_slab : nslab * rows_slab + EXTRA, :].astype(jnp.float32)
            here = (lane >= b * rows_slab) & (lane < (b + 1) * rows_slab)
            line = jnp.where(here, tail[q : q + 1], line)
        owner.append(line)
    owner = jnp.concatenate(owner, axis=1)[:, :depth]
    row = lax.broadcasted_iota(jnp.int32, (1, depth), 1)
    row = lax.rem(lax.rem(row, rows_slab), comps)
    wanted = sid_col[:, :1].astype(jnp.float32)
    match = owner == wanted
    picks = [jnp.where(match & (row == c), 1.0, 0.0).astype(jnp.bfloat16) for c in range(comps)]
    pick = jnp.concatenate(picks, axis=0)
    for s in range(nslab):
        stack = jnp.concatenate([part[z, s * rows_slab : (s + 1) * rows_slab, :] for part, z in pieces], axis=0)
        got = jnp.dot(pick, stack, preferred_element_type=jnp.float32)
        for c in range(comps):
            segs[c * refs : (c + 1) * refs, s * width : (s + 1) * width] = (
                got[c * refs : (c + 1) * refs] * mask[:, s * width : (s + 1) * width]
            )
    lane = lax.broadcasted_iota(jnp.int32, (8, LANES), 1)
    zero = jnp.zeros((8, LANES), jnp.float32)
    for i in range(chans // 8):
        ref_row = (i * 8) % refs
        off = off_col[ref_row : ref_row + 8, :]
        place = lax.bitwise_and(lane + off, LANES - 1)
        fine = lax.bitwise_and(off, LANES - 1)
        near = lane + fine < LANES
        far = off >= LANES
        turned = [
            jnp.take_along_axis(segs[i * 8 : i * 8 + 8, r * LANES : (r + 1) * LANES], place, axis=1)
            for r in range(chunks)
        ]
        turned += [zero, zero]
        moved = [jnp.where(near, turned[r], turned[r + 1]) for r in range(chunks + 1)]
        for r in range(chunks):
            segs[i * 8 : i * 8 + 8, r * LANES : (r + 1) * LANES] = jnp.where(far, moved[r + 1], moved[r])
    for i in range(chans // 8):
        top = i * 8 * tall
        mine = [segs[i * 8 : i * 8 + 8, r * LANES : (r + 1) * LANES] for r in range(chunks)] + [zero]
        for r in range(chunks):
            low[pl.ds(i * 8, 8), r, :] = mine[r]
            half = jnp.where(lane < LANES - SPAN, pltpu.roll(mine[r], SPAN, 1), pltpu.roll(mine[r + 1], SPAN, 1))
            high[pl.ds(i * 8, 8), r, :] = half
        for r in range(chunks, tall):
            low[pl.ds(i * 8, 8), r, :] = zero
            high[pl.ds(i * 8, 8), r, :] = zero
    kept = []
    for r in range(chunks):
        part = segs[:, r * LANES : (r + 1) * LANES]
        power = part * part
        lead = power.astype(jnp.bfloat16)
        rest = (power - lead.astype(jnp.float32)).astype(jnp.bfloat16)
        kept.append((lead, rest))
    reach = band.shape[0] // LANES
    for r in range(chunks):
        upto = min(reach, chunks - r)
        lead = jnp.concatenate([kept[r + p][0] for p in range(upto)], axis=1)
        rest = jnp.concatenate([kept[r + p][1] for p in range(upto)], axis=1)
        bands = band[: upto * LANES, :]
        sums = jnp.dot(lead, bands, preferred_element_type=jnp.float32)
        sums = sums + jnp.dot(rest, bands, preferred_element_type=jnp.float32)
        factor = scale[...] * lax.rsqrt(sums / taps + 1e-06)
        for i in range(chans // 8):
            norm[pl.ds(i * 8, 8), r, :] = factor[i * 8 : i * 8 + 8]
    span = filters.shape[2] // LANES
    for k in range(count):
        acc = jnp.zeros((chunks, LANES), jnp.float32)
        for c in range(comps):
            for j in range(js):
                ch = c * refs + k * js + j
                left = jnp.concatenate([low[ch, p : p + chunks, :] for p in range(span)], axis=1)
                right = jnp.concatenate([high[ch, p : p + chunks, :] for p in range(span)], axis=1)
                both = jnp.concatenate([left, right], axis=0).astype(jnp.bfloat16)
                res = lax.dot_general(
                    both, filters[ch], (((1,), (1,)), ((), ())), preferred_element_type=jnp.float32
                )
                wide = jnp.concatenate([res[:chunks], res[chunks:]], axis=1)
                acc = acc + wide * norm[ch]
        total[k] = acc
    place = lax.axis_index("slab") * lax.axis_size("sub") + lax.axis_index("sub")
    quarters = out.shape[0]
    each = chunks // quarters
    for q in range(quarters):
        target = lax.bitwise_xor(place, q)
        for e in range(each):
            line = total[:, target * each + e, :]
            out[q, :, e * LANES : (e + 1) * LANES] = line


def on_device(records, owner_slots, gap_start, gap_len, templates, station_ids, offsets):
    nloc, comps, width = records.shape
    count, js, _, taps = templates.shape
    nslab, nsub, ntmpl = (lax.axis_size(name) for name in ("slab", "sub", "tmpl"))
    time = width * nslab
    refs = count * js
    chans = comps * refs
    here, core = lax.axis_index("slab"), lax.axis_index("sub")
    half = nloc // nsub
    rows = half * comps
    rows_slab = round_up(rows, 16)
    mine = lax.dynamic_slice_in_dim(records, half * core, half, 0).reshape(rows, width)
    mine = jnp.pad(mine, ((0, rows_slab - rows), (0, 0)))
    own = lax.dynamic_slice_in_dim(owner_slots, half * core, half, 0)
    own = jnp.pad(jnp.repeat(own, comps), (0, rows_slab - rows), constant_values=-1)
    index = jnp.arange(EXTRA * width, dtype=jnp.int32) % rows_slab
    own = jnp.sum(jnp.where(index[:, None] == jnp.arange(rows_slab)[None, :], own[None, :], 0), axis=1)
    own = own.reshape(EXTRA, width).astype(records.dtype)
    block = jnp.zeros((nslab * rows_slab + EXTRA, width), records.dtype)
    block = lax.dynamic_update_slice(block, own, (nslab * rows_slab, 0))
    block = lax.dynamic_update_slice(block, mine, (here * rows_slab, 0))
    for d in range(1, nslab):
        got = lax.ppermute(mine, "slab", [(i, i ^ d) for i in range(nslab)])
        block = lax.dynamic_update_slice(block, got, ((here ^ d) * rows_slab, 0))
    if ntmpl <= 8:
        column = jnp.stack(
            [block] + [lax.ppermute(block, "tmpl", [(i, i ^ d) for i in range(ntmpl)]) for d in range(1, ntmpl)]
        )
    else:
        column = lax.all_gather(block, "tmpl", axis=0)
    parts = [column] + [
        lax.ppermute(column, "sub", [(i, i ^ d) for i in range(nsub)]) for d in range(1, nsub)
    ]
    vmem, smem = pl.BlockSpec(memory_space=pltpu.VMEM), pl.BlockSpec(memory_space=pltpu.SMEM)
    depth = round_up(taps + SPAN - 1, LANES)
    tables = pl.pallas_call(
        prepare_kernel,
        out_shape=[
            jax.ShapeDtypeStruct((chans, SPAN, depth), jnp.bfloat16),
            jax.ShapeDtypeStruct((chans, LANES), jnp.float32),
            jax.ShapeDtypeStruct((refs, LANES), jnp.int32),
            jax.ShapeDtypeStruct((refs, LANES), jnp.int32),
            jax.ShapeDtypeStruct((refs, time), jnp.float32),
            jax.ShapeDtypeStruct((round_up(taps + LANES - 1, LANES), LANES), jnp.bfloat16),
        ],
        in_specs=[smem, smem, vmem, vmem, vmem],
        out_specs=[vmem] * 6,
        compiler_params=pltpu.CompilerParams(vmem_limit_bytes=40 << 20),
        name="prepare",
    )(station_ids, offsets, gap_start, gap_len, templates.reshape(refs, comps, taps))
    chunks = time // LANES
    quarters = nslab * nsub

    def body(*args):
        correlate_kernel(comps, rows_slab, nslab, taps, *args)

    tall = chunks + 8
    sums = pl.pallas_call(
        body,
        out_shape=jax.ShapeDtypeStruct((quarters, count, time // quarters), jnp.float32),
        in_specs=[vmem] * (nsub + 6),
        out_specs=vmem,
        scratch_shapes=[
            pltpu.VMEM((chans, time), jnp.float32),
            pltpu.VMEM((chans, tall, LANES), jnp.float32),
            pltpu.VMEM((chans, tall, LANES), jnp.float32),
            pltpu.VMEM((chans, chunks, LANES), jnp.float32),
            pltpu.VMEM((count, chunks, LANES), jnp.float32),
        ],
        compiler_params=pltpu.CompilerParams(vmem_limit_bytes=40 << 20),
        name="correlate",
    )(*parts, *tables)
    result = jnp.zeros((nslab, count, time // quarters), jnp.float32)
    got = [sums[0]] + [
        lax.ppermute(sums[q], ("slab", "sub"), [(i, i ^ q) for i in range(quarters)]) for q in range(1, quarters)
    ]
    for d in range(nslab):
        line = sum(got[d * nsub + 1 : (d + 1) * nsub], got[d * nsub])
        result = lax.dynamic_update_slice(result, line[None], (here ^ d, 0, 0))
    return result.reshape(nslab * count, time // quarters)


def solution(mesh):
    in_specs = (
        P(("grp", "tmpl"), None, "slab"),
        P(("grp", "tmpl")),
        P("grp", None),
        P("grp", None),
        P(("grp", "tmpl", "slab"), "sub", None, None),
        P(("grp", "tmpl", "slab"), "sub"),
        P(("grp", "tmpl", "slab"), "sub"),
    )
    out_specs = P(("grp", "tmpl"), ("slab", "sub"))
    return jax.shard_map(
        on_device, mesh=mesh, in_specs=in_specs, out_specs=out_specs, check_vma=False
    )
```

time: 369 us -> 32.5 us (0.09)
  local copies, waits for them, and re-layouts: 215 us -> 2.81 us
  matrix products: 65.2 us -> 0 us
  other arithmetic: 32.9 us -> 0.42 us
  blocking collectives: 22.7 us -> 0 us
  between operations: 14.6 us -> 0.18 us
  Pallas kernels: 0 us -> 7.5 us
    gather x9 -> x0, local copies, waits for them, and re-layouts: 134 us -> none  [the longest x2 79.1 us: window(): seg = lax.dynamic_slice(data_ext, start, (1, comps, width + taps - 1))[0]]
    conv_general_dilated x2 -> x0, matrix products: 65.2 us -> none  [correlate(): lax.conv_general_dilated(segs.reshape(1, chans, width + taps - 1), block....]
    squeeze x4 -> x1, local copies, waits for them, and re-layouts: 32.3 us -> 0.01 us  [on_device(): sums[q]]
    another operation x2 -> x1, other arithmetic: 29.3 us -> 0.06 us  [on_device(): jnp.stack([block] + [lax.ppermute(block, 'tmpl', [(i, i ^ d) for i in ran...]
    concatenate x5 -> x0, local copies, waits for them, and re-layouts: 22.5 us -> none  [the longest x1 22.2 us: on_device(): data_ext = jnp.concatenate([gathered, ahead_rim], axis=2)]
    sqrt x1 -> x0, local copies, waits for them, and re-layouts: 21 us -> none  [window_rms(): return jnp.sqrt(sums / taps + 1e-06)]
    all_gather x1 -> x0, blocking collectives: 14.5 us -> none  [on_device(): lax.all_gather(masked, 'tmpl', axis=0, tiled=True)]
    ppermute x4 -> x8, waiting for transfers between devices: 0.01 us -> 11.7 us  [the longest x3 7.96 us: on_device(): lax.ppermute(block, 'tmpl', [(i, i ^ d) for i in range(ntmpl)])]
  transfers between devices with their start and end apart: 5 -> 8, of which waited for: 1 -> 5; matrix products, arithmetic and copies ran while one was open for 2% -> 5% of each run, Pallas kernels for 0% -> 12%
where the time goes in v1:
time: 32.5 us; the launch traced here: 32.4 us
  waiting for transfers between devices  11.7 us (36%)
  starting transfers between devices  9.79 us (30%)
  Pallas kernels  7.5 us (23%)
  local copies, waits for them, and re-layouts  2.81 us (9%)
  other arithmetic  0.42 us (1%)
    ppermute x3, waiting for transfers between devices, on_device(): lax.ppermute(block, 'tmpl', [(i, i ^ d) for i in range(ntmpl)])  7.96 us
    ppermute x3, starting transfers between devices, on_device(): lax.ppermute(block, 'tmpl', [(i, i ^ d) for i in range(ntmpl)])  4.7 us
    pallas_call x1, Pallas kernels, on_device(): pl.pallas_call(prepare_kernel, out_shape=[jax.ShapeDtypeStruct((chans, SP...  3.77 us
    pallas_call x1, Pallas kernels, on_device(): pl.pallas_call(body, out_shape=jax.ShapeDtypeStruct((quarters, count, tim...  3.73 us
    ppermute x3, waiting for transfers between devices, on_device(): lax.ppermute(sums[q], ('slab', 'sub'), [(i, i ^ q) for i in range(quarter...  3.02 us
    ppermute x1, starting transfers between devices, on_device(): got = lax.ppermute(mine, 'slab', [(i, i ^ d) for i in range(nslab)])  3 us
    ppermute x3, starting transfers between devices, on_device(): lax.ppermute(sums[q], ('slab', 'sub'), [(i, i ^ q) for i in range(quarter...  2.02 us
    unnamed x15, local copies, waits for them, and re-layouts  1.15 us
  transfers between devices with their start and end apart: 8, of which 5 were waited for; matrix products, arithmetic and copies ran while one was open for 5% of the time, Pallas kernels for 12%

profile of v1, /device:TPU:0, one launch (start us, length us, event | category | flops | bytes accessed | tf_op | source)
XLA Modules:
  0.0 32.4 jit_solution(1810122885816023608)
XLA Ops:
  0.0 0.0 copy-start
  0.0 0.0 copy-start.3
  0.0 0.0 copy-start.4
  0.0 0.0 copy-start.5
  0.0 0.0 copy-start.1
  0.0 0.0 copy-start.2
  0.0 0.9 %copy-done = bf16[32,3,512]{2,0,1:T(8,128)(2,1)S(1)} copy-done((bf16[32,3,512]{2,0,1:T(8,128)(2,1)S(1)}, bf16[32,3,512]{2,0,1:T(8,128)(2,1)}, u32[]{:S(2)}) %copy-start) | copy-done | bytes 98328
  1.0 3.0 %collective-permute-start = (bf16[48,512]{1,0:T(8,128)(2,1)S(1)}, bf16[48,512]{1,0:T(8,128)(2,1)S(1)}, u32[]{:S(2)}, u32[]{:S(2)}) collective-permute-start(bf16[48,512]{1,0:T(8,128)(2,1)S(1)} %reshape.23), channel_id=1, source_target_pairs={{0,2},{2,0},{1,3},{3,1},{4,6},{6,4},{5,7},{7,5},{8,10},{10,8},{9,1... | collective-permute-start | bytes 147464 | tf_op jit(solution)/shard_map/ppermute | solution.py:189
  4.0 0.7 %dynamic_slice.6 = s32[16]{0:T(128)S(1)} dynamic-slice(s32[32]{0:T(128)} %param.8, s32[]{:T(128)S(6)} %select_n.32), dynamic_slice_sizes={16} | dynamic-slice | bytes 132 | tf_op jit(solution)/shard_map/dynamic_slice | solution.py:180
  4.8 0.1 broadcast_in_dim.31
  4.8 0.1 broadcast_in_dim.32
  4.9 0.3 select_reduce_fusion
  5.3 0.7 %collective-permute-done = bf16[48,512]{1,0:T(8,128)(2,1)S(1)} collective-permute-done((bf16[48,512]{1,0:T(8,128)(2,1)S(1)}, bf16[48,512]{1,0:T(8,128)(2,1)S(1)}, u32[]{:S(2)}, u32[]{:S(2)}) %collective-permute-start) | collective-permute-done | bytes 49184 | tf_op jit(solution)/shard_map/ppermute | solution.py:189
  6.1 2.1 %collective-permute-start.1 = (bf16[112,512]{1,0:T(8,128)(2,1)S(1)}, bf16[112,512]{1,0:T(8,128)(2,1)S(1)}, u32[]{:S(2)}, u32[]{:S(2)}) collective-permute-start(bf16[112,512]{1,0:T(8,128)(2,1)S(1)} %constant_dynamic-update-slice_fusion), channel_id=1, source_target_pairs={{0,4},{4,0},{8,12},{12,8},{1,5},{5,1},{9,13},{13,9},{2,6},{6,2},{1... | collective-permute-start | bytes 344072 | tf_op jit(solution)/shard_map/ppermute | solution.py:193
  8.2 2.6 %collective-permute-start.2 = (bf16[112,512]{1,0:T(8,128)(2,1)S(1)}, bf16[112,512]{1,0:T(8,128)(2,1)S(1)}, u32[]{:S(2)}, u32[]{:S(2)}) collective-permute-start(bf16[112,512]{1,0:T(8,128)(2,1)S(1)} %constant_dynamic-update-slice_fusion), channel_id=1, source_target_pairs={{0,8},{4,12},{8,0},{12,4},{1,9},{5,13},{9,1},{13,5},{2,10},{6,14},... | collective-permute-start | bytes 344072 | tf_op jit(solution)/shard_map/ppermute | solution.py:193
  10.8 0.0 collective-permute-start.3
  10.8 1.3 %collective-permute-done.1 = bf16[112,512]{1,0:T(8,128)(2,1)S(1)} collective-permute-done((bf16[112,512]{1,0:T(8,128)(2,1)S(1)}, bf16[112,512]{1,0:T(8,128)(2,1)S(1)}, u32[]{:S(2)}, u32[]{:S(2)}) %collective-permute-start.1) | collective-permute-done | bytes 114720 | tf_op jit(solution)/shard_map/ppermute | solution.py:193
  12.1 6.7 %collective-permute-done.2 = bf16[112,512]{1,0:T(8,128)(2,1)S(1)} collective-permute-done((bf16[112,512]{1,0:T(8,128)(2,1)S(1)}, bf16[112,512]{1,0:T(8,128)(2,1)S(1)}, u32[]{:S(2)}, u32[]{:S(2)}) %collective-permute-start.2) | collective-permute-done | bytes 114720 | tf_op jit(solution)/shard_map/ppermute | solution.py:193
  18.7 0.0 collective-permute-done.3
  18.7 0.1 pad_maximum_fusion.args_0_
  18.8 0.1 collective-permute-start.4
  18.9 0.0 copy-done.3
  18.9 0.0 copy-done.4
  19.0 0.1 copy.18.gap_start
  19.1 0.0 copy-done.5
  19.1 0.1 copy.19.gap_len
  19.2 0.0 copy-done.1
  19.2 0.0 copy-done.2
  19.2 3.8 %prepare.1 = (bf16[120,64,384]{2,1,0:T(8,128)(2,1)S(1)}, f32[120,128]{1,0:T(8,128)S(1)}, s32[40,128]{1,0:T(8,128)S(1)}, s32[40,128]{1,0:T(8,128)S(1)}, f32[40,10...) custom-call(s32[4,10]{1,0:T(4,128)S(1)} %copy-done.1, s32[4,10]{1,0:T(4,128)S(1)} %copy-done.2, s32[128,4]{1,0:T(8,128)S(1)} %copy.18.gap_start, ...), custom_call_target="tpu_custom_call" | custom-call | tf_op jit(solution)/shard_map/prepare/pallas_call | solution.py:202
  23.0 0.0 collective-permute-done.4.args_1_
  23.0 3.7 %correlate.1 = f32[4,4,256]{2,1,0:T(4,128)S(1)} custom-call(bf16[4,112,512]{2,1,0:T(8,128)(2,1)S(1)} %pad_maximum_fusion.args_0_, bf16[4,112,512]{2,1,0:T(8,128)(2,1)S(1)} %collective-permute-done.4.args_1_, bf16[120,64,384]{2,1,0:T(8,128)(2,1)S(1)} %get-tuple-element.11.args_2_, f32[120,128]{1,0:T(8,128)S(1)} %get-tuple-element.12.args_3_, ...), custom_call_target="tpu_custom_call" | custom-call | tf_op jit(solution)/shard_map/correlate/pallas_call | solution.py:224
  26.7 0.6 %collective-permute-start.5 = (f32[4,256]{1,0:T(4,128)S(1)}, f32[4,256]{1,0:T(4,128)S(1)}, u32[]{:S(2)}, u32[]{:S(2)}) collective-permute-start(f32[4,256]{1,0:T(4,128)S(1)} %get-tuple-element.19), channel_id=1, source_target_pairs={{0,1},{1,0},{2,3},{3,2},{4,5},{5,4},{6,7},{7,6},{8,9},{9,8},{10,11... | collective-permute-start | bytes 12296 | tf_op jit(solution)/shard_map/ppermute | solution.py:241
  27.3 1.4 %collective-permute-start.6 = (f32[4,256]{1,0:T(4,128)S(1)}, f32[4,256]{1,0:T(4,128)S(1)}, u32[]{:S(2)}, u32[]{:S(2)}) collective-permute-start(f32[4,256]{1,0:T(4,128)S(1)} %get-tuple-element.18), channel_id=1, source_target_pairs={{0,2},{1,3},{2,0},{3,1},{4,6},{5,7},{6,4},{7,5},{8,10},{9,11},{10,... | collective-permute-start | bytes 12296 | tf_op jit(solution)/shard_map/ppermute | solution.py:241
  28.7 0.0 collective-permute-start.7
  28.8 0.0 collective-permute-done.5
  28.8 2.1 %collective-permute-done.6 = f32[4,256]{1,0:T(4,128)S(1)} collective-permute-done((f32[4,256]{1,0:T(4,128)S(1)}, f32[4,256]{1,0:T(4,128)S(1)}, u32[]{:S(2)}, u32[]{:S(2)}) %collective-permute-start.6) | collective-permute-done | bytes 4128 | tf_op jit(solution)/shard_map/ppermute | solution.py:241
  30.9 0.9 %collective-permute-done.7 = f32[4,256]{1,0:T(4,128)S(1)} collective-permute-done((f32[4,256]{1,0:T(4,128)S(1)}, f32[4,256]{1,0:T(4,128)S(1)}, u32[]{:S(2)}, u32[]{:S(2)}) %collective-permute-start.7) | collective-permute-done | bytes 4128 | tf_op jit(solution)/shard_map/ppermute | solution.py:241
  31.8 0.6 %reshape.25 = f32[8,256]{1,0:T(8,128)} reshape(f32[2,4,256]{2,1,0:T(4,128)S(1)} %bitcast_dynamic-update-slice_fusion) | data formatting | bytes 16384 | tf_op jit(solution)/shard_map/reshape | solution.py:246
  (14 shorter events, 0.2 us)
Async XLA Ops:
  0.0 0.9 %copy-start = (bf16[32,3,512]{2,0,1:T(8,128)(2,1)S(1)}, bf16[32,3,512]{2,0,1:T(8,128)(2,1)}, u32[]{:S(2)}) copy-start(bf16[32,3,512]{2,0,1:T(8,128)(2,1)} %param.7) | copy-start | bytes 294916
  0.0 18.9 %copy-start.3 = (bf16[4,10,3,300]{3,0,2,1:T(4,128)(2,1)S(1)}, bf16[4,10,3,300]{3,0,2,1:T(4,128)(2,1)}, u32[]{:S(2)}) copy-start(bf16[4,10,3,300]{3,0,2,1:T(4,128)(2,1)} %param.11) | copy-start | bytes 216004
  0.0 18.9 %copy-start.4 = (s32[128,4]{0,1:T(4,128)S(1)}, s32[128,4]{0,1:T(4,128)}, u32[]{:S(2)}) copy-start(s32[128,4]{0,1:T(4,128)} %param.9) | copy-start | bytes 6148
  0.0 19.1 %copy-start.5 = (s32[128,4]{0,1:T(4,128)S(1)}, s32[128,4]{0,1:T(4,128)}, u32[]{:S(2)}) copy-start(s32[128,4]{0,1:T(4,128)} %param.10) | copy-start | bytes 6148
  0.0 19.2 %copy-start.1 = (s32[4,10]{1,0:T(4,128)S(1)}, s32[4,10]{1,0:T(4,128)}, u32[]{:S(2)}) copy-start(s32[4,10]{1,0:T(4,128)} %sids.1) | copy-start | bytes 484
  0.0 19.2 %copy-start.2 = (s32[4,10]{1,0:T(4,128)S(1)}, s32[4,10]{1,0:T(4,128)}, u32[]{:S(2)}) copy-start(s32[4,10]{1,0:T(4,128)} %offs.1) | copy-start | bytes 484
  1.0 5.1 %collective-permute-start = (bf16[48,512]{1,0:T(8,128)(2,1)S(1)}, bf16[48,512]{1,0:T(8,128)(2,1)S(1)}, u32[]{:S(2)}, u32[]{:S(2)}) collective-permute-start(bf16[48,512]{1,0:T(8,128)(2,1)S(1)} %reshape.23), channel_id=1, source_target_pairs={{0,2},{2,0},{1,3},{3,1},{4,6},{6,4},{5,7},{7,5},{8,10},{10,8},{9,1... | collective-permute-start | bytes 147464 | tf_op jit(solution)/shard_map/ppermute | solution.py:189
  6.1 6.0 %collective-permute-start.1 = (bf16[112,512]{1,0:T(8,128)(2,1)S(1)}, bf16[112,512]{1,0:T(8,128)(2,1)S(1)}, u32[]{:S(2)}, u32[]{:S(2)}) collective-permute-start(bf16[112,512]{1,0:T(8,128)(2,1)S(1)} %constant_dynamic-update-slice_fusion), channel_id=1, source_target_pairs={{0,4},{4,0},{8,12},{12,8},{1,5},{5,1},{9,13},{13,9},{2,6},{6,2},{1... | collective-permute-start | bytes 344072 | tf_op jit(solution)/shard_map/ppermute | solution.py:193
  8.2 10.5 %collective-permute-start.2 = (bf16[112,512]{1,0:T(8,128)(2,1)S(1)}, bf16[112,512]{1,0:T(8,128)(2,1)S(1)}, u32[]{:S(2)}, u32[]{:S(2)}) collective-permute-start(bf16[112,512]{1,0:T(8,128)(2,1)S(1)} %constant_dynamic-update-slice_fusion), channel_id=1, source_target_pairs={{0,8},{4,12},{8,0},{12,4},{1,9},{5,13},{9,1},{13,5},{2,10},{6,14},... | collective-permute-start | bytes 344072 | tf_op jit(solution)/shard_map/ppermute | solution.py:193
  10.8 8.0 %collective-permute-start.3 = (bf16[112,512]{1,0:T(8,128)(2,1)S(1)}, bf16[112,512]{1,0:T(8,128)(2,1)S(1)}, u32[]{:S(2)}, u32[]{:S(2)}) collective-permute-start(bf16[112,512]{1,0:T(8,128)(2,1)S(1)} %constant_dynamic-update-slice_fusion), channel_id=1, source_target_pairs={{0,12},{4,8},{8,4},{12,0},{1,13},{5,9},{9,5},{13,1},{2,14},{6,10},... | collective-permute-start | bytes 344072 | tf_op jit(solution)/shard_map/ppermute | solution.py:193
  18.8 4.2 %collective-permute-start.4 = (bf16[4,112,512]{2,1,0:T(8,128)(2,1)S(1)}, bf16[4,112,512]{2,1,0:T(8,128)(2,1)S(1)}, u32[]{:S(2)}, u32[]{:S(2)}) collective-permute-start(bf16[4,112,512]{2,1,0:T(8,128)(2,1)S(1)} %pad_maximum_fusion.args_0_), channel_id=1, source_target_pairs={{0,1},{1,0},{2,3},{3,2},{4,5},{5,4},{6,7},{7,6},{8,9},{9,8},{10,11... | collective-permute-start | bytes 1376264 | tf_op jit(solution)/shard_map/ppermute | solution.py:198
  26.7 2.0 %collective-permute-start.5 = (f32[4,256]{1,0:T(4,128)S(1)}, f32[4,256]{1,0:T(4,128)S(1)}, u32[]{:S(2)}, u32[]{:S(2)}) collective-permute-start(f32[4,256]{1,0:T(4,128)S(1)} %get-tuple-element.19), channel_id=1, source_target_pairs={{0,1},{1,0},{2,3},{3,2},{4,5},{5,4},{6,7},{7,6},{8,9},{9,8},{10,11... | collective-permute-start | bytes 12296 | tf_op jit(solution)/shard_map/ppermute | solution.py:241
  27.3 3.6 %collective-permute-start.6 = (f32[4,256]{1,0:T(4,128)S(1)}, f32[4,256]{1,0:T(4,128)S(1)}, u32[]{:S(2)}, u32[]{:S(2)}) collective-permute-start(f32[4,256]{1,0:T(4,128)S(1)} %get-tuple-element.18), channel_id=1, source_target_pairs={{0,2},{1,3},{2,0},{3,1},{4,6},{5,7},{6,4},{7,5},{8,10},{9,11},{10,... | collective-permute-start | bytes 12296 | tf_op jit(solution)/shard_map/ppermute | solution.py:241
  28.7 3.1 %collective-permute-start.7 = (f32[4,256]{1,0:T(4,128)S(1)}, f32[4,256]{1,0:T(4,128)S(1)}, u32[]{:S(2)}, u32[]{:S(2)}) collective-permute-start(f32[4,256]{1,0:T(4,128)S(1)} %get-tuple-element.17), channel_id=1, source_target_pairs={{0,3},{1,2},{2,1},{3,0},{4,7},{5,6},{6,5},{7,4},{8,11},{9,10},{10,... | collective-permute-start | bytes 12296 | tf_op jit(solution)/shard_map/ppermute | solution.py:241

commit v2 on v1

--- a/solution.py
+++ b/solution.py
@@ -7,7 +7,7 @@
 
 LANES = 128
 SPAN = 64
-EXTRA = 16
+EXTRA = 8
 
 
 def round_up(value, step):
@@ -55,45 +55,45 @@
     band[...] = jnp.where((lead >= 0) & (lead < taps), 1.0, 0.0).astype(jnp.bfloat16)
 
 
-def correlate_kernel(comps, rows_slab, nslab, taps, *args):
-    nsub = len(args) - 6 - 6
-    blocks = args[:nsub]
-    filters, scale, sid_col, off_col, mask, band = args[nsub : nsub + 6]
-    out, segs, low, high, norm, total = args[nsub + 6 :]
+def correlate_kernel(comps, rows_slab, nslab, nsub, taps, *args):
+    heads, args = args[:nsub], args[nsub:]
+    tails, args = args[: nsub * (nslab - 1)], args[nsub * (nslab - 1) :]
+    filters, scale, sid_col, off_col, mask, band = args[:6]
+    keep, send, segs, low, high, norm, total = args[6:]
     refs, time = mask.shape
-    width = blocks[0].shape[2]
+    ntmpl, _, width = heads[0].shape
     chunks = time // LANES
-    per = width // LANES
     chans = comps * refs
-    count = out.shape[1]
+    count = keep.shape[1]
     js = refs // count
     tall = low.shape[1]
-    pieces = [(part, z) for part in blocks for z in range(part.shape[0])]
-    depth = len(pieces) * rows_slab
+    here, core = lax.axis_index("slab"), lax.axis_index("sub")
+    depth = nsub * ntmpl * rows_slab
     owner = []
     lines = round_up(depth, width) // width
     for q in range(lines):
         lane = lax.broadcasted_iota(jnp.int32, (1, width), 1) + q * width
         line = jnp.full((1, width), -1.0, jnp.float32)
-        for b, (part, z) in enumerate(pieces):
-            tail = part[z, nslab * rows_slab : nslab * rows_slab + EXTRA, :].astype(jnp.float32)
-            here = (lane >= b * rows_slab) & (lane < (b + 1) * rows_slab)
-            line = jnp.where(here, tail[q : q + 1], line)
+        for b in range(nsub * ntmpl):
+            tail = heads[b // ntmpl][b % ntmpl, rows_slab : rows_slab + EXTRA, :].astype(jnp.float32)
+            inside = (lane >= b * rows_slab) & (lane < (b + 1) * rows_slab)
+            line = jnp.where(inside, tail[q : q + 1], line)
         owner.append(line)
     owner = jnp.concatenate(owner, axis=1)[:, :depth]
     row = lax.broadcasted_iota(jnp.int32, (1, depth), 1)
-    row = lax.rem(lax.rem(row, rows_slab), comps)
+    row = lax.rem(row, rows_slab) // (rows_slab // comps)
     wanted = sid_col[:, :1].astype(jnp.float32)
     match = owner == wanted
     picks = [jnp.where(match & (row == c), 1.0, 0.0).astype(jnp.bfloat16) for c in range(comps)]
     pick = jnp.concatenate(picks, axis=0)
-    for s in range(nslab):
-        stack = jnp.concatenate([part[z, s * rows_slab : (s + 1) * rows_slab, :] for part, z in pieces], axis=0)
+    for d in range(nslab):
+        parts = heads if d == 0 else tails[(d - 1) * nsub : d * nsub]
+        stack = jnp.concatenate([part[z, :rows_slab, :] for part in parts for z in range(ntmpl)], axis=0)
         got = jnp.dot(pick, stack, preferred_element_type=jnp.float32)
+        spot = pl.ds(pl.multiple_of(lax.bitwise_xor(here, d) * width, LANES), width)
+        live = mask[:, spot]
         for c in range(comps):
-            segs[c * refs : (c + 1) * refs, s * width : (s + 1) * width] = (
-                got[c * refs : (c + 1) * refs] * mask[:, s * width : (s + 1) * width]
-            )
+            segs[c * refs : (c + 1) * refs, spot] = got[c * refs : (c + 1) * refs] * live
     lane = lax.broadcasted_iota(jnp.int32, (8, LANES), 1)
     zero = jnp.zeros((8, LANES), jnp.float32)
     for i in range(chans // 8):
@@ -154,14 +154,18 @@
                 wide = jnp.concatenate([res[:chunks], res[chunks:]], axis=1)
                 acc = acc + wide * norm[ch]
         total[k] = acc
-    place = lax.axis_index("slab") * lax.axis_size("sub") + lax.axis_index("sub")
-    quarters = out.shape[0]
-    each = chunks // quarters
-    for q in range(quarters):
-        target = lax.bitwise_xor(place, q)
+    each = chunks // (nslab * nsub)
+    for d in range(nslab):
         for e in range(each):
-            line = total[:, target * each + e, :]
-            out[q, :, e * LANES : (e + 1) * LANES] = line
+            first = lax.bitwise_xor(here, d) * nsub * each + e
+            keep[d, :, e * LANES : (e + 1) * LANES] = total[:, first + core * each, :]
+            for m in range(1, nsub):
+                other = first + lax.bitwise_xor(core, m) * each
+                send[m - 1, d, :, e * LANES : (e + 1) * LANES] = total[:, other, :]
+
+
+def swapped(value, axis, distance):
+    return lax.ppermute(value, axis, [(i, i ^ distance) for i in range(lax.axis_size(axis))])
 
 
 def on_device(records, owner_slots, gap_start, gap_len, templates, station_ids, offsets):
@@ -173,30 +177,23 @@
     chans = comps * refs
     here, core = lax.axis_index("slab"), lax.axis_index("sub")
     half = nloc // nsub
-    rows = half * comps
-    rows_slab = round_up(rows, 16)
-    mine = lax.dynamic_slice_in_dim(records, half * core, half, 0).reshape(rows, width)
-    mine = jnp.pad(mine, ((0, rows_slab - rows), (0, 0)))
+    high = round_up(half, 16)
+    rows_slab = comps * high
+    mine = lax.dynamic_slice_in_dim(records.transpose(1, 0, 2), half * core, half, 1)
+    mine = jnp.pad(mine, ((0, 0), (0, high - half), (0, 0))).reshape(rows_slab, width)
     own = lax.dynamic_slice_in_dim(owner_slots, half * core, half, 0)
-    own = jnp.pad(jnp.repeat(own, comps), (0, rows_slab - rows), constant_values=-1)
-    index = jnp.arange(EXTRA * width, dtype=jnp.int32) % rows_slab
-    own = jnp.sum(jnp.where(index[:, None] == jnp.arange(rows_slab)[None, :], own[None, :], 0), axis=1)
-    own = own.reshape(EXTRA, width).astype(records.dtype)
-    block = jnp.zeros((nslab * rows_slab + EXTRA, width), records.dtype)
-    block = lax.dynamic_update_slice(block, own, (nslab * rows_slab, 0))
-    block = lax.dynamic_update_slice(block, mine, (here * rows_slab, 0))
-    for d in range(1, nslab):
-        got = lax.ppermute(mine, "slab", [(i, i ^ d) for i in range(nslab)])
-        block = lax.dynamic_update_slice(block, got, ((here ^ d) * rows_slab, 0))
+    index = jnp.arange(EXTRA * width, dtype=jnp.int32).reshape(1, EXTRA, width) % high
+    slots = jnp.arange(half, dtype=jnp.int32)[:, None, None]
+    own = jnp.sum(jnp.where(index == slots, own[:, None, None] + 1, 0), axis=0) - 1
+    block = jnp.concatenate([mine, own.astype(records.dtype)], axis=0)
     if ntmpl <= 8:
-        column = jnp.stack(
-            [block] + [lax.ppermute(block, "tmpl", [(i, i ^ d) for i in range(ntmpl)]) for d in range(1, ntmpl)]
-        )
+        column = [block] + [swapped(block, "tmpl", d) for d in range(1, ntmpl)]
     else:
-        column = lax.all_gather(block, "tmpl", axis=0)
-    parts = [column] + [
-        lax.ppermute(column, "sub", [(i, i ^ d) for i in range(nsub)]) for d in range(1, nsub)
-    ]
+        column = list(lax.all_gather(block, "tmpl", axis=0))
+    head = jnp.stack(column)
+    waves = jnp.stack([part[:rows_slab] for part in column])
+    tails = [swapped(waves, "slab", d) for d in range(1, nslab)]
+    heads = [head] + [swapped(head, "sub", m) for m in range(1, nsub)]
     vmem, smem = pl.BlockSpec(memory_space=pltpu.VMEM), pl.BlockSpec(memory_space=pltpu.SMEM)
     depth = round_up(taps + SPAN - 1, LANES)
     tables = pl.pallas_call(
@@ -214,18 +211,25 @@
         compiler_params=pltpu.CompilerParams(vmem_limit_bytes=40 << 20),
         name="prepare",
     )(station_ids, offsets, gap_start, gap_len, templates.reshape(refs, comps, taps))
+    tails, tables = lax.optimization_barrier((tails, tables))
+    lasts = []
+    for tail in tails:
+        lasts += [tail] + [swapped(tail, "sub", m) for m in range(1, nsub)]
     chunks = time // LANES
-    quarters = nslab * nsub
+    each = width // nsub
 
     def body(*args):
-        correlate_kernel(comps, rows_slab, nslab, taps, *args)
+        correlate_kernel(comps, rows_slab, nslab, nsub, taps, *args)
 
     tall = chunks + 8
-    sums = pl.pallas_call(
+    keep, send = pl.pallas_call(
         body,
-        out_shape=jax.ShapeDtypeStruct((quarters, count, time // quarters), jnp.float32),
-        in_specs=[vmem] * (nsub + 6),
-        out_specs=vmem,
+        out_shape=[
+            jax.ShapeDtypeStruct((nslab, count, each), jnp.float32),
+            jax.ShapeDtypeStruct((nsub - 1, nslab, count, each), jnp.float32),
+        ],
+        in_specs=[vmem] * (nsub * nslab + 6),
+        out_specs=[vmem] * 2,
         scratch_shapes=[
             pltpu.VMEM((chans, time), jnp.float32),
             pltpu.VMEM((chans, tall, LANES), jnp.float32),
@@ -235,15 +239,17 @@
         ],
         compiler_params=pltpu.CompilerParams(vmem_limit_bytes=40 << 20),
         name="correlate",
-    )(*parts, *tables)
-    result = jnp.zeros((nslab, count, time // quarters), jnp.float32)
-    got = [sums[0]] + [
-        lax.ppermute(sums[q], ("slab", "sub"), [(i, i ^ q) for i in range(quarters)]) for q in range(1, quarters)
-    ]
-    for d in range(nslab):
-        line = sum(got[d * nsub + 1 : (d + 1) * nsub], got[d * nsub])
-        result = lax.dynamic_update_slice(result, line[None], (here ^ d, 0, 0))
-    return result.reshape(nslab * count, time // quarters)
+    )(*heads, *lasts, *tables)
+    for m in range(1, nsub):
+        keep = keep + swapped(send[m - 1], "sub", m)
+    lines = [keep[0]] + [swapped(keep[d], "slab", d) for d in range(1, nslab)]
+    result = []
+    for s in range(nslab):
+        line = lines[0]
+        for d in range(1, nslab):
+            line = jnp.where((here ^ d) == s, lines[d], line)
+        result.append(line)
+    return jnp.concatenate(result, axis=0)
 
 
 def solution(mesh):

time: 32.5 us -> 32.6 us (level)
  waiting for transfers between devices: 11.7 us -> 9.44 us
  local copies, waits for them, and re-layouts: 2.81 us -> 4.78 us
  other arithmetic: 0.42 us -> 1.53 us
  starting transfers between devices: 9.79 us -> 8.91 us
    unnamed x15 -> x9, local copies, waits for them, and re-layouts: 1.15 us -> 4.75 us
    ppermute x8, waiting for transfers between devices: 11.7 us -> 9.44 us  [swapped(): lax.ppermute(value, axis, [(i, i ^ distance) for i in range(lax.axis_size...]
    ppermute x8, starting transfers between devices: 9.79 us -> 8.91 us  [swapped(): lax.ppermute(value, axis, [(i, i ^ distance) for i in range(lax.axis_size...]
    dynamic_slice x3 -> x0, local copies, waits for them, and re-layouts: 0.78 us -> none  [the longest x1 0.73 us: on_device(): own = lax.dynamic_slice_in_dim(owner_slots, half * core, half, 0)]
    add x0 -> x2, other arithmetic: none -> 0.73 us  [the longest x1 0.73 us: on_device(): own[:, None, None] + 1]
    reshape x2 -> x0, local copies, waits for them, and re-layouts: 0.66 us -> none  [the longest x1 0.61 us: on_device(): return result.reshape(nslab * count, time // quarters)]
    concatenate x0 -> x1, other arithmetic: none -> 0.61 us  [on_device(): return jnp.concatenate(result, axis=0)]
  transfers between devices with their start and end apart: 8 -> 8, of which waited for: 5 -> 5; matrix products, arithmetic and copies ran while one was open for 5% -> 8% of each run, Pallas kernels for 12% -> 12%
where the time goes in v2:
time: 32.6 us; the launch traced here: 32.4 us
  waiting for transfers between devices  9.44 us (29%)
  starting transfers between devices  8.91 us (27%)
  Pallas kernels  7.62 us (23%)
  local copies, waits for them, and re-layouts  4.78 us (15%)
  other arithmetic  1.53 us (5%)
    ppermute x8, waiting for transfers between devices, swapped(): lax.ppermute(value, axis, [(i, i ^ distance) for i in range(lax.axis_size...  9.44 us
    ppermute x8, starting transfers between devices, swapped(): lax.ppermute(value, axis, [(i, i ^ distance) for i in range(lax.axis_size...  8.91 us
    unnamed x9, local copies, waits for them, and re-layouts  4.75 us
    pallas_call x1, Pallas kernels, on_device(): pl.pallas_call(body, out_shape=[jax.ShapeDtypeStruct((nslab, count, each)...  3.85 us
    pallas_call x1, Pallas kernels, on_device(): pl.pallas_call(prepare_kernel, out_shape=[jax.ShapeDtypeStruct((chans, SP...  3.76 us
    add x1, other arithmetic, on_device(): own[:, None, None] + 1  0.73 us
  transfers between devices with their start and end apart: 8, of which 5 were waited for; matrix products, arithmetic and copies ran while one was open for 8% of the time, Pallas kernels for 12%

profile of v2, /device:TPU:0, one launch (start us, length us, event | category | flops | bytes accessed | tf_op | source)
XLA Modules:
  0.0 32.4 jit_solution(16986671613074499811)
XLA Ops:
  0.0 0.0 copy-start
  0.0 0.9 %copy-done = bf16[32,3,512]{2,0,1:T(8,128)(2,1)S(1)} copy-done((bf16[32,3,512]{2,0,1:T(8,128)(2,1)S(1)}, bf16[32,3,512]{2,0,1:T(8,128)(2,1)}, u32[]{:S(2)}) %copy-start) | copy-done | bytes 98328
  0.9 0.7 %dynamic-slice_add_fusion = s32[16]{0:T(128)S(1)} fusion(s32[32]{0:T(128)} %param.8, s32[]{:T(128)S(6)} %select_n.35), kind=kLoop, calls=%fused_computation.18 | loop fusion | flops 16 | bytes 132 | tf_op jit(solution)/shard_map/add | solution.py:187
  1.6 0.1 select_reduce_fusion
  1.8 5.1 %collective-permute-start.2 = (bf16[56,512]{1,0:T(8,128)(2,1)S(1)}, bf16[56,512]{1,0:T(8,128)(2,1)S(1)}, u32[]{:S(2)}, u32[]{:S(2)}) collective-permute-start(bf16[56,512]{1,0:T(8,128)(2,1)S(1)} %get-tuple-element.36), channel_id=1, source_target_pairs={{0,12},{4,8},{8,4},{12,0},{1,13},{5,9},{9,5},{13,1},{2,14},{6,10},... | collective-permute-start | bytes 172040 | tf_op jit(solution)/shard_map/ppermute | solution.py:168
  6.9 0.0 collective-permute-start.1
  6.9 0.6 %collective-permute-start = (bf16[56,512]{1,0:T(8,128)(2,1)S(1)}, bf16[56,512]{1,0:T(8,128)(2,1)S(1)}, u32[]{:S(2)}, u32[]{:S(2)}) collective-permute-start(bf16[56,512]{1,0:T(8,128)(2,1)S(1)} %get-tuple-element.36), channel_id=1, source_target_pairs={{0,4},{4,0},{8,12},{12,8},{1,5},{5,1},{9,13},{13,9},{2,6},{6,2},{1... | collective-permute-start | bytes 172040 | tf_op jit(solution)/shard_map/ppermute | solution.py:168
  7.5 1.8 %collective-permute-done.2 = bf16[56,512]{1,0:T(8,128)(2,1)S(1)} collective-permute-done((bf16[56,512]{1,0:T(8,128)(2,1)S(1)}, bf16[56,512]{1,0:T(8,128)(2,1)S(1)}, u32[]{:S(2)}, u32[]{:S(2)}) %collective-permute-start.2) | collective-permute-done | bytes 57376 | tf_op jit(solution)/shard_map/ppermute | solution.py:168
  9.3 2.7 %collective-permute-done.1 = bf16[56,512]{1,0:T(8,128)(2,1)S(1)} collective-permute-done((bf16[56,512]{1,0:T(8,128)(2,1)S(1)}, bf16[56,512]{1,0:T(8,128)(2,1)S(1)}, u32[]{:S(2)}, u32[]{:S(2)}) %collective-permute-start.1) | collective-permute-done | bytes 57376 | tf_op jit(solution)/shard_map/ppermute | solution.py:168
  12.0 0.0 collective-permute-done
  12.0 1.6 %collective-permute-start.4 = (bf16[4,48,512]{2,1,0:T(8,128)(2,1)S(1)}, bf16[4,48,512]{2,1,0:T(8,128)(2,1)S(1)}, u32[]{:S(2)}, u32[]{:S(2)}) collective-permute-start(bf16[4,48,512]{2,1,0:T(8,128)(2,1)S(1)} %pad_maximum_fusion.1), channel_id=1, source_target_pairs={{0,2},{2,0},{1,3},{3,1},{4,6},{6,4},{5,7},{7,5},{8,10},{10,8},{9,1... | collective-permute-start | bytes 589832 | tf_op jit(solution)/shard_map/ppermute | solution.py:168
  13.6 0.1 collective-permute-start.3
  13.7 0.9 %copy.11 = bf16[4,10,3,300]{3,2,1,0:T(4,128)(2,1)S(1)} copy(bf16[4,10,3,300]{3,0,2,1:T(4,128)(2,1)} %param.11) | data formatting | bytes 144000 | tf_op args[4]
  14.7 0.8 %copy.12.gap_start = s32[128,4]{1,0:T(8,128)S(1)} copy(s32[128,4]{0,1:T(4,128)} %param.9) | data formatting | bytes 4096 | tf_op args[2]
  15.4 0.8 %copy.13.gap_len = s32[128,4]{1,0:T(8,128)S(1)} copy(s32[128,4]{0,1:T(4,128)} %param.10) | data formatting | bytes 4096 | tf_op args[3]
  16.2 0.0 copy-start.1
  16.2 0.7 %copy-done.1 = s32[4,10]{1,0:T(4,128)S(1)} copy-done((s32[4,10]{1,0:T(4,128)S(1)}, s32[4,10]{1,0:T(4,128)}, u32[]{:S(2)}) %copy-start.1) | copy-done | bytes 184
  16.9 0.0 copy-start.2
  16.9 0.7 %copy-done.2 = s32[4,10]{1,0:T(4,128)S(1)} copy-done((s32[4,10]{1,0:T(4,128)S(1)}, s32[4,10]{1,0:T(4,128)}, u32[]{:S(2)}) %copy-start.2) | copy-done | bytes 184
  17.6 3.8 %prepare.1 = (bf16[120,64,384]{2,1,0:T(8,128)(2,1)S(1)}, f32[120,128]{1,0:T(8,128)S(1)}, s32[40,128]{1,0:T(8,128)S(1)}, s32[40,128]{1,0:T(8,128)S(1)}, f32[40,10...) custom-call(s32[4,10]{1,0:T(4,128)S(1)} %copy-done.1, s32[4,10]{1,0:T(4,128)S(1)} %copy-done.2, s32[128,4]{1,0:T(8,128)S(1)} %copy.12.gap_start, ...), custom_call_target="tpu_custom_call" | custom-call | tf_op jit(solution)/shard_map/prepare/pallas_call | solution.py:199
  21.4 0.0 collective-permute-done.4.args_2_
  21.4 0.6 %collective-permute-start.5 = (bf16[4,48,512]{2,1,0:T(8,128)(2,1)S(1)}, bf16[4,48,512]{2,1,0:T(8,128)(2,1)S(1)}, u32[]{:S(2)}, u32[]{:S(2)}) collective-permute-start(bf16[4,48,512]{2,1,0:T(8,128)(2,1)S(1)} %collective-permute-done.4.args_2_), channel_id=1, source_target_pairs={{0,1},{1,0},{2,3},{3,2},{4,5},{5,4},{6,7},{7,6},{8,9},{9,8},{10,11... | collective-permute-start | bytes 589832 | tf_op jit(solution)/shard_map/ppermute | solution.py:168
  21.9 0.0 collective-permute-done.3.args_1_
  21.9 1.1 %collective-permute-done.5.args_3_ = bf16[4,48,512]{2,1,0:T(8,128)(2,1)S(1)} collective-permute-done((bf16[4,48,512]{2,1,0:T(8,128)(2,1)S(1)}, bf16[4,48,512]{2,1,0:T(8,128)(2,1)S(1)}, u32[]{:S(2)}, u32[]{:S(2)}) %collective-permute-start.5) | collective-permute-done | bytes 196640 | tf_op jit(solution)/shard_map/ppermute | solution.py:168
  23.0 3.9 %correlate.1 = (f32[2,4,256]{2,1,0:T(4,128)S(1)}, f32[1,2,4,256]{3,2,1,0:T(4,128)S(1)}) custom-call(bf16[4,56,512]{2,1,0:T(8,128)(2,1)S(1)} %pad_maximum_fusion.args_0_, bf16[4,56,512]{2,1,0:T(8,128)(2,1)S(1)} %collective-permute-done.3.args_1_, bf16[4,48,512]{2,1,0:T(8,128)(2,1)S(1)} %collective-permute-done.4.args_2_, ...), custom_call_target="tpu_custom_call" | custom-call | tf_op jit(solution)/shard_map/correlate/pallas_call | solution.py:225
  26.9 0.4 %collective-permute-start.6 = (f32[2,4,256]{2,1,0:T(4,128)S(1)}, f32[2,4,256]{2,1,0:T(4,128)S(1)}, u32[]{:S(2)}, u32[]{:S(2)}) collective-permute-start(f32[2,4,256]{2,1,0:T(4,128)S(1)} %bitcast.27), channel_id=1, source_target_pairs={{0,1},{1,0},{2,3},{3,2},{4,5},{5,4},{6,7},{7,6},{8,9},{9,8},{10,11... | collective-permute-start | bytes 24584 | tf_op jit(solution)/shard_map/ppermute | solution.py:168
  27.3 0.8 %collective-permute-done.6 = f32[2,4,256]{2,1,0:T(4,128)S(1)} collective-permute-done((f32[2,4,256]{2,1,0:T(4,128)S(1)}, f32[2,4,256]{2,1,0:T(4,128)S(1)}, u32[]{:S(2)}, u32[]{:S(2)}) %collective-permute-start.6) | collective-permute-done | bytes 8224 | tf_op jit(solution)/shard_map/ppermute | solution.py:168
  28.2 0.5 %collective-permute-start.7 = (f32[4,256]{1,0:T(4,128)S(1)}, f32[4,256]{1,0:T(4,128)S(1)}, u32[]{:S(2)}, u32[]{:S(2)}) collective-permute-start(f32[4,256]{1,0:T(4,128)S(1)} %slice_bitcast_fusion.4), channel_id=1, source_target_pairs={{0,2},{2,0},{1,3},{3,1},{4,6},{6,4},{5,7},{7,5},{8,10},{10,8},{9,1... | collective-permute-start | bytes 12296 | tf_op jit(solution)/shard_map/ppermute | solution.py:168
  28.7 3.1 %collective-permute-done.7 = f32[4,256]{1,0:T(4,128)S(1)} collective-permute-done((f32[4,256]{1,0:T(4,128)S(1)}, f32[4,256]{1,0:T(4,128)S(1)}, u32[]{:S(2)}, u32[]{:S(2)}) %collective-permute-start.7) | collective-permute-done | bytes 4128 | tf_op jit(solution)/shard_map/ppermute | solution.py:168
  31.8 0.6 %pad_maximum_fusion.3 = f32[8,256]{1,0:T(8,128)} fusion(f32[4,256]{1,0:T(4,128)S(1)} %get-tuple-element.38, f32[4,256]{1,0:T(4,128)S(1)} %get-tuple-element.37), kind=kLoop, calls=%fused_computation.13 | loop fusion | flops 2048 | bytes 16384 | tf_op jit(solution)/shard_map/concatenate | solution.py:252
  (12 shorter events, 0.1 us)
Async XLA Ops:
  0.0 0.9 %copy-start = (bf16[32,3,512]{2,0,1:T(8,128)(2,1)S(1)}, bf16[32,3,512]{2,0,1:T(8,128)(2,1)}, u32[]{:S(2)}) copy-start(bf16[32,3,512]{2,0,1:T(8,128)(2,1)} %param.7) | copy-start | bytes 294916
  1.8 7.5 %collective-permute-start.2 = (bf16[56,512]{1,0:T(8,128)(2,1)S(1)}, bf16[56,512]{1,0:T(8,128)(2,1)S(1)}, u32[]{:S(2)}, u32[]{:S(2)}) collective-permute-start(bf16[56,512]{1,0:T(8,128)(2,1)S(1)} %get-tuple-element.36), channel_id=1, source_target_pairs={{0,12},{4,8},{8,4},{12,0},{1,13},{5,9},{9,5},{13,1},{2,14},{6,10},... | collective-permute-start | bytes 172040 | tf_op jit(solution)/shard_map/ppermute | solution.py:168
  6.9 5.1 %collective-permute-start.1 = (bf16[56,512]{1,0:T(8,128)(2,1)S(1)}, bf16[56,512]{1,0:T(8,128)(2,1)S(1)}, u32[]{:S(2)}, u32[]{:S(2)}) collective-permute-start(bf16[56,512]{1,0:T(8,128)(2,1)S(1)} %get-tuple-element.36), channel_id=1, source_target_pairs={{0,8},{4,12},{8,0},{12,4},{1,9},{5,13},{9,1},{13,5},{2,10},{6,14},... | collective-permute-start | bytes 172040 | tf_op jit(solution)/shard_map/ppermute | solution.py:168
  6.9 5.1 %collective-permute-start = (bf16[56,512]{1,0:T(8,128)(2,1)S(1)}, bf16[56,512]{1,0:T(8,128)(2,1)S(1)}, u32[]{:S(2)}, u32[]{:S(2)}) collective-permute-start(bf16[56,512]{1,0:T(8,128)(2,1)S(1)} %get-tuple-element.36), channel_id=1, source_target_pairs={{0,4},{4,0},{8,12},{12,8},{1,5},{5,1},{9,13},{13,9},{2,6},{6,2},{1... | collective-permute-start | bytes 172040 | tf_op jit(solution)/shard_map/ppermute | solution.py:168
  12.0 9.4 %collective-permute-start.4 = (bf16[4,48,512]{2,1,0:T(8,128)(2,1)S(1)}, bf16[4,48,512]{2,1,0:T(8,128)(2,1)S(1)}, u32[]{:S(2)}, u32[]{:S(2)}) collective-permute-start(bf16[4,48,512]{2,1,0:T(8,128)(2,1)S(1)} %pad_maximum_fusion.1), channel_id=1, source_target_pairs={{0,2},{2,0},{1,3},{3,1},{4,6},{6,4},{5,7},{7,5},{8,10},{10,8},{9,1... | collective-permute-start | bytes 589832 | tf_op jit(solution)/shard_map/ppermute | solution.py:168
  13.6 8.3 %collective-permute-start.3 = (bf16[4,56,512]{2,1,0:T(8,128)(2,1)S(1)}, bf16[4,56,512]{2,1,0:T(8,128)(2,1)S(1)}, u32[]{:S(2)}, u32[]{:S(2)}) collective-permute-start(bf16[4,56,512]{2,1,0:T(8,128)(2,1)S(1)} %pad_maximum_fusion.args_0_), channel_id=1, source_target_pairs={{0,1},{1,0},{2,3},{3,2},{4,5},{5,4},{6,7},{7,6},{8,9},{9,8},{10,11... | collective-permute-start | bytes 688136 | tf_op jit(solution)/shard_map/ppermute | solution.py:168
  16.2 0.7 %copy-start.1 = (s32[4,10]{1,0:T(4,128)S(1)}, s32[4,10]{1,0:T(4,128)}, u32[]{:S(2)}) copy-start(s32[4,10]{1,0:T(4,128)} %sids.1) | copy-start | bytes 484
  16.9 0.7 %copy-start.2 = (s32[4,10]{1,0:T(4,128)S(1)}, s32[4,10]{1,0:T(4,128)}, u32[]{:S(2)}) copy-start(s32[4,10]{1,0:T(4,128)} %offs.1) | copy-start | bytes 484
  21.4 1.6 %collective-permute-start.5 = (bf16[4,48,512]{2,1,0:T(8,128)(2,1)S(1)}, bf16[4,48,512]{2,1,0:T(8,128)(2,1)S(1)}, u32[]{:S(2)}, u32[]{:S(2)}) collective-permute-start(bf16[4,48,512]{2,1,0:T(8,128)(2,1)S(1)} %collective-permute-done.4.args_2_), channel_id=1, source_target_pairs={{0,1},{1,0},{2,3},{3,2},{4,5},{5,4},{6,7},{7,6},{8,9},{9,8},{10,11... | collective-permute-start | bytes 589832 | tf_op jit(solution)/shard_map/ppermute | solution.py:168
  26.9 1.3 %collective-permute-start.6 = (f32[2,4,256]{2,1,0:T(4,128)S(1)}, f32[2,4,256]{2,1,0:T(4,128)S(1)}, u32[]{:S(2)}, u32[]{:S(2)}) collective-permute-start(f32[2,4,256]{2,1,0:T(4,128)S(1)} %bitcast.27), channel_id=1, source_target_pairs={{0,1},{1,0},{2,3},{3,2},{4,5},{5,4},{6,7},{7,6},{8,9},{9,8},{10,11... | collective-permute-start | bytes 24584 | tf_op jit(solution)/shard_map/ppermute | solution.py:168
  28.2 3.6 %collective-permute-start.7 = (f32[4,256]{1,0:T(4,128)S(1)}, f32[4,256]{1,0:T(4,128)S(1)}, u32[]{:S(2)}, u32[]{:S(2)}) collective-permute-start(f32[4,256]{1,0:T(4,128)S(1)} %slice_bitcast_fusion.4), channel_id=1, source_target_pairs={{0,2},{2,0},{1,3},{3,1},{4,6},{6,4},{5,7},{7,5},{8,10},{10,8},{9,1... | collective-permute-start | bytes 12296 | tf_op jit(solution)/shard_map/ppermute | solution.py:168

commit v3 on v2

--- a/solution.py
+++ b/solution.py
@@ -1,3 +1,5 @@
+import functools
+
 import jax
 import jax.numpy as jnp
 from jax import lax
@@ -7,6 +9,7 @@
 
 LANES = 128
 SPAN = 64
+GROUP = 4
 EXTRA = 8
 
 
@@ -14,45 +17,68 @@
     return -(-value // step) * step
 
 
-def prepare_kernel(sids, offs, gap_start, gap_len, templates, filters, scale, sid_col, off_col, mask, band):
+def pack_kernel(owner_slots, records, block, sems):
+    comps, nloc, width = records.shape
+    half = (block.shape[0] - EXTRA) // comps
+    first = pl.multiple_of(lax.axis_index("sub") * half, half)
+    copies = []
+    for c in range(comps):
+        source, place = records.at[c, pl.ds(first, half), :], block.at[c * half : (c + 1) * half, :]
+        copies.append(pltpu.make_async_copy(source, place, sems.at[c]))
+        copies[-1].start()
+    lane = lax.rem(lax.broadcasted_iota(jnp.int32, (EXTRA, width), 1), half)
+    line = jnp.full((EXTRA, width), -1, jnp.int32)
+    for i in range(half):
+        line = jnp.where(lane == i, owner_slots[first + i], line)
+    block[comps * half :, :] = line.astype(jnp.float32).astype(block.dtype)
+    for copy in copies:
+        copy.wait()
+
+
+def tables_kernel(taps, sids, offs, gap_start, gap_len, sid_col, off_col, mask, band):
     count, js = sids.shape
     refs = count * js
-    comps, taps = templates.shape[1:]
-    nstation = gap_start.shape[0]
-    depth = filters.shape[2]
+    nstation = gap_start.shape[1]
     for k in range(count):
         for j in range(js):
             row = k * js + j
             sid_col[row, :] = jnp.full((LANES,), sids[k, j], jnp.int32)
             off_col[row, :] = jnp.full((LANES,), offs[k, j], jnp.int32)
-
-    def one_ref(r, carry):
-        wave = templates[r].astype(jnp.float32)
-        wave = jnp.concatenate([wave, jnp.zeros((comps, depth - taps), jnp.float32)], axis=1)
-        power = jnp.sum(wave * wave, axis=1, keepdims=True) / taps
-        factor = 1.0 / (taps * jnp.sqrt(power + 1e-06))
-        for c in range(comps):
-            scale[pl.ds(c * refs + r, 1), :] = jnp.broadcast_to(factor[c : c + 1], (1, LANES))
-            rows = jnp.broadcast_to(wave[c : c + 1], (SPAN, depth))
-            rows = pltpu.roll(rows, 0, 1, stride=1, stride_axis=0)
-            filters[c * refs + r] = rows.astype(jnp.bfloat16)
-        return carry
-
-    lax.fori_loop(0, refs, one_ref, 0, unroll=4)
     own = lax.broadcasted_iota(jnp.int32, (refs, nstation), 1) == sid_col[:, :nstation]
-    own = jnp.where(own, 1.0, 0.0)
-    starts = gap_start[...]
-    ends = starts + gap_len[...]
+    starts = gap_start[...].astype(jnp.float32)
+    ends = starts + gap_len[...].astype(jnp.float32)
     live = jnp.ones(mask.shape, jnp.float32)
     times = lax.broadcasted_iota(jnp.int32, mask.shape, 1).astype(jnp.float32)
-    first = jnp.dot(own, starts.astype(jnp.float32), precision=lax.Precision.HIGHEST)
-    last = jnp.dot(own, ends.astype(jnp.float32), precision=lax.Precision.HIGHEST)
-    for g in range(starts.shape[1]):
-        inside = (times >= first[:, g : g + 1] - 0.5) & (times < last[:, g : g + 1] - 0.5)
-        live = jnp.where(inside, 0.0, live)
+    for g in range(starts.shape[0]):
+        first = jnp.sum(jnp.where(own, starts[g : g + 1], 0.0), axis=1, keepdims=True)
+        last = jnp.sum(jnp.where(own, ends[g : g + 1], 0.0), axis=1, keepdims=True)
+        live = jnp.where((times >= first) & (times < last), 0.0, live)
     mask[...] = live
-    lead = lax.broadcasted_iota(jnp.int32, band.shape, 0) - lax.broadcasted_iota(jnp.int32, band.shape, 1)
+    rows = lax.rem(lax.broadcasted_iota(jnp.int32, band.shape, 0), LANES)
+    cols = lax.broadcasted_iota(jnp.int32, band.shape, 1)
+    lead = rows + (cols // LANES) * LANES - lax.rem(cols, LANES)
     band[...] = jnp.where((lead >= 0) & (lead < taps), 1.0, 0.0).astype(jnp.bfloat16)
+
+
+def filters_kernel(templates, filters, scale):
+    js, comps, count, taps = templates.shape
+    refs = count * js
+    depth = filters.shape[2]
+
+    def one_station(j, carry):
+        for c in range(comps):
+            wave = templates[j, c].astype(jnp.float32)
+            wave = jnp.concatenate([wave, jnp.zeros((count, depth - taps), jnp.float32)], axis=1)
+            power = jnp.sum(wave * wave, axis=1, keepdims=True) / taps
+            factor = 1.0 / (taps * jnp.sqrt(power + 1e-06))
+            for k in range(count):
+                ch = c * refs + k * js + j
+                scale[pl.ds(ch, 1), :] = jnp.broadcast_to(factor[k : k + 1], (1, LANES))
+                rows = jnp.broadcast_to(wave[k : k + 1], (SPAN, depth))
+                filters[ch] = pltpu.roll(rows, 0, 1, stride=1, stride_axis=0).astype(jnp.bfloat16)
+        return carry
+
+    lax.fori_loop(0, js, one_station, 0)
 
 
 def correlate_kernel(comps, rows_slab, nslab, nsub, taps, *args):
@@ -121,46 +147,52 @@
         for r in range(chunks, tall):
             low[pl.ds(i * 8, 8), r, :] = zero
             high[pl.ds(i * 8, 8), r, :] = zero
-    kept = []
-    for r in range(chunks):
+    reach = band.shape[1] // LANES
+    sums = {}
+    for r in reversed(range(chunks)):
         part = segs[:, r * LANES : (r + 1) * LANES]
         power = part * part
         lead = power.astype(jnp.bfloat16)
         rest = (power - lead.astype(jnp.float32)).astype(jnp.bfloat16)
-        kept.append((lead, rest))
-    reach = band.shape[0] // LANES
-    for r in range(chunks):
-        upto = min(reach, chunks - r)
-        lead = jnp.concatenate([kept[r + p][0] for p in range(upto)], axis=1)
-        rest = jnp.concatenate([kept[r + p][1] for p in range(upto)], axis=1)
-        bands = band[: upto * LANES, :]
-        sums = jnp.dot(lead, bands, preferred_element_type=jnp.float32)
-        sums = sums + jnp.dot(rest, bands, preferred_element_type=jnp.float32)
-        factor = scale[...] * lax.rsqrt(sums / taps + 1e-06)
+        sums[r] = jnp.dot(jnp.concatenate([lead, rest], axis=1), band[...], preferred_element_type=jnp.float32)
+        window = sums[r][:, :LANES]
+        for p in range(1, min(reach, chunks - r)):
+            window = window + sums[r + p][:, p * LANES : (p + 1) * LANES]
+        factor = scale[...] * lax.rsqrt(window / taps + 1e-06)
         for i in range(chans // 8):
             norm[pl.ds(i * 8, 8), r, :] = factor[i * 8 : i * 8 + 8]
     span = filters.shape[2] // LANES
+    accs = [jnp.zeros((chunks, LANES), jnp.float32) for _ in range(count)]
+    side = lax.broadcasted_iota(jnp.int32, (chunks, LANES), 1) < SPAN
+    for base in range(0, chans, GROUP):
+        rows = []
+        for ch in range(base, base + GROUP):
+            for source in (low, high):
+                rows.append(jnp.concatenate([source[ch, p : p + chunks, :] for p in range(span)], axis=1))
+        both = jnp.concatenate(rows, axis=0).astype(jnp.bfloat16)
+        weights = filters[base : base + GROUP].reshape(GROUP * SPAN, span * LANES)
+        res = lax.dot_general(both, weights, (((1,), (1,)), ((), ())), preferred_element_type=jnp.float32)
+        for g in range(GROUP):
+            left = (g // 2) * LANES
+            tile = res[2 * g * chunks : 2 * (g + 1) * chunks, left : left + LANES]
+            early, late = tile[:chunks], tile[chunks:]
+            if g % 2 == 0:
+                wide = jnp.where(side, early, pltpu.roll(late, SPAN, 1))
+            else:
+                wide = jnp.where(side, pltpu.roll(early, SPAN, 1), late)
+            k = ((base + g) % refs) // js
+            accs[k] = accs[k] + wide * norm[base + g]
     for k in range(count):
-        acc = jnp.zeros((chunks, LANES), jnp.float32)
-        for c in range(comps):
-            for j in range(js):
-                ch = c * refs + k * js + j
-                left = jnp.concatenate([low[ch, p : p + chunks, :] for p in range(span)], axis=1)
-                right = jnp.concatenate([high[ch, p : p + chunks, :] for p in range(span)], axis=1)
-                both = jnp.concatenate([left, right], axis=0).astype(jnp.bfloat16)
-                res = lax.dot_general(
-                    both, filters[ch], (((1,), (1,)), ((), ())), preferred_element_type=jnp.float32
-                )
-                wide = jnp.concatenate([res[:chunks], res[chunks:]], axis=1)
-                acc = acc + wide * norm[ch]
-        total[k] = acc
+        total[k] = accs[k]
     each = chunks // (nslab * nsub)
     for d in range(nslab):
         for e in range(each):
             first = lax.bitwise_xor(here, d) * nsub * each + e
-            keep[d, :, e * LANES : (e + 1) * LANES] = total[:, first + core * each, :]
+            turn = nsub - 1 if d else 0
+            near = first + lax.bitwise_xor(core, turn) * each
+            keep[d, :, e * LANES : (e + 1) * LANES] = total[:, near, :]
             for m in range(1, nsub):
-                other = first + lax.bitwise_xor(core, m) * each
+                other = first + lax.bitwise_xor(core, m ^ turn) * each
                 send[m - 1, d, :, e * LANES : (e + 1) * LANES] = total[:, other, :]
 
 
@@ -176,42 +208,62 @@
     refs = count * js
     chans = comps * refs
     here, core = lax.axis_index("slab"), lax.axis_index("sub")
+    vmem, smem = pl.BlockSpec(memory_space=pltpu.VMEM), pl.BlockSpec(memory_space=pltpu.SMEM)
     half = nloc // nsub
     high = round_up(half, 16)
     rows_slab = comps * high
-    mine = lax.dynamic_slice_in_dim(records.transpose(1, 0, 2), half * core, half, 1)
-    mine = jnp.pad(mine, ((0, 0), (0, high - half), (0, 0))).reshape(rows_slab, width)
-    own = lax.dynamic_slice_in_dim(owner_slots, half * core, half, 0)
-    index = jnp.arange(EXTRA * width, dtype=jnp.int32).reshape(1, EXTRA, width) % high
-    slots = jnp.arange(half, dtype=jnp.int32)[:, None, None]
-    own = jnp.sum(jnp.where(index == slots, own[:, None, None] + 1, 0), axis=0) - 1
-    block = jnp.concatenate([mine, own.astype(records.dtype)], axis=0)
+    if high == half:
+        block = pl.pallas_call(
+            pack_kernel,
+            out_shape=jax.ShapeDtypeStruct((rows_slab + EXTRA, width), records.dtype),
+            in_specs=[smem, pl.BlockSpec(memory_space=pl.ANY)],
+            out_specs=vmem,
+            scratch_shapes=[pltpu.SemaphoreType.DMA((comps,))],
+            name="pack",
+        )(owner_slots, records.transpose(1, 0, 2))
+    else:
+        mine = lax.dynamic_slice_in_dim(records.transpose(1, 0, 2), half * core, half, 1)
+        mine = jnp.pad(mine, ((0, 0), (0, high - half), (0, 0))).reshape(rows_slab, width)
+        own = lax.dynamic_slice_in_dim(owner_slots, half * core, half, 0)
+        index = jnp.arange(EXTRA * width, dtype=jnp.int32).reshape(1, EXTRA, width) % high
+        slots = jnp.arange(half, dtype=jnp.int32)[:, None, None]
+        own = jnp.sum(jnp.where(index == slots, own[:, None, None] + 1, 0), axis=0) - 1
+        block = jnp.concatenate([mine, own.astype(records.dtype)], axis=0)
     if ntmpl <= 8:
         column = [block] + [swapped(block, "tmpl", d) for d in range(1, ntmpl)]
     else:
         column = list(lax.all_gather(block, "tmpl", axis=0))
+    reach = round_up(taps + LANES - 1, LANES)
+    tables = pl.pallas_call(
+        functools.partial(tables_kernel, taps),
+        out_shape=[
+            jax.ShapeDtypeStruct((refs, LANES), jnp.int32),
+            jax.ShapeDtypeStruct((refs, LANES), jnp.int32),
+            jax.ShapeDtypeStruct((refs, time), jnp.float32),
+            jax.ShapeDtypeStruct((2 * LANES, reach), jnp.bfloat16),
+        ],
+        in_specs=[smem, smem, vmem, vmem],
+        out_specs=[vmem] * 4,
+        name="tables",
+    )(station_ids, offsets, gap_start.T, gap_len.T)
+    column, tables = lax.optimization_barrier((column, tables))
     head = jnp.stack(column)
     waves = jnp.stack([part[:rows_slab] for part in column])
     tails = [swapped(waves, "slab", d) for d in range(1, nslab)]
     heads = [head] + [swapped(head, "sub", m) for m in range(1, nsub)]
-    vmem, smem = pl.BlockSpec(memory_space=pltpu.VMEM), pl.BlockSpec(memory_space=pltpu.SMEM)
     depth = round_up(taps + SPAN - 1, LANES)
-    tables = pl.pallas_call(
-        prepare_kernel,
+    bank = pl.pallas_call(
+        filters_kernel,
         out_shape=[
             jax.ShapeDtypeStruct((chans, SPAN, depth), jnp.bfloat16),
             jax.ShapeDtypeStruct((chans, LANES), jnp.float32),
-            jax.ShapeDtypeStruct((refs, LANES), jnp.int32),
-            jax.ShapeDtypeStruct((refs, LANES), jnp.int32),
-            jax.ShapeDtypeStruct((refs, time), jnp.float32),
-            jax.ShapeDtypeStruct((round_up(taps + LANES - 1, LANES), LANES), jnp.bfloat16),
         ],
-        in_specs=[smem, smem, vmem, vmem, vmem],
-        out_specs=[vmem] * 6,
+        in_specs=[vmem],
+        out_specs=[vmem] * 2,
         compiler_params=pltpu.CompilerParams(vmem_limit_bytes=40 << 20),
-        name="prepare",
-    )(station_ids, offsets, gap_start, gap_len, templates.reshape(refs, comps, taps))
-    tails, tables = lax.optimization_barrier((tails, tables))
+        name="filters",
+    )(templates.transpose(1, 2, 0, 3))
+    tails, bank = lax.optimization_barrier((tails, bank))
     lasts = []
     for tail in tails:
         lasts += [tail] + [swapped(tail, "sub", m) for m in range(1, nsub)]
@@ -239,10 +291,12 @@
         ],
         compiler_params=pltpu.CompilerParams(vmem_limit_bytes=40 << 20),
         name="correlate",
-    )(*heads, *lasts, *tables)
+    )(*heads, *lasts, *bank, *tables)
     for m in range(1, nsub):
         keep = keep + swapped(send[m - 1], "sub", m)
-    lines = [keep[0]] + [swapped(keep[d], "slab", d) for d in range(1, nslab)]
+    lines = [keep[0]]
+    for d in range(1, nslab):
+        lines.append(swapped(keep[d], ("slab", "sub"), d * nsub + nsub - 1))
     result = []
     for s in range(nslab):
         line = lines[0]

time: 32.6 us -> 34.7 us (1.064)
  Pallas kernels: 7.62 us -> 9.97 us
  waiting for transfers between devices: 9.44 us -> 8.54 us
    pallas_call x1 -> x3, Pallas kernels: 3.76 us -> 6.45 us  [the longest x1 2.6 us: on_device(): pl.pallas_call(filters_kernel, out_shape=[jax.ShapeDtypeStruct((chans, SP...]
    ppermute x8, waiting for transfers between devices: 9.44 us -> 8.54 us  [swapped(): lax.ppermute(value, axis, [(i, i ^ distance) for i in range(lax.axis_size...]
    another operation x2 -> x1, other arithmetic: 0.04 us -> 0.85 us  [on_device(): head = jnp.stack(column)]
    another operation x3 -> x2, local copies, waits for them, and re-layouts: 0.01 us -> 0.82 us  [on_device(): waves = jnp.stack([part[:rows_slab] for part in column])]
    add x1 -> x0, other arithmetic: 0.73 us -> none  [on_device(): own[:, None, None] + 1]
    unnamed x9 -> x10, local copies, waits for them, and re-layouts: 4.75 us -> 4.2 us
  transfers between devices with their start and end apart: 8 -> 8, of which waited for: 5 -> 5; matrix products, arithmetic and copies ran while one was open for 8% -> 2% of each run, Pallas kernels for 12% -> 13%
where the time goes in v3:
time: 34.7 us; the launch traced here: 34.2 us
  Pallas kernels  9.97 us (29%)
  starting transfers between devices  9.09 us (26%)
  waiting for transfers between devices  8.54 us (25%)
  local copies, waits for them, and re-layouts  5.02 us (14%)
  other arithmetic  1.49 us (4%)
    ppermute x8, starting transfers between devices, swapped(): lax.ppermute(value, axis, [(i, i ^ distance) for i in range(lax.axis_size...  9.09 us
    ppermute x8, waiting for transfers between devices, swapped(): lax.ppermute(value, axis, [(i, i ^ distance) for i in range(lax.axis_size...  8.54 us
    unnamed x10, local copies, waits for them, and re-layouts  4.2 us
    pallas_call x1, Pallas kernels, on_device(): pl.pallas_call(body, out_shape=[jax.ShapeDtypeStruct((nslab, count, each)...  3.52 us
    pallas_call x1, Pallas kernels, on_device(): pl.pallas_call(filters_kernel, out_shape=[jax.ShapeDtypeStruct((chans, SP...  2.6 us
    pallas_call x1, Pallas kernels, on_device(): pl.pallas_call(pack_kernel, out_shape=jax.ShapeDtypeStruct((rows_slab + E...  2.07 us
    pallas_call x1, Pallas kernels, on_device(): pl.pallas_call(functools.partial(tables_kernel, taps), out_shape=[jax.Sha...  1.79 us
    another operation x1, other arithmetic, on_device(): head = jnp.stack(column)  0.85 us
  transfers between devices with their start and end apart: 8, of which 5 were waited for; matrix products, arithmetic and copies ran while one was open for 2% of the time, Pallas kernels for 13%

profile of v3, /device:TPU:0, one launch (start us, length us, event | category | flops | bytes accessed | tf_op | source)
XLA Modules:
  0.0 34.2 jit_solution(554228105355205262)
XLA Ops:
  0.0 2.1 %pack.1 = bf16[56,512]{1,0:T(8,128)(2,1)} custom-call(s32[32]{0:T(128)} %owner_slots.1, bf16[3,32,512]{2,1,0:T(8,128)(2,1)} %bitcast.31), custom_call_target="tpu_custom_call" | custom-call | tf_op jit(solution)/shard_map/pack/pallas_call | solution.py:216
  2.1 3.1 %collective-permute-start = (bf16[56,512]{1,0:T(8,128)(2,1)}, bf16[56,512]{1,0:T(8,128)(2,1)S(1)}, u32[]{:S(2)}, u32[]{:S(2)}) collective-permute-start(bf16[56,512]{1,0:T(8,128)(2,1)} %pack.1), channel_id=1, source_target_pairs={{0,4},{4,0},{8,12},{12,8},{1,5},{5,1},{9,13},{13,9},{2,6},{6,2},{1... | collective-permute-start | bytes 172040 | tf_op jit(solution)/shard_map/ppermute | solution.py:200
  5.2 2.6 %collective-permute-start.1 = (bf16[56,512]{1,0:T(8,128)(2,1)}, bf16[56,512]{1,0:T(8,128)(2,1)S(1)}, u32[]{:S(2)}, u32[]{:S(2)}) collective-permute-start(bf16[56,512]{1,0:T(8,128)(2,1)} %pack.1), channel_id=1, source_target_pairs={{0,8},{4,12},{8,0},{12,4},{1,9},{5,13},{9,1},{13,5},{2,10},{6,14},... | collective-permute-start | bytes 172040 | tf_op jit(solution)/shard_map/ppermute | solution.py:200
  7.8 0.0 collective-permute-start.2
  7.8 1.8 %tables.1 = (s32[40,128]{1,0:T(8,128)}, s32[40,128]{1,0:T(8,128)}, f32[40,1024]{1,0:T(8,128)}, bf16[256,512]{1,0:T(8,128)(2,1)}) custom-call(s32[4,10]{1,0:T(4,128)} %sids.1, s32[4,10]{1,0:T(4,128)} %offs.1, s32[4,128]{1,0:T(4,128)} %bitcast.32, s32[4,128]{1,0:T(4,128)} %bitcast.33), custom_call_target="tpu_custom_call" | custom-call | tf_op jit(solution)/shard_map/tables/pallas_call | solution.py:237
  9.5 0.0 collective-permute-done
  9.6 2.0 %collective-permute-done.1 = bf16[56,512]{1,0:T(8,128)(2,1)S(1)} collective-permute-done((bf16[56,512]{1,0:T(8,128)(2,1)}, bf16[56,512]{1,0:T(8,128)(2,1)S(1)}, u32[]{:S(2)}, u32[]{:S(2)}) %collective-permute-start.1) | collective-permute-done | bytes 57376 | tf_op jit(solution)/shard_map/ppermute | solution.py:200
  11.6 2.4 %collective-permute-done.2 = bf16[56,512]{1,0:T(8,128)(2,1)S(1)} collective-permute-done((bf16[56,512]{1,0:T(8,128)(2,1)}, bf16[56,512]{1,0:T(8,128)(2,1)S(1)}, u32[]{:S(2)}, u32[]{:S(2)}) %collective-permute-start.2) | collective-permute-done | bytes 57376 | tf_op jit(solution)/shard_map/ppermute | solution.py:200
  13.9 0.8 %slice_bitcast_fusion.2 = (bf16[1,48,512]{2,1,0:T(8,128)(2,1)S(1)}, bf16[1,48,512]{2,1,0:T(8,128)(2,1)S(1)}) fusion(bf16[56,512]{1,0:T(8,128)(2,1)S(1)} %collective-permute-done, bf16[56,512]{1,0:T(8,128)(2,1)} %pack.1), kind=kLoop, calls=%fused_computation.4 | loop fusion | bytes 196608 | tf_op jit(solution)/shard_map/stack | solution.py:251
  14.8 1.6 %collective-permute-start.4 = (bf16[4,48,512]{2,1,0:T(8,128)(2,1)S(1)}, bf16[4,48,512]{2,1,0:T(8,128)(2,1)S(1)}, u32[]{:S(2)}, u32[]{:S(2)}) collective-permute-start(bf16[4,48,512]{2,1,0:T(8,128)(2,1)S(1)} %pad_maximum_fusion.1), channel_id=1, source_target_pairs={{0,2},{2,0},{1,3},{3,1},{4,6},{6,4},{5,7},{7,5},{8,10},{10,8},{9,1... | collective-permute-start | bytes 589832 | tf_op jit(solution)/shard_map/ppermute | solution.py:200
  16.4 0.8 %pad_maximum_fusion.args_0_ = bf16[4,56,512]{2,1,0:T(8,128)(2,1)S(1)} fusion(bf16[1,56,512]{2,1,0:T(8,128)(2,1)S(1)} %bitcast.30, bf16[1,56,512]{2,1,0:T(8,128)(2,1)S(1)} %bitcast.29, bf16[1,56,512]{2,1,0:T(8,128)(2,1)S(1)} %bitcast.28, bf16[1,56,512]{2,1,0:T(8,128)(2,1)} %bitcast.27), kind=kLoop, calls=%fused_computation | loop fusion | flops 344064 | bytes 458752 | tf_op jit(solution)/shard_map/stack | solution.py:250
  17.2 0.1 collective-permute-start.3
  17.3 0.0 copy-start.2
  17.3 0.9 %copy-done.2 = bf16[4,10,3,300]{3,0,2,1:T(4,128)(2,1)S(1)} copy-done((bf16[4,10,3,300]{3,0,2,1:T(4,128)(2,1)S(1)}, bf16[4,10,3,300]{3,0,2,1:T(4,128)(2,1)}, u32[]{:S(2)}) %copy-start.2) | copy-done | bytes 72024
  18.2 2.6 %filters.1 = (bf16[120,64,384]{2,1,0:T(8,128)(2,1)S(1)}, f32[120,128]{1,0:T(8,128)S(1)}) custom-call(bf16[10,3,4,300]{3,2,1,0:T(4,128)(2,1)S(1)} %bitcast.25), custom_call_target="tpu_custom_call" | custom-call | tf_op jit(solution)/shard_map/filters/pallas_call | solution.py:255
  20.8 0.0 collective-permute-done.4.args_2_
  20.8 0.6 %collective-permute-start.5 = (bf16[4,48,512]{2,1,0:T(8,128)(2,1)S(1)}, bf16[4,48,512]{2,1,0:T(8,128)(2,1)S(1)}, u32[]{:S(2)}, u32[]{:S(2)}) collective-permute-start(bf16[4,48,512]{2,1,0:T(8,128)(2,1)S(1)} %collective-permute-done.4.args_2_), channel_id=1, source_target_pairs={{0,1},{1,0},{2,3},{3,2},{4,5},{5,4},{6,7},{7,6},{8,9},{9,8},{10,11... | collective-permute-start | bytes 589832 | tf_op jit(solution)/shard_map/ppermute | solution.py:200
  21.4 0.0 collective-permute-done.3.args_1_
  21.4 1.1 %collective-permute-done.5.args_3_ = bf16[4,48,512]{2,1,0:T(8,128)(2,1)S(1)} collective-permute-done((bf16[4,48,512]{2,1,0:T(8,128)(2,1)S(1)}, bf16[4,48,512]{2,1,0:T(8,128)(2,1)S(1)}, u32[]{:S(2)}, u32[]{:S(2)}) %collective-permute-start.5) | collective-permute-done | bytes 196640 | tf_op jit(solution)/shard_map/ppermute | solution.py:200
  22.4 0.0 copy-start
  22.4 0.9 %copy-done = bf16[256,512]{1,0:T(8,128)(2,1)S(1)} copy-done((bf16[256,512]{1,0:T(8,128)(2,1)S(1)}, bf16[256,512]{1,0:T(8,128)(2,1)}, u32[]{:S(2)}) %copy-start) | copy-done | bytes 262168
  23.4 0.0 copy-start.1
  23.4 0.9 %copy-done.1 = f32[40,1024]{1,0:T(8,128)S(1)} copy-done((f32[40,1024]{1,0:T(8,128)S(1)}, f32[40,1024]{1,0:T(8,128)}, u32[]{:S(2)}) %copy-start.1) | copy-done | bytes 163864
  24.3 0.0 copy-start.3
  24.3 0.7 %copy-done.3 = s32[40,128]{1,0:T(8,128)S(1)} copy-done((s32[40,128]{1,0:T(8,128)S(1)}, s32[40,128]{1,0:T(8,128)}, u32[]{:S(2)}) %copy-start.3) | copy-done | bytes 20504
  25.0 0.0 copy-start.4
  25.0 0.7 %copy-done.4 = s32[40,128]{1,0:T(8,128)S(1)} copy-done((s32[40,128]{1,0:T(8,128)S(1)}, s32[40,128]{1,0:T(8,128)}, u32[]{:S(2)}) %copy-start.4) | copy-done | bytes 20504
  25.7 3.5 %correlate.1 = (f32[2,4,256]{2,1,0:T(4,128)S(1)}, f32[1,2,4,256]{3,2,1,0:T(4,128)S(1)}) custom-call(bf16[4,56,512]{2,1,0:T(8,128)(2,1)S(1)} %pad_maximum_fusion.args_0_, bf16[4,56,512]{2,1,0:T(8,128)(2,1)S(1)} %collective-permute-done.3.args_1_, bf16[4,48,512]{2,1,0:T(8,128)(2,1)S(1)} %collective-permute-done.4.args_2_, ...), custom_call_target="tpu_custom_call" | custom-call | tf_op jit(solution)/shard_map/correlate/pallas_call | solution.py:277
  29.3 0.4 %collective-permute-start.6 = (f32[2,4,256]{2,1,0:T(4,128)S(1)}, f32[2,4,256]{2,1,0:T(4,128)S(1)}, u32[]{:S(2)}, u32[]{:S(2)}) collective-permute-start(f32[2,4,256]{2,1,0:T(4,128)S(1)} %bitcast.26), channel_id=1, source_target_pairs={{0,1},{1,0},{2,3},{3,2},{4,5},{5,4},{6,7},{7,6},{8,9},{9,8},{10,11... | collective-permute-start | bytes 24584 | tf_op jit(solution)/shard_map/ppermute | solution.py:200
  29.7 0.8 %collective-permute-done.6 = f32[2,4,256]{2,1,0:T(4,128)S(1)} collective-permute-done((f32[2,4,256]{2,1,0:T(4,128)S(1)}, f32[2,4,256]{2,1,0:T(4,128)S(1)}, u32[]{:S(2)}, u32[]{:S(2)}) %collective-permute-start.6) | collective-permute-done | bytes 8224 | tf_op jit(solution)/shard_map/ppermute | solution.py:200
  30.5 0.8 %collective-permute-start.7 = (f32[4,256]{1,0:T(4,128)S(1)}, f32[4,256]{1,0:T(4,128)S(1)}, u32[]{:S(2)}, u32[]{:S(2)}) collective-permute-start(f32[4,256]{1,0:T(4,128)S(1)} %slice_bitcast_fusion.5), channel_id=1, source_target_pairs={{0,3},{1,2},{2,1},{3,0},{4,7},{5,6},{6,5},{7,4},{8,11},{9,10},{10,... | collective-permute-start | bytes 12296 | tf_op jit(solution)/shard_map/ppermute | solution.py:200
  31.3 2.2 %collective-permute-done.7 = f32[4,256]{1,0:T(4,128)S(1)} collective-permute-done((f32[4,256]{1,0:T(4,128)S(1)}, f32[4,256]{1,0:T(4,128)S(1)}, u32[]{:S(2)}, u32[]{:S(2)}) %collective-permute-start.7) | collective-permute-done | bytes 4128 | tf_op jit(solution)/shard_map/ppermute | solution.py:200
  33.6 0.6 %pad_maximum_fusion.2 = f32[8,256]{1,0:T(8,128)} fusion(f32[4,256]{1,0:T(4,128)S(1)} %get-tuple-element.44, f32[4,256]{1,0:T(4,128)S(1)} %get-tuple-element.43), kind=kLoop, calls=%fused_computation.6 | loop fusion | flops 2048 | bytes 16384 | tf_op jit(solution)/shard_map/concatenate | solution.py:306
  (5 shorter events, 0.1 us)
Async XLA Ops:
  2.1 7.5 %collective-permute-start = (bf16[56,512]{1,0:T(8,128)(2,1)}, bf16[56,512]{1,0:T(8,128)(2,1)S(1)}, u32[]{:S(2)}, u32[]{:S(2)}) collective-permute-start(bf16[56,512]{1,0:T(8,128)(2,1)} %pack.1), channel_id=1, source_target_pairs={{0,4},{4,0},{8,12},{12,8},{1,5},{5,1},{9,13},{13,9},{2,6},{6,2},{1... | collective-permute-start | bytes 172040 | tf_op jit(solution)/shard_map/ppermute | solution.py:200
  5.2 6.4 %collective-permute-start.1 = (bf16[56,512]{1,0:T(8,128)(2,1)}, bf16[56,512]{1,0:T(8,128)(2,1)S(1)}, u32[]{:S(2)}, u32[]{:S(2)}) collective-permute-start(bf16[56,512]{1,0:T(8,128)(2,1)} %pack.1), channel_id=1, source_target_pairs={{0,8},{4,12},{8,0},{12,4},{1,9},{5,13},{9,1},{13,5},{2,10},{6,14},... | collective-permute-start | bytes 172040 | tf_op jit(solution)/shard_map/ppermute | solution.py:200
  7.8 6.2 %collective-permute-start.2 = (bf16[56,512]{1,0:T(8,128)(2,1)}, bf16[56,512]{1,0:T(8,128)(2,1)S(1)}, u32[]{:S(2)}, u32[]{:S(2)}) collective-permute-start(bf16[56,512]{1,0:T(8,128)(2,1)} %pack.1), channel_id=1, source_target_pairs={{0,12},{4,8},{8,4},{12,0},{1,13},{5,9},{9,5},{13,1},{2,14},{6,10},... | collective-permute-start | bytes 172040 | tf_op jit(solution)/shard_map/ppermute | solution.py:200
  14.8 6.0 %collective-permute-start.4 = (bf16[4,48,512]{2,1,0:T(8,128)(2,1)S(1)}, bf16[4,48,512]{2,1,0:T(8,128)(2,1)S(1)}, u32[]{:S(2)}, u32[]{:S(2)}) collective-permute-start(bf16[4,48,512]{2,1,0:T(8,128)(2,1)S(1)} %pad_maximum_fusion.1), channel_id=1, source_target_pairs={{0,2},{2,0},{1,3},{3,1},{4,6},{6,4},{5,7},{7,5},{8,10},{10,8},{9,1... | collective-permute-start | bytes 589832 | tf_op jit(solution)/shard_map/ppermute | solution.py:200
  17.2 4.2 %collective-permute-start.3 = (bf16[4,56,512]{2,1,0:T(8,128)(2,1)S(1)}, bf16[4,56,512]{2,1,0:T(8,128)(2,1)S(1)}, u32[]{:S(2)}, u32[]{:S(2)}) collective-permute-start(bf16[4,56,512]{2,1,0:T(8,128)(2,1)S(1)} %pad_maximum_fusion.args_0_), channel_id=1, source_target_pairs={{0,1},{1,0},{2,3},{3,2},{4,5},{5,4},{6,7},{7,6},{8,9},{9,8},{10,11... | collective-permute-start | bytes 688136 | tf_op jit(solution)/shard_map/ppermute | solution.py:200
  17.3 0.9 %copy-start.2 = (bf16[4,10,3,300]{3,0,2,1:T(4,128)(2,1)S(1)}, bf16[4,10,3,300]{3,0,2,1:T(4,128)(2,1)}, u32[]{:S(2)}) copy-start(bf16[4,10,3,300]{3,0,2,1:T(4,128)(2,1)} %param.11) | copy-start | bytes 216004
  20.8 1.6 %collective-permute-start.5 = (bf16[4,48,512]{2,1,0:T(8,128)(2,1)S(1)}, bf16[4,48,512]{2,1,0:T(8,128)(2,1)S(1)}, u32[]{:S(2)}, u32[]{:S(2)}) collective-permute-start(bf16[4,48,512]{2,1,0:T(8,128)(2,1)S(1)} %collective-permute-done.4.args_2_), channel_id=1, source_target_pairs={{0,1},{1,0},{2,3},{3,2},{4,5},{5,4},{6,7},{7,6},{8,9},{9,8},{10,11... | collective-permute-start | bytes 589832 | tf_op jit(solution)/shard_map/ppermute | solution.py:200
  22.4 0.9 %copy-start = (bf16[256,512]{1,0:T(8,128)(2,1)S(1)}, bf16[256,512]{1,0:T(8,128)(2,1)}, u32[]{:S(2)}) copy-start(bf16[256,512]{1,0:T(8,128)(2,1)} %get-tuple-element.40.args_9_) | copy-start | bytes 786436
  23.4 0.9 %copy-start.1 = (f32[40,1024]{1,0:T(8,128)S(1)}, f32[40,1024]{1,0:T(8,128)}, u32[]{:S(2)}) copy-start(f32[40,1024]{1,0:T(8,128)} %get-tuple-element.39.args_8_) | copy-start | bytes 491524
  24.3 0.7 %copy-start.3 = (s32[40,128]{1,0:T(8,128)S(1)}, s32[40,128]{1,0:T(8,128)}, u32[]{:S(2)}) copy-start(s32[40,128]{1,0:T(8,128)} %get-tuple-element.37.args_6_) | copy-start | bytes 61444
  25.0 0.7 %copy-start.4 = (s32[40,128]{1,0:T(8,128)S(1)}, s32[40,128]{1,0:T(8,128)}, u32[]{:S(2)}) copy-start(s32[40,128]{1,0:T(8,128)} %get-tuple-element.38.args_7_) | copy-start | bytes 61444
  29.3 1.3 %collective-permute-start.6 = (f32[2,4,256]{2,1,0:T(4,128)S(1)}, f32[2,4,256]{2,1,0:T(4,128)S(1)}, u32[]{:S(2)}, u32[]{:S(2)}) collective-permute-start(f32[2,4,256]{2,1,0:T(4,128)S(1)} %bitcast.26), channel_id=1, source_target_pairs={{0,1},{1,0},{2,3},{3,2},{4,5},{5,4},{6,7},{7,6},{8,9},{9,8},{10,11... | collective-permute-start | bytes 24584 | tf_op jit(solution)/shard_map/ppermute | solution.py:200
  30.5 3.0 %collective-permute-start.7 = (f32[4,256]{1,0:T(4,128)S(1)}, f32[4,256]{1,0:T(4,128)S(1)}, u32[]{:S(2)}, u32[]{:S(2)}) collective-permute-start(f32[4,256]{1,0:T(4,128)S(1)} %slice_bitcast_fusion.5), channel_id=1, source_target_pairs={{0,3},{1,2},{2,1},{3,0},{4,7},{5,6},{6,5},{7,4},{8,11},{9,10},{10,... | collective-permute-start | bytes 12296 | tf_op jit(solution)/shard_map/ppermute | solution.py:200

commit v4 on v3

--- a/solution.py
+++ b/solution.py
@@ -219,6 +219,7 @@
             in_specs=[smem, pl.BlockSpec(memory_space=pl.ANY)],
             out_specs=vmem,
             scratch_shapes=[pltpu.SemaphoreType.DMA((comps,))],
+            compiler_params=pltpu.CompilerParams(vmem_limit_bytes=4 << 20),
             name="pack",
         )(owner_slots, records.transpose(1, 0, 2))
     else:
@@ -244,6 +245,7 @@
         ],
         in_specs=[smem, smem, vmem, vmem],
         out_specs=[vmem] * 4,
+        compiler_params=pltpu.CompilerParams(vmem_limit_bytes=8 << 20),
         name="tables",
     )(station_ids, offsets, gap_start.T, gap_len.T)
     column, tables = lax.optimization_barrier((column, tables))
@@ -260,7 +262,7 @@
         ],
         in_specs=[vmem],
         out_specs=[vmem] * 2,
-        compiler_params=pltpu.CompilerParams(vmem_limit_bytes=40 << 20),
+        compiler_params=pltpu.CompilerParams(vmem_limit_bytes=24 << 20),
         name="filters",
     )(templates.transpose(1, 2, 0, 3))
     tails, bank = lax.optimization_barrier((tails, bank))

time: 34.7 us -> 29.8 us (0.86)
  Pallas kernels: 9.97 us -> 7.74 us
  waiting for transfers between devices: 8.54 us -> 7.11 us
  other arithmetic: 1.49 us -> 0.68 us
    ppermute x8, waiting for transfers between devices: 8.54 us -> 7.11 us  [swapped(): lax.ppermute(value, axis, [(i, i ^ distance) for i in range(lax.axis_size...]
    pallas_call x1, Pallas kernels: 2.07 us -> 0.67 us  [on_device(): pl.pallas_call(pack_kernel, out_shape=jax.ShapeDtypeStruct((rows_slab + E...]
    unnamed x10 -> x14, local copies, waits for them, and re-layouts: 4.2 us -> 5.16 us
    pallas_call x1, Pallas kernels: 1.79 us -> 0.94 us  [on_device(): pl.pallas_call(functools.partial(tables_kernel, taps), out_shape=[jax.Sha...]
    another operation x1, other arithmetic: 0.85 us -> 0.03 us  [on_device(): head = jnp.stack(column)]
    another operation x2, local copies, waits for them, and re-layouts: 0.82 us -> 0.02 us  [on_device(): waves = jnp.stack([part[:rows_slab] for part in column])]
  transfers between devices with their start and end apart: 8 -> 8, of which waited for: 5 -> 5; matrix products, arithmetic and copies ran while one was open for 2% -> 0% of each run, Pallas kernels for 13% -> 12%
where the time goes in v4:
time: 29.8 us; the launch traced here: 29.6 us
  starting transfers between devices  8.76 us (29%)
  Pallas kernels  7.74 us (26%)
  waiting for transfers between devices  7.11 us (24%)
  local copies, waits for them, and re-layouts  5.18 us (17%)
  other arithmetic  0.68 us (2%)
    ppermute x8, starting transfers between devices, swapped(): lax.ppermute(value, axis, [(i, i ^ distance) for i in range(lax.axis_size...  8.76 us
    ppermute x8, waiting for transfers between devices, swapped(): lax.ppermute(value, axis, [(i, i ^ distance) for i in range(lax.axis_size...  7.11 us
    unnamed x14, local copies, waits for them, and re-layouts  5.16 us
    pallas_call x1, Pallas kernels, on_device(): pl.pallas_call(body, out_shape=[jax.ShapeDtypeStruct((nslab, count, each)...  3.54 us
    pallas_call x1, Pallas kernels, on_device(): pl.pallas_call(filters_kernel, out_shape=[jax.ShapeDtypeStruct((chans, SP...  2.6 us
    pallas_call x1, Pallas kernels, on_device(): pl.pallas_call(functools.partial(tables_kernel, taps), out_shape=[jax.Sha...  0.94 us
    pallas_call x1, Pallas kernels, on_device(): pl.pallas_call(pack_kernel, out_shape=jax.ShapeDtypeStruct((rows_slab + E...  0.67 us
    concatenate x1, other arithmetic, on_device(): return jnp.concatenate(result, axis=0)  0.61 us
  transfers between devices with their start and end apart: 8, of which 5 were waited for; matrix products, arithmetic and copies ran while one was open for 0% of the time, Pallas kernels for 12%

profile of v4, /device:TPU:0, one launch (start us, length us, event | category | flops | bytes accessed | tf_op | source)
XLA Modules:
  0.0 29.6 jit_solution(5251649332407745769)
XLA Ops:
  0.0 0.0 copy-start
  0.0 0.9 %copy-done = bf16[32,3,512]{2,0,1:T(8,128)(2,1)S(1)} copy-done((bf16[32,3,512]{2,0,1:T(8,128)(2,1)S(1)}, bf16[32,3,512]{2,0,1:T(8,128)(2,1)}, u32[]{:S(2)}) %copy-start) | copy-done | bytes 98328
  0.9 0.0 copy-start.6
  0.9 0.7 %copy-done.6 = s32[32]{0:T(128)S(1)} copy-done((s32[32]{0:T(128)S(1)}, s32[32]{0:T(128)}, u32[]{:S(2)}) %copy-start.6) | copy-done | bytes 152
  1.5 0.7 %pack.1 = bf16[56,512]{1,0:T(8,128)(2,1)S(1)} custom-call(s32[32]{0:T(128)S(1)} %copy-done.6, bf16[3,32,512]{2,1,0:T(8,128)(2,1)S(1)} %bitcast.26), custom_call_target="tpu_custom_call" | custom-call | tf_op jit(solution)/shard_map/pack/pallas_call | solution.py:216
  2.2 3.1 %collective-permute-start = (bf16[56,512]{1,0:T(8,128)(2,1)S(1)}, bf16[56,512]{1,0:T(8,128)(2,1)S(1)}, u32[]{:S(2)}, u32[]{:S(2)}) collective-permute-start(bf16[56,512]{1,0:T(8,128)(2,1)S(1)} %pack.1), channel_id=1, source_target_pairs={{0,4},{4,0},{8,12},{12,8},{1,5},{5,1},{9,13},{13,9},{2,6},{6,2},{1... | collective-permute-start | bytes 172040 | tf_op jit(solution)/shard_map/ppermute | solution.py:200
  5.3 2.6 %collective-permute-start.1 = (bf16[56,512]{1,0:T(8,128)(2,1)S(1)}, bf16[56,512]{1,0:T(8,128)(2,1)S(1)}, u32[]{:S(2)}, u32[]{:S(2)}) collective-permute-start(bf16[56,512]{1,0:T(8,128)(2,1)S(1)} %pack.1), channel_id=1, source_target_pairs={{0,8},{4,12},{8,0},{12,4},{1,9},{5,13},{9,1},{13,5},{2,10},{6,14},... | collective-permute-start | bytes 172040 | tf_op jit(solution)/shard_map/ppermute | solution.py:200
  7.9 0.0 collective-permute-start.2
  7.9 0.0 copy-start.2
  7.9 0.7 %copy-done.2 = s32[4,10]{1,0:T(4,128)S(1)} copy-done((s32[4,10]{1,0:T(4,128)S(1)}, s32[4,10]{1,0:T(4,128)}, u32[]{:S(2)}) %copy-start.2) | copy-done | bytes 184
  8.6 0.0 copy-start.3
  8.6 0.7 %copy-done.3 = s32[4,10]{1,0:T(4,128)S(1)} copy-done((s32[4,10]{1,0:T(4,128)S(1)}, s32[4,10]{1,0:T(4,128)}, u32[]{:S(2)}) %copy-start.3) | copy-done | bytes 184
  9.3 0.0 copy-start.4
  9.3 0.7 %copy-done.4 = s32[128,4]{0,1:T(4,128)S(1)} copy-done((s32[128,4]{0,1:T(4,128)S(1)}, s32[128,4]{0,1:T(4,128)}, u32[]{:S(2)}) %copy-start.4) | copy-done | bytes 2072
  10.0 0.0 copy-start.5
  10.0 0.7 %copy-done.5 = s32[128,4]{0,1:T(4,128)S(1)} copy-done((s32[128,4]{0,1:T(4,128)S(1)}, s32[128,4]{0,1:T(4,128)}, u32[]{:S(2)}) %copy-start.5) | copy-done | bytes 2072
  10.6 0.9 %tables.1 = (s32[40,128]{1,0:T(8,128)S(1)}, s32[40,128]{1,0:T(8,128)S(1)}, f32[40,1024]{1,0:T(8,128)S(1)}, bf16[256,512]{1,0:T(8,128)(2,1)S(1)}) custom-call(s32[4,10]{1,0:T(4,128)S(1)} %copy-done.2, s32[4,10]{1,0:T(4,128)S(1)} %copy-done.3, s32[4,128]{1,0:T(4,128)S(1)} %bitcast.28, s32[4,128]{1,0:T(4,128)S(1)} %bitcast.29), custom_call_target="tpu_custom_call" | custom-call | tf_op jit(solution)/shard_map/tables/pallas_call | solution.py:238
  11.6 0.0 collective-permute-done
  11.6 0.0 collective-permute-done.1
  11.6 2.3 %collective-permute-done.2 = bf16[56,512]{1,0:T(8,128)(2,1)S(1)} collective-permute-done((bf16[56,512]{1,0:T(8,128)(2,1)S(1)}, bf16[56,512]{1,0:T(8,128)(2,1)S(1)}, u32[]{:S(2)}, u32[]{:S(2)}) %collective-permute-start.2) | collective-permute-done | bytes 57376 | tf_op jit(solution)/shard_map/ppermute | solution.py:200
  13.9 1.6 %collective-permute-start.4 = (bf16[4,48,512]{2,1,0:T(8,128)(2,1)S(1)}, bf16[4,48,512]{2,1,0:T(8,128)(2,1)S(1)}, u32[]{:S(2)}, u32[]{:S(2)}) collective-permute-start(bf16[4,48,512]{2,1,0:T(8,128)(2,1)S(1)} %pad_maximum_fusion.1), channel_id=1, source_target_pairs={{0,2},{2,0},{1,3},{3,1},{4,6},{6,4},{5,7},{7,5},{8,10},{10,8},{9,1... | collective-permute-start | bytes 589832 | tf_op jit(solution)/shard_map/ppermute | solution.py:200
  15.5 0.1 collective-permute-start.3
  15.6 0.0 copy-start.1
  15.6 0.9 %copy-done.1 = bf16[4,10,3,300]{3,0,2,1:T(4,128)(2,1)S(1)} copy-done((bf16[4,10,3,300]{3,0,2,1:T(4,128)(2,1)S(1)}, bf16[4,10,3,300]{3,0,2,1:T(4,128)(2,1)}, u32[]{:S(2)}) %copy-start.1) | copy-done | bytes 72024
  16.5 2.6 %filters.1 = (bf16[120,64,384]{2,1,0:T(8,128)(2,1)S(1)}, f32[120,128]{1,0:T(8,128)S(1)}) custom-call(bf16[10,3,4,300]{3,2,1,0:T(4,128)(2,1)S(1)} %bitcast.27), custom_call_target="tpu_custom_call" | custom-call | tf_op jit(solution)/shard_map/filters/pallas_call | solution.py:257
  19.1 0.6 %collective-permute-done.4.args_2_ = bf16[4,48,512]{2,1,0:T(8,128)(2,1)S(1)} collective-permute-done((bf16[4,48,512]{2,1,0:T(8,128)(2,1)S(1)}, bf16[4,48,512]{2,1,0:T(8,128)(2,1)S(1)}, u32[]{:S(2)}, u32[]{:S(2)}) %collective-permute-start.4) | collective-permute-done | bytes 196640 | tf_op jit(solution)/shard_map/ppermute | solution.py:200
  19.7 0.0 collective-permute-start.5
  19.7 0.0 collective-permute-done.3.args_1_
  19.7 1.4 %collective-permute-done.5.args_3_ = bf16[4,48,512]{2,1,0:T(8,128)(2,1)S(1)} collective-permute-done((bf16[4,48,512]{2,1,0:T(8,128)(2,1)S(1)}, bf16[4,48,512]{2,1,0:T(8,128)(2,1)S(1)}, u32[]{:S(2)}, u32[]{:S(2)}) %collective-permute-start.5) | collective-permute-done | bytes 196640 | tf_op jit(solution)/shard_map/ppermute | solution.py:200
  21.1 3.5 %correlate.1 = (f32[2,4,256]{2,1,0:T(4,128)S(1)}, f32[1,2,4,256]{3,2,1,0:T(4,128)S(1)}) custom-call(bf16[4,56,512]{2,1,0:T(8,128)(2,1)S(1)} %pad_maximum_fusion.args_0_, bf16[4,56,512]{2,1,0:T(8,128)(2,1)S(1)} %collective-permute-done.3.args_1_, bf16[4,48,512]{2,1,0:T(8,128)(2,1)S(1)} %collective-permute-done.4.args_2_, ...), custom_call_target="tpu_custom_call" | custom-call | tf_op jit(solution)/shard_map/correlate/pallas_call | solution.py:279
  24.7 0.2 collective-permute-start.6
  24.9 1.0 %collective-permute-done.6 = f32[2,4,256]{2,1,0:T(4,128)S(1)} collective-permute-done((f32[2,4,256]{2,1,0:T(4,128)S(1)}, f32[2,4,256]{2,1,0:T(4,128)S(1)}, u32[]{:S(2)}, u32[]{:S(2)}) %collective-permute-start.6) | collective-permute-done | bytes 8224 | tf_op jit(solution)/shard_map/ppermute | solution.py:200
  25.9 1.3 %collective-permute-start.7 = (f32[4,256]{1,0:T(4,128)S(1)}, f32[4,256]{1,0:T(4,128)S(1)}, u32[]{:S(2)}, u32[]{:S(2)}) collective-permute-start(f32[4,256]{1,0:T(4,128)S(1)} %slice_bitcast_fusion.5), channel_id=1, source_target_pairs={{0,3},{1,2},{2,1},{3,0},{4,7},{5,6},{6,5},{7,4},{8,11},{9,10},{10,... | collective-permute-start | bytes 12296 | tf_op jit(solution)/shard_map/ppermute | solution.py:200
  27.2 1.8 %collective-permute-done.7 = f32[4,256]{1,0:T(4,128)S(1)} collective-permute-done((f32[4,256]{1,0:T(4,128)S(1)}, f32[4,256]{1,0:T(4,128)S(1)}, u32[]{:S(2)}, u32[]{:S(2)}) %collective-permute-start.7) | collective-permute-done | bytes 4128 | tf_op jit(solution)/shard_map/ppermute | solution.py:200
  29.0 0.6 %pad_maximum_fusion.2 = f32[8,256]{1,0:T(8,128)} fusion(f32[4,256]{1,0:T(4,128)S(1)} %get-tuple-element.44, f32[4,256]{1,0:T(4,128)S(1)} %get-tuple-element.43), kind=kLoop, calls=%fused_computation.6 | loop fusion | flops 2048 | bytes 16384 | tf_op jit(solution)/shard_map/concatenate | solution.py:308
  (7 shorter events, 0.1 us)
Async XLA Ops:
  0.0 0.9 %copy-start = (bf16[32,3,512]{2,0,1:T(8,128)(2,1)S(1)}, bf16[32,3,512]{2,0,1:T(8,128)(2,1)}, u32[]{:S(2)}) copy-start(bf16[32,3,512]{2,0,1:T(8,128)(2,1)} %param.7) | copy-start | bytes 294916
  0.9 0.7 %copy-start.6 = (s32[32]{0:T(128)S(1)}, s32[32]{0:T(128)}, u32[]{:S(2)}) copy-start(s32[32]{0:T(128)} %owner_slots.1) | copy-start | bytes 388
  2.2 9.4 %collective-permute-start = (bf16[56,512]{1,0:T(8,128)(2,1)S(1)}, bf16[56,512]{1,0:T(8,128)(2,1)S(1)}, u32[]{:S(2)}, u32[]{:S(2)}) collective-permute-start(bf16[56,512]{1,0:T(8,128)(2,1)S(1)} %pack.1), channel_id=1, source_target_pairs={{0,4},{4,0},{8,12},{12,8},{1,5},{5,1},{9,13},{13,9},{2,6},{6,2},{1... | collective-permute-start | bytes 172040 | tf_op jit(solution)/shard_map/ppermute | solution.py:200
  5.3 6.3 %collective-permute-start.1 = (bf16[56,512]{1,0:T(8,128)(2,1)S(1)}, bf16[56,512]{1,0:T(8,128)(2,1)S(1)}, u32[]{:S(2)}, u32[]{:S(2)}) collective-permute-start(bf16[56,512]{1,0:T(8,128)(2,1)S(1)} %pack.1), channel_id=1, source_target_pairs={{0,8},{4,12},{8,0},{12,4},{1,9},{5,13},{9,1},{13,5},{2,10},{6,14},... | collective-permute-start | bytes 172040 | tf_op jit(solution)/shard_map/ppermute | solution.py:200
  7.9 6.0 %collective-permute-start.2 = (bf16[56,512]{1,0:T(8,128)(2,1)S(1)}, bf16[56,512]{1,0:T(8,128)(2,1)S(1)}, u32[]{:S(2)}, u32[]{:S(2)}) collective-permute-start(bf16[56,512]{1,0:T(8,128)(2,1)S(1)} %pack.1), channel_id=1, source_target_pairs={{0,12},{4,8},{8,4},{12,0},{1,13},{5,9},{9,5},{13,1},{2,14},{6,10},... | collective-permute-start | bytes 172040 | tf_op jit(solution)/shard_map/ppermute | solution.py:200
  7.9 0.7 %copy-start.2 = (s32[4,10]{1,0:T(4,128)S(1)}, s32[4,10]{1,0:T(4,128)}, u32[]{:S(2)}) copy-start(s32[4,10]{1,0:T(4,128)} %sids.1) | copy-start | bytes 484
  8.6 0.7 %copy-start.3 = (s32[4,10]{1,0:T(4,128)S(1)}, s32[4,10]{1,0:T(4,128)}, u32[]{:S(2)}) copy-start(s32[4,10]{1,0:T(4,128)} %offs.1) | copy-start | bytes 484
  9.3 0.7 %copy-start.4 = (s32[128,4]{0,1:T(4,128)S(1)}, s32[128,4]{0,1:T(4,128)}, u32[]{:S(2)}) copy-start(s32[128,4]{0,1:T(4,128)} %param.9) | copy-start | bytes 6148
  10.0 0.7 %copy-start.5 = (s32[128,4]{0,1:T(4,128)S(1)}, s32[128,4]{0,1:T(4,128)}, u32[]{:S(2)}) copy-start(s32[128,4]{0,1:T(4,128)} %param.10) | copy-start | bytes 6148
  13.9 5.7 %collective-permute-start.4 = (bf16[4,48,512]{2,1,0:T(8,128)(2,1)S(1)}, bf16[4,48,512]{2,1,0:T(8,128)(2,1)S(1)}, u32[]{:S(2)}, u32[]{:S(2)}) collective-permute-start(bf16[4,48,512]{2,1,0:T(8,128)(2,1)S(1)} %pad_maximum_fusion.1), channel_id=1, source_target_pairs={{0,2},{2,0},{1,3},{3,1},{4,6},{6,4},{5,7},{7,5},{8,10},{10,8},{9,1... | collective-permute-start | bytes 589832 | tf_op jit(solution)/shard_map/ppermute | solution.py:200
  15.5 4.2 %collective-permute-start.3 = (bf16[4,56,512]{2,1,0:T(8,128)(2,1)S(1)}, bf16[4,56,512]{2,1,0:T(8,128)(2,1)S(1)}, u32[]{:S(2)}, u32[]{:S(2)}) collective-permute-start(bf16[4,56,512]{2,1,0:T(8,128)(2,1)S(1)} %pad_maximum_fusion.args_0_), channel_id=1, source_target_pairs={{0,1},{1,0},{2,3},{3,2},{4,5},{5,4},{6,7},{7,6},{8,9},{9,8},{10,11... | collective-permute-start | bytes 688136 | tf_op jit(solution)/shard_map/ppermute | solution.py:200
  15.6 0.9 %copy-start.1 = (bf16[4,10,3,300]{3,0,2,1:T(4,128)(2,1)S(1)}, bf16[4,10,3,300]{3,0,2,1:T(4,128)(2,1)}, u32[]{:S(2)}) copy-start(bf16[4,10,3,300]{3,0,2,1:T(4,128)(2,1)} %param.11) | copy-start | bytes 216004
  19.7 1.4 %collective-permute-start.5 = (bf16[4,48,512]{2,1,0:T(8,128)(2,1)S(1)}, bf16[4,48,512]{2,1,0:T(8,128)(2,1)S(1)}, u32[]{:S(2)}, u32[]{:S(2)}) collective-permute-start(bf16[4,48,512]{2,1,0:T(8,128)(2,1)S(1)} %collective-permute-done.4.args_2_), channel_id=1, source_target_pairs={{0,1},{1,0},{2,3},{3,2},{4,5},{5,4},{6,7},{7,6},{8,9},{9,8},{10,11... | collective-permute-start | bytes 589832 | tf_op jit(solution)/shard_map/ppermute | solution.py:200
  24.7 1.2 %collective-permute-start.6 = (f32[2,4,256]{2,1,0:T(4,128)S(1)}, f32[2,4,256]{2,1,0:T(4,128)S(1)}, u32[]{:S(2)}, u32[]{:S(2)}) collective-permute-start(f32[2,4,256]{2,1,0:T(4,128)S(1)} %bitcast.30), channel_id=1, source_target_pairs={{0,1},{1,0},{2,3},{3,2},{4,5},{5,4},{6,7},{7,6},{8,9},{9,8},{10,11... | collective-permute-start | bytes 24584 | tf_op jit(solution)/shard_map/ppermute | solution.py:200
  25.9 3.0 %collective-permute-start.7 = (f32[4,256]{1,0:T(4,128)S(1)}, f32[4,256]{1,0:T(4,128)S(1)}, u32[]{:S(2)}, u32[]{:S(2)}) collective-permute-start(f32[4,256]{1,0:T(4,128)S(1)} %slice_bitcast_fusion.5), channel_id=1, source_target_pairs={{0,3},{1,2},{2,1},{3,0},{4,7},{5,6},{6,5},{7,4},{8,11},{9,10},{10,... | collective-permute-start | bytes 12296 | tf_op jit(solution)/shard_map/ppermute | solution.py:200

commit v5 on v3

v5 whole, which is shorter than its diff:
```python
import functools

import jax
import jax.numpy as jnp
from jax import lax
from jax.experimental import pallas as pl
from jax.experimental.pallas import tpu as pltpu
from jax.sharding import PartitionSpec as P

LANES = 128
SPAN = 64
EXTRA = 8


def round_up(value, step):
    return -(-value // step) * step


def pack_kernel(owner_slots, records, block, owners, sems):
    comps, _, width = records.shape
    half = (block.shape[0] - EXTRA) // comps
    first = pl.multiple_of(lax.axis_index("sub") * half, half)
    copies = [pltpu.make_async_copy(owner_slots, owners, sems.at[comps])]
    for c in range(comps):
        source, place = records.at[c, pl.ds(first, half), :], block.at[c * half : (c + 1) * half, :]
        copies.append(pltpu.make_async_copy(source, place, sems.at[c]))
    for copy in copies:
        copy.start()
    copies[0].wait()
    lane = lax.rem(lax.broadcasted_iota(jnp.int32, (EXTRA, width), 1), half)
    line = jnp.full((EXTRA, width), -1, jnp.int32)
    for i in range(half):
        line = jnp.where(lane == i, owners[first + i], line)
    block[comps * half :, :] = line.astype(jnp.float32).astype(block.dtype)
    for copy in copies[1:]:
        copy.wait()


def tables_kernel(taps, nfar, *args):
    fars, args = args[:nfar], args[nfar:]
    sids_in, offs_in, start_in, len_in, sid_col, off_col, mask, band = args[:8]
    sids, offs, gap_start, gap_len, sems = args[8:]
    pairs = ((sids_in, sids), (offs_in, offs), (start_in, gap_start), (len_in, gap_len))
    copies = [pltpu.make_async_copy(source, place, sems.at[i]) for i, (source, place) in enumerate(pairs)]
    for copy in copies:
        copy.start()
    rows = lax.rem(lax.broadcasted_iota(jnp.int32, band.shape, 0), LANES)
    cols = lax.broadcasted_iota(jnp.int32, band.shape, 1)
    lead = rows + (cols // LANES) * LANES - lax.rem(cols, LANES)
    band[...] = jnp.where((lead >= 0) & (lead < taps), 1.0, 0.0).astype(jnp.bfloat16)
    for copy in copies:
        copy.wait()
    count, js = sids.shape
    refs = count * js
    nstation = gap_start.shape[1]
    for k in range(count):
        for j in range(js):
            row = j * count + k
            off_col[row, :] = jnp.full((LANES,), offs[k, j], jnp.int32)
            for d, source in enumerate((sids,) + tuple(fars)):
                sid_col[d, row, :] = jnp.full((LANES,), source[k, j], jnp.int32)
    own = lax.broadcasted_iota(jnp.int32, (refs, nstation), 1) == sid_col[0, :, :nstation]
    starts = gap_start[...].astype(jnp.float32)
    ends = starts + gap_len[...].astype(jnp.float32)
    live = jnp.ones(mask.shape, jnp.float32)
    times = lax.broadcasted_iota(jnp.int32, mask.shape, 1).astype(jnp.float32)
    for g in range(starts.shape[0]):
        first = jnp.sum(jnp.where(own, starts[g : g + 1], 0.0), axis=1, keepdims=True)
        last = jnp.sum(jnp.where(own, ends[g : g + 1], 0.0), axis=1, keepdims=True)
        live = jnp.where((times >= first) & (times < last), 0.0, live)
    mask[...] = live


def filters_kernel(begin, templates, filters, scale):
    js, comps, count, taps = templates.shape
    groups, depth, _ = filters.shape

    def one_group(i, carry):
        g = begin + i
        wave = templates[lax.rem(g, js), g // js].astype(jnp.float32)
        wave = jnp.concatenate([wave, jnp.zeros((count, depth - taps), jnp.float32)], axis=1)
        power = jnp.sum(wave * wave, axis=1, keepdims=True) / taps
        factor = 1.0 / (taps * jnp.sqrt(power + 1e-06))
        rows = []
        for k in range(count):
            scale[pl.ds(i * count + k, 1), :] = jnp.broadcast_to(factor[k : k + 1], (1, LANES))
            row = jnp.broadcast_to(wave[k : k + 1], (SPAN, depth))
            rows.append(pltpu.roll(row, 0, 1, stride=1, stride_axis=0))
        filters[i] = jnp.concatenate(rows, axis=0).T.astype(jnp.bfloat16)
        return carry

    lax.fori_loop(0, groups, one_group, 0)


def select_kernel(comps, rows_slab, nsub, *args):
    heads, (sid_col, mask, near), fars = args[:nsub], args[nsub : nsub + 3], args[nsub + 3 :]
    refs = mask.shape[0]
    ntmpl, _, width = heads[0].shape
    here = lax.axis_index("slab")
    depth = nsub * ntmpl * rows_slab
    owner = []
    for q in range(round_up(depth, width) // width):
        lane = lax.broadcasted_iota(jnp.int32, (1, width), 1) + q * width
        line = jnp.full((1, width), -1.0, jnp.float32)
        for b in range(nsub * ntmpl):
            tail = heads[b // ntmpl][b % ntmpl, rows_slab : rows_slab + EXTRA, :].astype(jnp.float32)
            inside = (lane >= b * rows_slab) & (lane < (b + 1) * rows_slab)
            line = jnp.where(inside, tail[q : q + 1], line)
        owner.append(line)
    owner = jnp.concatenate(owner, axis=1)[:, :depth]
    row = lax.broadcasted_iota(jnp.int32, (1, depth), 1)
    row = lax.rem(row, rows_slab) // (rows_slab // comps)
    stack = jnp.concatenate([part[z, :rows_slab, :] for part in heads for z in range(ntmpl)], axis=0)
    owners = [jnp.where(row == c, owner, -1.0) for c in range(comps)]
    for d, out in enumerate((near,) + tuple(fars)):
        wanted = sid_col[d, :, :1].astype(jnp.float32)
        pick = [jnp.where(owners[c] == wanted, 1.0, 0.0).astype(jnp.bfloat16) for c in range(comps)]
        got = jnp.dot(jnp.concatenate(pick, axis=0), stack, preferred_element_type=jnp.float32)
        if d:
            out[...] = got.astype(out.dtype)
        else:
            live = mask[:, pl.ds(pl.multiple_of(here * width, LANES), width)]
            for c in range(comps):
                out[c * refs : (c + 1) * refs, :] = got[c * refs : (c + 1) * refs] * live


def correlate_kernel(nslab, nsub, taps, nbank, *args):
    near, fars, args = args[0], args[1:nslab], args[nslab:]
    banks, scales, args = args[:nbank], args[nbank : 2 * nbank], args[2 * nbank :]
    off_col, mask, band, keep, send, segs, low, high, norm, total = args
    refs, time = mask.shape
    chans, width = near.shape
    comps = chans // refs
    chunks = time // LANES
    count = keep.shape[1]
    tall = low.shape[1]
    here, core = lax.axis_index("slab"), lax.axis_index("sub")
    for d in range(nslab):
        spot = pl.ds(pl.multiple_of(lax.bitwise_xor(here, d) * width, LANES), width)
        if d == 0:
            segs[:, spot] = near[...]
        else:
            live = mask[:, spot]
            for c in range(comps):
                got = fars[d - 1][c * refs : (c + 1) * refs, :].astype(jnp.float32)
                segs[c * refs : (c + 1) * refs, spot] = got * live
    lane = lax.broadcasted_iota(jnp.int32, (8, LANES), 1)
    zero = jnp.zeros((8, LANES), jnp.float32)
    for i in range(chans // 8):
        ref_row = (i * 8) % refs
        off = off_col[ref_row : ref_row + 8, :]
        place = lax.bitwise_and(lane + off, LANES - 1)
        fine = lax.bitwise_and(off, LANES - 1)
        close = lane + fine < LANES
        far = off >= LANES
        turned = [
            jnp.take_along_axis(segs[i * 8 : i * 8 + 8, r * LANES : (r + 1) * LANES], place, axis=1)
            for r in range(chunks)
        ]
        turned += [zero, zero]
        moved = [jnp.where(close, turned[r], turned[r + 1]) for r in range(chunks + 1)]
        mine = [jnp.where(far, moved[r + 1], moved[r]) for r in range(chunks)] + [zero]
        for r in range(chunks):
            segs[i * 8 : i * 8 + 8, r * LANES : (r + 1) * LANES] = mine[r]
            low[pl.ds(i * 8, 8), r, :] = mine[r]
            half = jnp.where(lane < LANES - SPAN, pltpu.roll(mine[r], SPAN, 1), pltpu.roll(mine[r + 1], SPAN, 1))
            high[pl.ds(i * 8, 8), r, :] = half
        for r in range(chunks, tall):
            low[pl.ds(i * 8, 8), r, :] = zero
            high[pl.ds(i * 8, 8), r, :] = zero
    reach = band.shape[1] // LANES
    scale = jnp.concatenate([part[...] for part in scales], axis=0)
    sums = {}
    for r in reversed(range(chunks)):
        part = segs[:, r * LANES : (r + 1) * LANES]
        power = part * part
        lead = power.astype(jnp.bfloat16)
        rest = (power - lead.astype(jnp.float32)).astype(jnp.bfloat16)
        sums[r] = jnp.dot(jnp.concatenate([lead, rest], axis=1), band[...], preferred_element_type=jnp.float32)
        window = sums[r][:, :LANES]
        for p in range(1, min(reach, chunks - r)):
            window = window + sums[r + p][:, p * LANES : (p + 1) * LANES]
        factor = scale * lax.rsqrt(window / taps + 1e-06)
        for i in range(chans // 8):
            norm[pl.ds(i * 8, 8), r, :] = factor[i * 8 : i * 8 + 8]
    span = banks[0].shape[1] // LANES
    accs = [jnp.zeros((chunks, LANES), jnp.float32) for _ in range(count)]
    side = lax.broadcasted_iota(jnp.int32, (chunks, LANES), 1) < SPAN
    weights = [(bank, i) for bank in banks for i in range(bank.shape[0])]
    for g, (bank, i) in enumerate(weights):
        base = g * count
        rows = []
        for ch in range(base, base + count):
            for source in (low, high):
                rows.append(jnp.concatenate([source[ch, p : p + chunks, :] for p in range(span)], axis=1))
        both = jnp.concatenate(rows, axis=0).astype(jnp.bfloat16)
        res = jnp.dot(both, bank[i], preferred_element_type=jnp.float32)
        for k in range(count):
            left = (k // 2) * LANES
            tile = res[2 * k * chunks : 2 * (k + 1) * chunks, left : left + LANES]
            early, late = tile[:chunks], tile[chunks:]
            if k % 2 == 0:
                wide = jnp.where(side, early, pltpu.roll(late, SPAN, 1))
            else:
                wide = jnp.where(side, pltpu.roll(early, SPAN, 1), late)
            accs[k] = accs[k] + wide * norm[base + k]
    for k in range(count):
        total[k] = accs[k]
    each = chunks // (nslab * nsub)
    for d in range(nslab):
        for e in range(each):
            first = lax.bitwise_xor(here, d) * nsub * each + e
            turn = nsub - 1 if d else 0
            mine = first + lax.bitwise_xor(core, turn) * each
            keep[d, :, e * LANES : (e + 1) * LANES] = total[:, mine, :]
            for m in range(1, nsub):
                other = first + lax.bitwise_xor(core, m ^ turn) * each
                send[m - 1, d, :, e * LANES : (e + 1) * LANES] = total[:, other, :]


def swapped(value, axis, distance):
    return lax.ppermute(value, axis, [(i, i ^ distance) for i in range(lax.axis_size(axis))])


def params(mib):
    return pltpu.CompilerParams(vmem_limit_bytes=mib << 20)


def on_device(records, owner_slots, gap_start, gap_len, templates, station_ids, offsets):
    nloc, comps, width = records.shape
    count, js, _, taps = templates.shape
    nslab, nsub, ntmpl = (lax.axis_size(name) for name in ("slab", "sub", "tmpl"))
    time = width * nslab
    refs = count * js
    chans = comps * refs
    here, core = lax.axis_index("slab"), lax.axis_index("sub")
    vmem, smem = pl.BlockSpec(memory_space=pltpu.VMEM), pl.BlockSpec(memory_space=pltpu.SMEM)
    hbm = pl.BlockSpec(memory_space=pltpu.HBM)
    half = nloc // nsub
    high = round_up(half, 16)
    rows_slab = comps * high
    if high == half:
        block = pl.pallas_call(
            pack_kernel,
            out_shape=jax.ShapeDtypeStruct((rows_slab + EXTRA, width), records.dtype),
            in_specs=[hbm, hbm],
            out_specs=vmem,
            scratch_shapes=[pltpu.SMEM((nloc,), jnp.int32), pltpu.SemaphoreType.DMA((comps + 1,))],
            compiler_params=params(4),
            name="pack",
        )(owner_slots, records.transpose(1, 0, 2))
    else:
        mine = lax.dynamic_slice_in_dim(records.transpose(1, 0, 2), half * core, half, 1)
        mine = jnp.pad(mine, ((0, 0), (0, high - half), (0, 0))).reshape(rows_slab, width)
        own = lax.dynamic_slice_in_dim(owner_slots, half * core, half, 0)
        index = jnp.arange(EXTRA * width, dtype=jnp.int32).reshape(1, EXTRA, width) % high
        slots = jnp.arange(half, dtype=jnp.int32)[:, None, None]
        own = jnp.sum(jnp.where(index == slots, own[:, None, None] + 1, 0), axis=0) - 1
        block = jnp.concatenate([mine, own.astype(records.dtype)], axis=0)
    if ntmpl <= 8:
        column = [block] + [swapped(block, "tmpl", d) for d in range(1, ntmpl)]
    else:
        column = list(lax.all_gather(block, "tmpl", axis=0))
    asked = [swapped(station_ids, "slab", d) for d in range(1, nslab)]
    reach = round_up(taps + LANES - 1, LANES)
    sid_col, off_col, mask, band = pl.pallas_call(
        functools.partial(tables_kernel, taps, nslab - 1),
        out_shape=[
            jax.ShapeDtypeStruct((nslab, refs, LANES), jnp.int32),
            jax.ShapeDtypeStruct((refs, LANES), jnp.int32),
            jax.ShapeDtypeStruct((refs, time), jnp.float32),
            jax.ShapeDtypeStruct((2 * LANES, reach), jnp.bfloat16),
        ],
        in_specs=[smem] * (nslab - 1) + [hbm] * 4,
        out_specs=[vmem] * 4,
        scratch_shapes=[
            pltpu.SMEM(station_ids.shape, jnp.int32),
            pltpu.SMEM(offsets.shape, jnp.int32),
            pltpu.VMEM(gap_start.T.shape, jnp.int32),
            pltpu.VMEM(gap_len.T.shape, jnp.int32),
            pltpu.SemaphoreType.DMA((4,)),
        ],
        compiler_params=params(8),
        name="tables",
    )(*asked, station_ids, offsets, gap_start.T, gap_len.T)
    depth = round_up(taps + SPAN - 1, LANES)
    waves = templates.transpose(1, 2, 0, 3)

    def bank(begin, groups, source):
        return pl.pallas_call(
            functools.partial(filters_kernel, begin),
            out_shape=[
                jax.ShapeDtypeStruct((groups, depth, count * SPAN), jnp.bfloat16),
                jax.ShapeDtypeStruct((groups * count, LANES), jnp.float32),
            ],
            in_specs=[vmem],
            out_specs=[vmem] * 2,
            compiler_params=params(16),
            name="filters",
        )(source)

    groups = comps * js
    early = groups // 2 // 2 * 2
    bank_a, scale_a = bank(0, early, waves)
    column, bank_a, mask = lax.optimization_barrier((column, bank_a, mask))
    head = jnp.stack(column)
    heads = [head] + [swapped(head, "sub", m) for m in range(1, nsub)]
    near, *fars = pl.pallas_call(
        functools.partial(select_kernel, comps, rows_slab, nsub),
        out_shape=[jax.ShapeDtypeStruct((chans, width), jnp.float32)]
        + [jax.ShapeDtypeStruct((chans, width), records.dtype)] * (nslab - 1),
        in_specs=[vmem] * (nsub + 2),
        out_specs=[vmem] * nslab,
        compiler_params=params(16),
        name="select",
    )(*heads, sid_col, mask)
    fars = [swapped(far, "slab", d + 1) for d, far in enumerate(fars)]
    bank_b, scale_b = bank(early, groups - early, waves)
    fars, bank_b = lax.optimization_barrier((fars, bank_b))
    chunks = time // LANES
    each = width // nsub
    tall = chunks + 8
    keep, send = pl.pallas_call(
        functools.partial(correlate_kernel, nslab, nsub, taps, 2),
        out_shape=[
            jax.ShapeDtypeStruct((nslab, count, each), jnp.float32),
            jax.ShapeDtypeStruct((nsub - 1, nslab, count, each), jnp.float32),
        ],
        in_specs=[vmem] * (nslab + 7),
        out_specs=[vmem] * 2,
        scratch_shapes=[
            pltpu.VMEM((chans, time), jnp.float32),
            pltpu.VMEM((chans, tall, LANES), jnp.float32),
            pltpu.VMEM((chans, tall, LANES), jnp.float32),
            pltpu.VMEM((chans, chunks, LANES), jnp.float32),
            pltpu.VMEM((count, chunks, LANES), jnp.float32),
        ],
        compiler_params=params(32),
        name="correlate",
    )(near, *fars, bank_a, bank_b, scale_a, scale_b, off_col, mask, band)
    for m in range(1, nsub):
        keep = keep + swapped(send[m - 1], "sub", m)
    lines = [keep[0]]
    for d in range(1, nslab):
        lines.append(swapped(keep[d], ("slab", "sub"), d * nsub + nsub - 1))
    result = []
    for s in range(nslab):
        line = lines[0]
        for d in range(1, nslab):
            line = jnp.where((here ^ d) == s, lines[d], line)
        result.append(line)
    return jnp.concatenate(result, axis=0)


def solution(mesh):
    in_specs = (
        P(("grp", "tmpl"), None, "slab"),
        P(("grp", "tmpl")),
        P("grp", None),
        P("grp", None),
        P(("grp", "tmpl", "slab"), "sub", None, None),
        P(("grp", "tmpl", "slab"), "sub"),
        P(("grp", "tmpl", "slab"), "sub"),
    )
    out_specs = P(("grp", "tmpl"), ("slab", "sub"))
    return jax.shard_map(
        on_device, mesh=mesh, in_specs=in_specs, out_specs=out_specs, check_vma=False
    )
```

time: 34.7 us -> 33 us (0.951)
  waiting for transfers between devices: 8.54 us -> 4.9 us
  Pallas kernels: 9.97 us -> 12 us
  local copies, waits for them, and re-layouts: 5.02 us -> 6.05 us
  other arithmetic: 1.49 us -> 0.65 us
    ppermute x8, waiting for transfers between devices: 8.54 us -> 4.9 us  [swapped(): lax.ppermute(value, axis, [(i, i ^ distance) for i in range(lax.axis_size...]
    pallas_call x3 -> x5, Pallas kernels: 7.9 us -> 11.3 us  [the longest x2 7.09 us: bank(): pl.pallas_call(functools.partial(filters_kernel, begin), out_shape=[jax.S...]
    unnamed x10 -> x16, local copies, waits for them, and re-layouts: 4.2 us -> 6.05 us
    pallas_call x1, Pallas kernels: 2.07 us -> 0.61 us  [on_device(): pl.pallas_call(pack_kernel, out_shape=jax.ShapeDtypeStruct((rows_slab + E...]
    another operation x1, other arithmetic: 0.85 us -> 0.03 us  [on_device(): head = jnp.stack(column)]
    another operation x2 -> x0, local copies, waits for them, and re-layouts: 0.82 us -> none  [on_device(): waves = jnp.stack([part[:rows_slab] for part in column])]
  transfers between devices with their start and end apart: 8 -> 8, of which waited for: 5 -> 4; matrix products, arithmetic and copies ran while one was open for 2% -> 0% of each run, Pallas kernels for 13% -> 26%
where the time goes in v5:
time: 33 us; the launch traced here: 32.7 us
  Pallas kernels  12 us (36%)
  starting transfers between devices  9.06 us (27%)
  local copies, waits for them, and re-layouts  6.05 us (18%)
  waiting for transfers between devices  4.9 us (15%)
  other arithmetic  0.65 us (2%)
    ppermute x8, starting transfers between devices, swapped(): lax.ppermute(value, axis, [(i, i ^ distance) for i in range(lax.axis_size...  9.06 us
    pallas_call x2, Pallas kernels, bank(): pl.pallas_call(functools.partial(filters_kernel, begin), out_shape=[jax.S...  7.09 us
    unnamed x16, local copies, waits for them, and re-layouts  6.05 us
    ppermute x8, waiting for transfers between devices, swapped(): lax.ppermute(value, axis, [(i, i ^ distance) for i in range(lax.axis_size...  4.9 us
    pallas_call x1, Pallas kernels, on_device(): pl.pallas_call(functools.partial(correlate_kernel, nslab, nsub, taps, 2),...  2.52 us
    pallas_call x1, Pallas kernels, on_device(): pl.pallas_call(functools.partial(tables_kernel, taps, nslab - 1), out_sha...  1.4 us
  transfers between devices with their start and end apart: 8, of which 4 were waited for; matrix products, arithmetic and copies ran while one was open for 0% of the time, Pallas kernels for 26%

profile of v5, /device:TPU:0, one launch (start us, length us, event | category | flops | bytes accessed | tf_op | source)
XLA Modules:
  0.0 32.7 jit_solution(10932580635107385947)
XLA Ops:
  0.0 0.0 copy-start.2
  0.0 0.9 %copy-done.2 = bf16[32,3,512]{2,0,1:T(8,128)(2,1)S(1)} copy-done((bf16[32,3,512]{2,0,1:T(8,128)(2,1)S(1)}, bf16[32,3,512]{2,0,1:T(8,128)(2,1)}, u32[]{:S(2)}) %copy-start.2) | copy-done | bytes 98328
  0.9 0.0 copy-start.7
  0.9 0.7 %copy-done.7 = s32[32]{0:T(128)S(1)} copy-done((s32[32]{0:T(128)S(1)}, s32[32]{0:T(128)}, u32[]{:S(2)}) %copy-start.7) | copy-done | bytes 152
  1.5 0.6 %pack.1 = bf16[56,512]{1,0:T(8,128)(2,1)S(1)} custom-call(s32[32]{0:T(128)S(1)} %copy-done.7, bf16[3,32,512]{2,1,0:T(8,128)(2,1)S(1)} %bitcast.20), custom_call_target="tpu_custom_call" | custom-call | tf_op jit(solution)/shard_map/pack/pallas_call | solution.py:243
  2.2 3.1 %collective-permute-start = (bf16[56,512]{1,0:T(8,128)(2,1)S(1)}, bf16[56,512]{1,0:T(8,128)(2,1)S(1)}, u32[]{:S(2)}, u32[]{:S(2)}) collective-permute-start(bf16[56,512]{1,0:T(8,128)(2,1)S(1)} %pack.1), channel_id=1, source_target_pairs={{0,4},{4,0},{8,12},{12,8},{1,5},{5,1},{9,13},{13,9},{2,6},{6,2},{1... | collective-permute-start | bytes 172040 | tf_op jit(solution)/shard_map/ppermute | solution.py:222
  5.3 2.6 %collective-permute-start.1 = (bf16[56,512]{1,0:T(8,128)(2,1)S(1)}, bf16[56,512]{1,0:T(8,128)(2,1)S(1)}, u32[]{:S(2)}, u32[]{:S(2)}) collective-permute-start(bf16[56,512]{1,0:T(8,128)(2,1)S(1)} %pack.1), channel_id=1, source_target_pairs={{0,8},{4,12},{8,0},{12,4},{1,9},{5,13},{9,1},{13,5},{2,10},{6,14},... | collective-permute-start | bytes 172040 | tf_op jit(solution)/shard_map/ppermute | solution.py:222
  7.8 0.0 collective-permute-start.2
  7.8 1.7 %collective-permute-start.3 = (s32[4,10]{1,0:T(4,128)}, s32[4,10]{1,0:T(4,128)S(1)}, u32[]{:S(2)}, u32[]{:S(2)}) collective-permute-start(s32[4,10]{1,0:T(4,128)} %args_1_.4), channel_id=1, source_target_pairs={{0,2},{2,0},{1,3},{3,1},{4,6},{6,4},{5,7},{7,5},{8,10},{10,8},{9,1... | collective-permute-start | bytes 488 | tf_op jit(solution)/shard_map/ppermute | solution.py:222
  9.6 0.0 copy-start
  9.6 0.9 %copy-done = bf16[4,10,3,300]{3,0,2,1:T(4,128)(2,1)S(1)} copy-done((bf16[4,10,3,300]{3,0,2,1:T(4,128)(2,1)S(1)}, bf16[4,10,3,300]{3,0,2,1:T(4,128)(2,1)}, u32[]{:S(2)}) %copy-start) | copy-done | bytes 72024
  10.4 3.3 %filters.2 = (bf16[14,384,256]{2,1,0:T(8,128)(2,1)S(1)}, f32[56,128]{1,0:T(8,128)S(1)}) custom-call(bf16[10,3,4,300]{3,2,1,0:T(4,128)(2,1)S(1)} %bitcast.17), custom_call_target="tpu_custom_call" | custom-call | tf_op jit(solution)/shard_map/filters/pallas_call | solution.py:290
  13.8 0.0 collective-permute-done.3.args_0_
  13.8 0.0 copy-start.3
  13.8 0.7 %copy-done.3 = s32[4,10]{1,0:T(4,128)S(1)} copy-done((s32[4,10]{1,0:T(4,128)S(1)}, s32[4,10]{1,0:T(4,128)}, u32[]{:S(2)}) %copy-start.3) | copy-done | bytes 184
  14.5 0.0 copy-start.4
  14.5 0.7 %copy-done.4 = s32[4,10]{1,0:T(4,128)S(1)} copy-done((s32[4,10]{1,0:T(4,128)S(1)}, s32[4,10]{1,0:T(4,128)}, u32[]{:S(2)}) %copy-start.4) | copy-done | bytes 184
  15.1 0.0 copy-start.5
  15.1 0.7 %copy-done.5 = s32[128,4]{0,1:T(4,128)S(1)} copy-done((s32[128,4]{0,1:T(4,128)S(1)}, s32[128,4]{0,1:T(4,128)}, u32[]{:S(2)}) %copy-start.5) | copy-done | bytes 2072
  15.8 0.0 copy-start.6
  15.8 0.7 %copy-done.6 = s32[128,4]{0,1:T(4,128)S(1)} copy-done((s32[128,4]{0,1:T(4,128)S(1)}, s32[128,4]{0,1:T(4,128)}, u32[]{:S(2)}) %copy-start.6) | copy-done | bytes 2072
  16.5 1.4 %tables.1 = (s32[2,40,128]{2,1,0:T(8,128)S(1)}, s32[40,128]{1,0:T(8,128)S(1)}, f32[40,1024]{1,0:T(8,128)S(1)}, bf16[256,512]{1,0:T(8,128)(2,1)S(1)}) custom-call(s32[4,10]{1,0:T(4,128)S(1)} %collective-permute-done.3.args_0_, s32[4,10]{1,0:T(4,128)S(1)} %copy-done.3, s32[4,10]{1,0:T(4,128)S(1)} %copy-done.4, s32[4,128]{1,0:T(4,128)S(1)} %bitcast.21, ...), custom_call_target="tpu_custom_call" | custom-call | tf_op jit(solution)/shard_map/tables/pallas_call | solution.py:266
  17.9 0.0 collective-permute-done
  17.9 0.0 collective-permute-done.1
  17.9 0.0 collective-permute-done.2
  18.0 0.1 collective-permute-start.4
  18.1 1.5 %collective-permute-done.4.args_1_ = bf16[4,56,512]{2,1,0:T(8,128)(2,1)S(1)} collective-permute-done((bf16[4,56,512]{2,1,0:T(8,128)(2,1)S(1)}, bf16[4,56,512]{2,1,0:T(8,128)(2,1)S(1)}, u32[]{:S(2)}, u32[]{:S(2)}) %collective-permute-start.4) | collective-permute-done | bytes 229408 | tf_op jit(solution)/shard_map/ppermute | solution.py:222
  19.5 0.3 %select.1 = (f32[120,512]{1,0:T(8,128)S(1)}, bf16[120,512]{1,0:T(8,128)(2,1)S(1)}) custom-call(bf16[4,56,512]{2,1,0:T(8,128)(2,1)S(1)} %pad_maximum_fusion.args_0_, bf16[4,56,512]{2,1,0:T(8,128)(2,1)S(1)} %collective-permute-done.4.args_1_, s32[2,40,128]{2,1,0:T(8,128)S(1)} %get-tuple-element.31.args_2_, f32[40,1024]{1,0:T(8,128)S(1)} %get-tuple-element.32.args_3_.args_7_), custom_call_target="tpu_custom_call" | custom-call | tf_op jit(solution)/shard_map/select/pallas_call | solution.py:308
  19.9 0.4 %collective-permute-start.5 = (bf16[120,512]{1,0:T(8,128)(2,1)S(1)}, bf16[120,512]{1,0:T(8,128)(2,1)S(1)}, u32[]{:S(2)}, u32[]{:S(2)}) collective-permute-start(bf16[120,512]{1,0:T(8,128)(2,1)S(1)} %get-tuple-element.34), channel_id=1, source_target_pairs={{0,2},{2,0},{1,3},{3,1},{4,6},{6,4},{5,7},{7,5},{8,10},{10,8},{9,1... | collective-permute-start | bytes 368648 | tf_op jit(solution)/shard_map/ppermute | solution.py:222
  20.3 0.0 copy-start.1
  20.3 0.9 %copy-done.1 = bf16[4,10,3,300]{3,0,2,1:T(4,128)(2,1)S(1)} copy-done((bf16[4,10,3,300]{3,0,2,1:T(4,128)(2,1)S(1)}, bf16[4,10,3,300]{3,0,2,1:T(4,128)(2,1)}, u32[]{:S(2)}) %copy-start.1) | copy-done | bytes 72024
  21.2 3.8 %filters.3 = (bf16[16,384,256]{2,1,0:T(8,128)(2,1)S(1)}, f32[64,128]{1,0:T(8,128)S(1)}) custom-call(bf16[10,3,4,300]{3,2,1,0:T(4,128)(2,1)S(1)} %bitcast.18), custom_call_target="tpu_custom_call" | custom-call | tf_op jit(solution)/shard_map/filters/pallas_call | solution.py:290
  24.9 0.4 %collective-permute-done.5.args_1_ = bf16[120,512]{1,0:T(8,128)(2,1)S(1)} collective-permute-done((bf16[120,512]{1,0:T(8,128)(2,1)S(1)}, bf16[120,512]{1,0:T(8,128)(2,1)S(1)}, u32[]{:S(2)}, u32[]{:S(2)}) %collective-permute-start.5) | collective-permute-done | bytes 122912 | tf_op jit(solution)/shard_map/ppermute | solution.py:222
  25.3 2.5 %correlate.1 = (f32[2,4,256]{2,1,0:T(4,128)S(1)}, f32[1,2,4,256]{3,2,1,0:T(4,128)S(1)}) custom-call(f32[120,512]{1,0:T(8,128)S(1)} %get-tuple-element.33.args_0_, bf16[120,512]{1,0:T(8,128)(2,1)S(1)} %collective-permute-done.5.args_1_, bf16[14,384,256]{2,1,0:T(8,128)(2,1)S(1)} %get-tuple-element.37.args_2_, ...), custom_call_target="tpu_custom_call" | custom-call | tf_op jit(solution)/shard_map/correlate/pallas_call | solution.py:323
  27.8 0.1 collective-permute-start.6
  27.9 1.2 %collective-permute-done.6 = f32[2,4,256]{2,1,0:T(4,128)S(1)} collective-permute-done((f32[2,4,256]{2,1,0:T(4,128)S(1)}, f32[2,4,256]{2,1,0:T(4,128)S(1)}, u32[]{:S(2)}, u32[]{:S(2)}) %collective-permute-start.6) | collective-permute-done | bytes 8224 | tf_op jit(solution)/shard_map/ppermute | solution.py:222
  29.1 1.1 %collective-permute-start.7 = (f32[4,256]{1,0:T(4,128)S(1)}, f32[4,256]{1,0:T(4,128)S(1)}, u32[]{:S(2)}, u32[]{:S(2)}) collective-permute-start(f32[4,256]{1,0:T(4,128)S(1)} %slice_bitcast_fusion.1), channel_id=1, source_target_pairs={{0,3},{1,2},{2,1},{3,0},{4,7},{5,6},{6,5},{7,4},{8,11},{9,10},{10,... | collective-permute-start | bytes 12296 | tf_op jit(solution)/shard_map/ppermute | solution.py:222
  30.2 1.9 %collective-permute-done.7 = f32[4,256]{1,0:T(4,128)S(1)} collective-permute-done((f32[4,256]{1,0:T(4,128)S(1)}, f32[4,256]{1,0:T(4,128)S(1)}, u32[]{:S(2)}, u32[]{:S(2)}) %collective-permute-start.7) | collective-permute-done | bytes 4128 | tf_op jit(solution)/shard_map/ppermute | solution.py:222
  32.1 0.6 %pad_maximum_fusion.1 = f32[8,256]{1,0:T(8,128)} fusion(f32[4,256]{1,0:T(4,128)S(1)} %get-tuple-element.46, f32[4,256]{1,0:T(4,128)S(1)} %get-tuple-element.45), kind=kLoop, calls=%fused_computation.1 | loop fusion | flops 2048 | bytes 16384 | tf_op jit(solution)/shard_map/concatenate | solution.py:352
  (4 shorter events, 0.0 us)
Async XLA Ops:
  0.0 0.9 %copy-start.2 = (bf16[32,3,512]{2,0,1:T(8,128)(2,1)S(1)}, bf16[32,3,512]{2,0,1:T(8,128)(2,1)}, u32[]{:S(2)}) copy-start(bf16[32,3,512]{2,0,1:T(8,128)(2,1)} %param.7) | copy-start | bytes 294916
  0.9 0.7 %copy-start.7 = (s32[32]{0:T(128)S(1)}, s32[32]{0:T(128)}, u32[]{:S(2)}) copy-start(s32[32]{0:T(128)} %owner_slots.1) | copy-start | bytes 388
  2.2 15.7 %collective-permute-start = (bf16[56,512]{1,0:T(8,128)(2,1)S(1)}, bf16[56,512]{1,0:T(8,128)(2,1)S(1)}, u32[]{:S(2)}, u32[]{:S(2)}) collective-permute-start(bf16[56,512]{1,0:T(8,128)(2,1)S(1)} %pack.1), channel_id=1, source_target_pairs={{0,4},{4,0},{8,12},{12,8},{1,5},{5,1},{9,13},{13,9},{2,6},{6,2},{1... | collective-permute-start | bytes 172040 | tf_op jit(solution)/shard_map/ppermute | solution.py:222
  5.3 12.7 %collective-permute-start.1 = (bf16[56,512]{1,0:T(8,128)(2,1)S(1)}, bf16[56,512]{1,0:T(8,128)(2,1)S(1)}, u32[]{:S(2)}, u32[]{:S(2)}) collective-permute-start(bf16[56,512]{1,0:T(8,128)(2,1)S(1)} %pack.1), channel_id=1, source_target_pairs={{0,8},{4,12},{8,0},{12,4},{1,9},{5,13},{9,1},{13,5},{2,10},{6,14},... | collective-permute-start | bytes 172040 | tf_op jit(solution)/shard_map/ppermute | solution.py:222
  7.8 10.1 %collective-permute-start.2 = (bf16[56,512]{1,0:T(8,128)(2,1)S(1)}, bf16[56,512]{1,0:T(8,128)(2,1)S(1)}, u32[]{:S(2)}, u32[]{:S(2)}) collective-permute-start(bf16[56,512]{1,0:T(8,128)(2,1)S(1)} %pack.1), channel_id=1, source_target_pairs={{0,12},{4,8},{8,4},{12,0},{1,13},{5,9},{9,5},{13,1},{2,14},{6,10},... | collective-permute-start | bytes 172040 | tf_op jit(solution)/shard_map/ppermute | solution.py:222
  7.8 5.9 %collective-permute-start.3 = (s32[4,10]{1,0:T(4,128)}, s32[4,10]{1,0:T(4,128)S(1)}, u32[]{:S(2)}, u32[]{:S(2)}) collective-permute-start(s32[4,10]{1,0:T(4,128)} %args_1_.4), channel_id=1, source_target_pairs={{0,2},{2,0},{1,3},{3,1},{4,6},{6,4},{5,7},{7,5},{8,10},{10,8},{9,1... | collective-permute-start | bytes 488 | tf_op jit(solution)/shard_map/ppermute | solution.py:222
  9.6 0.9 %copy-start = (bf16[4,10,3,300]{3,0,2,1:T(4,128)(2,1)S(1)}, bf16[4,10,3,300]{3,0,2,1:T(4,128)(2,1)}, u32[]{:S(2)}) copy-start(bf16[4,10,3,300]{3,0,2,1:T(4,128)(2,1)} %param.11) | copy-start | bytes 216004
  13.8 0.7 %copy-start.3 = (s32[4,10]{1,0:T(4,128)S(1)}, s32[4,10]{1,0:T(4,128)}, u32[]{:S(2)}) copy-start(s32[4,10]{1,0:T(4,128)} %args_1_.4) | copy-start | bytes 484
  14.5 0.7 %copy-start.4 = (s32[4,10]{1,0:T(4,128)S(1)}, s32[4,10]{1,0:T(4,128)}, u32[]{:S(2)}) copy-start(s32[4,10]{1,0:T(4,128)} %args_2_.4) | copy-start | bytes 484
  15.1 0.7 %copy-start.5 = (s32[128,4]{0,1:T(4,128)S(1)}, s32[128,4]{0,1:T(4,128)}, u32[]{:S(2)}) copy-start(s32[128,4]{0,1:T(4,128)} %param.9) | copy-start | bytes 6148
  15.8 0.7 %copy-start.6 = (s32[128,4]{0,1:T(4,128)S(1)}, s32[128,4]{0,1:T(4,128)}, u32[]{:S(2)}) copy-start(s32[128,4]{0,1:T(4,128)} %param.10) | copy-start | bytes 6148
  18.0 1.6 %collective-permute-start.4 = (bf16[4,56,512]{2,1,0:T(8,128)(2,1)S(1)}, bf16[4,56,512]{2,1,0:T(8,128)(2,1)S(1)}, u32[]{:S(2)}, u32[]{:S(2)}) collective-permute-start(bf16[4,56,512]{2,1,0:T(8,128)(2,1)S(1)} %pad_maximum_fusion.args_0_), channel_id=1, source_target_pairs={{0,1},{1,0},{2,3},{3,2},{4,5},{5,4},{6,7},{7,6},{8,9},{9,8},{10,11... | collective-permute-start | bytes 688136 | tf_op jit(solution)/shard_map/ppermute | solution.py:222
  19.9 5.4 %collective-permute-start.5 = (bf16[120,512]{1,0:T(8,128)(2,1)S(1)}, bf16[120,512]{1,0:T(8,128)(2,1)S(1)}, u32[]{:S(2)}, u32[]{:S(2)}) collective-permute-start(bf16[120,512]{1,0:T(8,128)(2,1)S(1)} %get-tuple-element.34), channel_id=1, source_target_pairs={{0,2},{2,0},{1,3},{3,1},{4,6},{6,4},{5,7},{7,5},{8,10},{10,8},{9,1... | collective-permute-start | bytes 368648 | tf_op jit(solution)/shard_map/ppermute | solution.py:222
  20.3 0.9 %copy-start.1 = (bf16[4,10,3,300]{3,0,2,1:T(4,128)(2,1)S(1)}, bf16[4,10,3,300]{3,0,2,1:T(4,128)(2,1)}, u32[]{:S(2)}) copy-start(bf16[4,10,3,300]{3,0,2,1:T(4,128)(2,1)} %param.11) | copy-start | bytes 216004
  27.8 1.2 %collective-permute-start.6 = (f32[2,4,256]{2,1,0:T(4,128)S(1)}, f32[2,4,256]{2,1,0:T(4,128)S(1)}, u32[]{:S(2)}, u32[]{:S(2)}) collective-permute-start(f32[2,4,256]{2,1,0:T(4,128)S(1)} %bitcast.23), channel_id=1, source_target_pairs={{0,1},{1,0},{2,3},{3,2},{4,5},{5,4},{6,7},{7,6},{8,9},{9,8},{10,11... | collective-permute-start | bytes 24584 | tf_op jit(solution)/shard_map/ppermute | solution.py:222
  29.1 3.0 %collective-permute-start.7 = (f32[4,256]{1,0:T(4,128)S(1)}, f32[4,256]{1,0:T(4,128)S(1)}, u32[]{:S(2)}, u32[]{:S(2)}) collective-permute-start(f32[4,256]{1,0:T(4,128)S(1)} %slice_bitcast_fusion.1), channel_id=1, source_target_pairs={{0,3},{1,2},{2,1},{3,0},{4,7},{5,6},{6,5},{7,4},{8,11},{9,10},{10,... | collective-permute-start | bytes 12296 | tf_op jit(solution)/shard_map/ppermute | solution.py:222

commit v6 on v5

--- a/solution.py
+++ b/solution.py
@@ -36,30 +36,27 @@
         copy.wait()
 
 
-def tables_kernel(taps, nfar, *args):
-    fars, args = args[:nfar], args[nfar:]
-    sids_in, offs_in, start_in, len_in, sid_col, off_col, mask, band = args[:8]
-    sids, offs, gap_start, gap_len, sems = args[8:]
-    pairs = ((sids_in, sids), (offs_in, offs), (start_in, gap_start), (len_in, gap_len))
+def tables_kernel(sids_in, offs_in, start_in, len_in, waves_in, sid_col, off_col, mask, band, scale, waves, *scratch):
+    sids, offs, gap_start, gap_len, sems = scratch
+    pairs = ((waves_in, waves), (sids_in, sids), (offs_in, offs), (start_in, gap_start), (len_in, gap_len))
     copies = [pltpu.make_async_copy(source, place, sems.at[i]) for i, (source, place) in enumerate(pairs)]
     for copy in copies:
         copy.start()
+    js, comps, count, taps = waves.shape
+    refs = count * js
     rows = lax.rem(lax.broadcasted_iota(jnp.int32, band.shape, 0), LANES)
     cols = lax.broadcasted_iota(jnp.int32, band.shape, 1)
     lead = rows + (cols // LANES) * LANES - lax.rem(cols, LANES)
     band[...] = jnp.where((lead >= 0) & (lead < taps), 1.0, 0.0).astype(jnp.bfloat16)
     for copy in copies:
         copy.wait()
-    count, js = sids.shape
-    refs = count * js
-    nstation = gap_start.shape[1]
     for k in range(count):
         for j in range(js):
             row = j * count + k
             off_col[row, :] = jnp.full((LANES,), offs[k, j], jnp.int32)
-            for d, source in enumerate((sids,) + tuple(fars)):
-                sid_col[d, row, :] = jnp.full((LANES,), source[k, j], jnp.int32)
-    own = lax.broadcasted_iota(jnp.int32, (refs, nstation), 1) == sid_col[0, :, :nstation]
+            sid_col[row, :] = jnp.full((LANES,), sids[k, j], jnp.int32)
+    nstation = gap_start.shape[1]
+    own = lax.broadcasted_iota(jnp.int32, (refs, nstation), 1) == sid_col[:, :nstation]
     starts = gap_start[...].astype(jnp.float32)
     ends = starts + gap_len[...].astype(jnp.float32)
     live = jnp.ones(mask.shape, jnp.float32)
@@ -69,31 +66,37 @@
         last = jnp.sum(jnp.where(own, ends[g : g + 1], 0.0), axis=1, keepdims=True)
         live = jnp.where((times >= first) & (times < last), 0.0, live)
     mask[...] = live
-
-
-def filters_kernel(begin, templates, filters, scale):
-    js, comps, count, taps = templates.shape
+    for c in range(comps):
+        for j in range(js):
+            wave = waves[j, c].astype(jnp.float32)
+            power = jnp.sum(wave * wave, axis=1, keepdims=True) / taps
+            factor = 1.0 / (taps * jnp.sqrt(power + 1e-06))
+            first = (c * js + j) * count
+            scale[first : first + count, :] = jnp.broadcast_to(factor, (count, LANES))
+
+
+def filters_kernel(begin, waves, filters):
+    js, _, count, taps = waves.shape
     groups, depth, _ = filters.shape
 
     def one_group(i, carry):
         g = begin + i
-        wave = templates[lax.rem(g, js), g // js].astype(jnp.float32)
+        wave = waves[lax.rem(g, js), g // js].astype(jnp.float32)
         wave = jnp.concatenate([wave, jnp.zeros((count, depth - taps), jnp.float32)], axis=1)
-        power = jnp.sum(wave * wave, axis=1, keepdims=True) / taps
-        factor = 1.0 / (taps * jnp.sqrt(power + 1e-06))
         rows = []
         for k in range(count):
-            scale[pl.ds(i * count + k, 1), :] = jnp.broadcast_to(factor[k : k + 1], (1, LANES))
             row = jnp.broadcast_to(wave[k : k + 1], (SPAN, depth))
             rows.append(pltpu.roll(row, 0, 1, stride=1, stride_axis=0))
         filters[i] = jnp.concatenate(rows, axis=0).T.astype(jnp.bfloat16)
         return carry
 
-    lax.fori_loop(0, groups, one_group, 0)
+    lax.fori_loop(0, groups, one_group, 0, unroll=5)
 
 
 def select_kernel(comps, rows_slab, nsub, *args):
-    heads, (sid_col, mask, near), fars = args[:nsub], args[nsub : nsub + 3], args[nsub + 3 :]
+    heads, args = args[:nsub], args[nsub:]
+    nslab = len(args) // 2
+    sid_cols, mask, outs = args[:nslab], args[nslab], args[nslab + 1 :]
     refs = mask.shape[0]
     ntmpl, _, width = heads[0].shape
     here = lax.axis_index("slab")
@@ -112,8 +115,8 @@
     row = lax.rem(row, rows_slab) // (rows_slab // comps)
     stack = jnp.concatenate([part[z, :rows_slab, :] for part in heads for z in range(ntmpl)], axis=0)
     owners = [jnp.where(row == c, owner, -1.0) for c in range(comps)]
-    for d, out in enumerate((near,) + tuple(fars)):
-        wanted = sid_col[d, :, :1].astype(jnp.float32)
+    for d, out in enumerate(outs):
+        wanted = sid_cols[d][:, :1].astype(jnp.float32)
         pick = [jnp.where(owners[c] == wanted, 1.0, 0.0).astype(jnp.bfloat16) for c in range(comps)]
         got = jnp.dot(jnp.concatenate(pick, axis=0), stack, preferred_element_type=jnp.float32)
         if d:
@@ -126,8 +129,8 @@
 
 def correlate_kernel(nslab, nsub, taps, nbank, *args):
     near, fars, args = args[0], args[1:nslab], args[nslab:]
-    banks, scales, args = args[:nbank], args[nbank : 2 * nbank], args[2 * nbank :]
-    off_col, mask, band, keep, send, segs, low, high, norm, total = args
+    banks, args = args[:nbank], args[nbank:]
+    off_col, mask, band, scale, keep, send, segs, low, high, norm, total = args
     refs, time = mask.shape
     chans, width = near.shape
     comps = chans // refs
@@ -169,7 +172,6 @@
             low[pl.ds(i * 8, 8), r, :] = zero
             high[pl.ds(i * 8, 8), r, :] = zero
     reach = band.shape[1] // LANES
-    scale = jnp.concatenate([part[...] for part in scales], axis=0)
     sums = {}
     for r in reversed(range(chunks)):
         part = segs[:, r * LANES : (r + 1) * LANES]
@@ -180,7 +182,7 @@
         window = sums[r][:, :LANES]
         for p in range(1, min(reach, chunks - r)):
             window = window + sums[r + p][:, p * LANES : (p + 1) * LANES]
-        factor = scale * lax.rsqrt(window / taps + 1e-06)
+        factor = scale[...] * lax.rsqrt(window / taps + 1e-06)
         for i in range(chans // 8):
             norm[pl.ds(i * 8, 8), r, :] = factor[i * 8 : i * 8 + 8]
     span = banks[0].shape[1] // LANES
@@ -222,6 +224,10 @@
     return lax.ppermute(value, axis, [(i, i ^ distance) for i in range(lax.axis_size(axis))])
 
 
+def stays(value):
+    return pltpu.with_memory_space_constraint(value, pltpu.HBM)
+
+
 def params(mib):
     return pltpu.CompilerParams(vmem_limit_bytes=mib << 20)
 
@@ -248,7 +254,7 @@
             scratch_shapes=[pltpu.SMEM((nloc,), jnp.int32), pltpu.SemaphoreType.DMA((comps + 1,))],
             compiler_params=params(4),
             name="pack",
-        )(owner_slots, records.transpose(1, 0, 2))
+        )(stays(owner_slots), stays(records.transpose(1, 0, 2)))
     else:
         mine = lax.dynamic_slice_in_dim(records.transpose(1, 0, 2), half * core, half, 1)
         mine = jnp.pad(mine, ((0, 0), (0, high - half), (0, 0))).reshape(rows_slab, width)
@@ -261,61 +267,60 @@
         column = [block] + [swapped(block, "tmpl", d) for d in range(1, ntmpl)]
     else:
         column = list(lax.all_gather(block, "tmpl", axis=0))
-    asked = [swapped(station_ids, "slab", d) for d in range(1, nslab)]
+    waves = templates.transpose(1, 2, 0, 3)
     reach = round_up(taps + LANES - 1, LANES)
-    sid_col, off_col, mask, band = pl.pallas_call(
-        functools.partial(tables_kernel, taps, nslab - 1),
+    sid_col, off_col, mask, band, scale, waves = pl.pallas_call(
+        tables_kernel,
         out_shape=[
-            jax.ShapeDtypeStruct((nslab, refs, LANES), jnp.int32),
+            jax.ShapeDtypeStruct((refs, LANES), jnp.int32),
             jax.ShapeDtypeStruct((refs, LANES), jnp.int32),
             jax.ShapeDtypeStruct((refs, time), jnp.float32),
             jax.ShapeDtypeStruct((2 * LANES, reach), jnp.bfloat16),
+            jax.ShapeDtypeStruct((chans, LANES), jnp.float32),
+            jax.ShapeDtypeStruct(waves.shape, waves.dtype),
         ],
-        in_specs=[smem] * (nslab - 1) + [hbm] * 4,
-        out_specs=[vmem] * 4,
+        in_specs=[hbm] * 5,
+        out_specs=[vmem] * 6,
         scratch_shapes=[
             pltpu.SMEM(station_ids.shape, jnp.int32),
             pltpu.SMEM(offsets.shape, jnp.int32),
             pltpu.VMEM(gap_start.T.shape, jnp.int32),
             pltpu.VMEM(gap_len.T.shape, jnp.int32),
-            pltpu.SemaphoreType.DMA((4,)),
+            pltpu.SemaphoreType.DMA((5,)),
         ],
         compiler_params=params(8),
         name="tables",
-    )(*asked, station_ids, offsets, gap_start.T, gap_len.T)
+    )(*[stays(value) for value in (station_ids, offsets, gap_start.T, gap_len.T, waves)])
+    sid_cols = [sid_col] + [swapped(sid_col, "slab", d) for d in range(1, nslab)]
     depth = round_up(taps + SPAN - 1, LANES)
-    waves = templates.transpose(1, 2, 0, 3)
-
-    def bank(begin, groups, source):
+
+    def bank(begin, groups):
         return pl.pallas_call(
             functools.partial(filters_kernel, begin),
-            out_shape=[
-                jax.ShapeDtypeStruct((groups, depth, count * SPAN), jnp.bfloat16),
-                jax.ShapeDtypeStruct((groups * count, LANES), jnp.float32),
-            ],
+            out_shape=jax.ShapeDtypeStruct((groups, depth, count * SPAN), jnp.bfloat16),
             in_specs=[vmem],
-            out_specs=[vmem] * 2,
+            out_specs=vmem,
             compiler_params=params(16),
             name="filters",
-        )(source)
+        )(waves)
 
     groups = comps * js
-    early = groups // 2 // 2 * 2
-    bank_a, scale_a = bank(0, early, waves)
-    column, bank_a, mask = lax.optimization_barrier((column, bank_a, mask))
+    early = groups // 3
+    bank_a = bank(0, early)
+    column, sid_cols, bank_a = lax.optimization_barrier((column, sid_cols, bank_a))
     head = jnp.stack(column)
     heads = [head] + [swapped(head, "sub", m) for m in range(1, nsub)]
     near, *fars = pl.pallas_call(
         functools.partial(select_kernel, comps, rows_slab, nsub),
         out_shape=[jax.ShapeDtypeStruct((chans, width), jnp.float32)]
         + [jax.ShapeDtypeStruct((chans, width), records.dtype)] * (nslab - 1),
-        in_specs=[vmem] * (nsub + 2),
+        in_specs=[vmem] * (nsub + nslab + 1),
         out_specs=[vmem] * nslab,
         compiler_params=params(16),
         name="select",
-    )(*heads, sid_col, mask)
+    )(*heads, *sid_cols, mask)
     fars = [swapped(far, "slab", d + 1) for d, far in enumerate(fars)]
-    bank_b, scale_b = bank(early, groups - early, waves)
+    bank_b = bank(early, groups - early)
     fars, bank_b = lax.optimization_barrier((fars, bank_b))
     chunks = time // LANES
     each = width // nsub
@@ -326,7 +331,7 @@
             jax.ShapeDtypeStruct((nslab, count, each), jnp.float32),
             jax.ShapeDtypeStruct((nsub - 1, nslab, count, each), jnp.float32),
         ],
-        in_specs=[vmem] * (nslab + 7),
+        in_specs=[vmem] * (nslab + 6),
         out_specs=[vmem] * 2,
         scratch_shapes=[
             pltpu.VMEM((chans, time), jnp.float32),
@@ -337,7 +342,7 @@
         ],
         compiler_params=params(32),
         name="correlate",
-    )(near, *fars, bank_a, bank_b, scale_a, scale_b, off_col, mask, band)
+    )(near, *fars, bank_a, bank_b, off_col, mask, band, scale)
     for m in range(1, nsub):
         keep = keep + swapped(send[m - 1], "sub", m)
     lines = [keep[0]]

time: 33 us -> 27.4 us (0.83)
  local copies, waits for them, and re-layouts: 6.05 us -> 0.01 us
  Pallas kernels: 12 us -> 8.53 us
  waiting for transfers between devices: 4.9 us -> 7.53 us
  starting transfers between devices: 9.06 us -> 10.4 us
    unnamed x16 -> x0, local copies, waits for them, and re-layouts: 6.05 us -> none
    pallas_call x3, Pallas kernels: 8.49 us -> 4.93 us  [the longest x2 3.74 us: bank(): pl.pallas_call(functools.partial(filters_kernel, begin), out_shape=jax.Sh...]
    ppermute x8, waiting for transfers between devices: 4.9 us -> 7.53 us  [swapped(): lax.ppermute(value, axis, [(i, i ^ distance) for i in range(lax.axis_size...]
    ppermute x8, starting transfers between devices: 9.06 us -> 10.4 us  [swapped(): lax.ppermute(value, axis, [(i, i ^ distance) for i in range(lax.axis_size...]
  transfers between devices with their start and end apart: 8 -> 8, of which waited for: 4 -> 6; matrix products, arithmetic and copies ran while one was open for 0% -> 0% of each run, Pallas kernels for 26% -> 18%
where the time goes in v6:
time: 27.4 us; the launch traced here: 27.2 us
  starting transfers between devices  10.4 us (38%)
  Pallas kernels  8.53 us (31%)
  waiting for transfers between devices  7.53 us (27%)
  other arithmetic  0.65 us (2%)
    ppermute x8, starting transfers between devices, swapped(): lax.ppermute(value, axis, [(i, i ^ distance) for i in range(lax.axis_size...  10.4 us
    ppermute x8, waiting for transfers between devices, swapped(): lax.ppermute(value, axis, [(i, i ^ distance) for i in range(lax.axis_size...  7.53 us
    pallas_call x2, Pallas kernels, bank(): pl.pallas_call(functools.partial(filters_kernel, begin), out_shape=jax.Sh...  3.74 us
    pallas_call x1, Pallas kernels, on_device(): pl.pallas_call(functools.partial(correlate_kernel, nslab, nsub, taps, 2),...  2.48 us
    pallas_call x1, Pallas kernels, on_device(): pl.pallas_call(tables_kernel, out_shape=[jax.ShapeDtypeStruct((refs, LANE...  1.19 us
    pallas_call x1, Pallas kernels, on_device(): pl.pallas_call(pack_kernel, out_shape=jax.ShapeDtypeStruct((rows_slab + E...  0.79 us
    concatenate x1, other arithmetic, on_device(): return jnp.concatenate(result, axis=0)  0.61 us
  transfers between devices with their start and end apart: 8, of which 6 were waited for; matrix products, arithmetic and copies ran while one was open for 0% of the time, Pallas kernels for 18%

profile of v6, /device:TPU:0, one launch (start us, length us, event | category | flops | bytes accessed | tf_op | source)
XLA Modules:
  0.0 27.2 jit_solution(3210723742103429091)
XLA Ops:
  0.0 0.8 %pack.1 = bf16[56,512]{1,0:T(8,128)(2,1)S(1)} custom-call(s32[32]{0:T(128)} %owner_slots.1, bf16[3,32,512]{2,1,0:T(8,128)(2,1)} %bitcast.19), custom_call_target="tpu_custom_call" | custom-call | tf_op jit(solution)/shard_map/pack/pallas_call | solution.py:249
  0.8 3.1 %collective-permute-start = (bf16[56,512]{1,0:T(8,128)(2,1)S(1)}, bf16[56,512]{1,0:T(8,128)(2,1)S(1)}, u32[]{:S(2)}, u32[]{:S(2)}) collective-permute-start(bf16[56,512]{1,0:T(8,128)(2,1)S(1)} %pack.1), channel_id=1, source_target_pairs={{0,4},{4,0},{8,12},{12,8},{1,5},{5,1},{9,13},{13,9},{2,6},{6,2},{1... | collective-permute-start | bytes 172040 | tf_op jit(solution)/shard_map/ppermute | solution.py:224
  3.9 2.6 %collective-permute-start.1 = (bf16[56,512]{1,0:T(8,128)(2,1)S(1)}, bf16[56,512]{1,0:T(8,128)(2,1)S(1)}, u32[]{:S(2)}, u32[]{:S(2)}) collective-permute-start(bf16[56,512]{1,0:T(8,128)(2,1)S(1)} %pack.1), channel_id=1, source_target_pairs={{0,8},{4,12},{8,0},{12,4},{1,9},{5,13},{9,1},{13,5},{2,10},{6,14},... | collective-permute-start | bytes 172040 | tf_op jit(solution)/shard_map/ppermute | solution.py:224
  6.5 0.0 collective-permute-start.2
  6.5 1.2 %tables.1 = (s32[40,128]{1,0:T(8,128)S(1)}, s32[40,128]{1,0:T(8,128)S(1)}, f32[40,1024]{1,0:T(8,128)S(1)}, bf16[256,512]{1,0:T(8,128)(2,1)S(1)}, f32[120,128]{1,...) custom-call(s32[4,10]{1,0:T(4,128)} %sids_in.1, s32[4,10]{1,0:T(4,128)} %offs_in.1, s32[4,128]{1,0:T(4,128)} %bitcast.24, ...), custom_call_target="tpu_custom_call" | custom-call | tf_op jit(solution)/shard_map/tables/pallas_call | solution.py:272
  7.7 1.8 %collective-permute-start.3 = (s32[40,128]{1,0:T(8,128)S(1)}, s32[40,128]{1,0:T(8,128)S(1)}, u32[]{:S(2)}, u32[]{:S(2)}) collective-permute-start(s32[40,128]{1,0:T(8,128)S(1)} %get-tuple-element.30.args_2_), channel_id=1, source_target_pairs={{0,2},{2,0},{1,3},{3,1},{4,6},{6,4},{5,7},{7,5},{8,10},{10,8},{9,1... | collective-permute-start | bytes 61448 | tf_op jit(solution)/shard_map/ppermute | solution.py:224
  9.5 1.2 %filters.2.args_2_ = bf16[10,384,256]{2,1,0:T(8,128)(2,1)S(1)} custom-call(bf16[10,3,4,300]{3,2,1,0:T(4,128)(2,1)S(1)} %get-tuple-element.25.waves), custom_call_target="tpu_custom_call" | custom-call | tf_op jit(solution)/shard_map/filters/pallas_call | solution.py:298
  10.7 0.8 %collective-permute-done.3.args_3_ = s32[40,128]{1,0:T(8,128)S(1)} collective-permute-done((s32[40,128]{1,0:T(8,128)S(1)}, s32[40,128]{1,0:T(8,128)S(1)}, u32[]{:S(2)}, u32[]{:S(2)}) %collective-permute-start.3) | collective-permute-done | bytes 20512 | tf_op jit(solution)/shard_map/ppermute | solution.py:224
  11.5 0.0 collective-permute-done
  11.5 0.0 collective-permute-done.1
  11.5 0.9 %collective-permute-done.2 = bf16[56,512]{1,0:T(8,128)(2,1)S(1)} collective-permute-done((bf16[56,512]{1,0:T(8,128)(2,1)S(1)}, bf16[56,512]{1,0:T(8,128)(2,1)S(1)}, u32[]{:S(2)}, u32[]{:S(2)}) %collective-permute-start.2) | collective-permute-done | bytes 57376 | tf_op jit(solution)/shard_map/ppermute | solution.py:224
  12.5 0.1 collective-permute-start.4
  12.6 1.5 %collective-permute-done.4.args_1_ = bf16[4,56,512]{2,1,0:T(8,128)(2,1)S(1)} collective-permute-done((bf16[4,56,512]{2,1,0:T(8,128)(2,1)S(1)}, bf16[4,56,512]{2,1,0:T(8,128)(2,1)S(1)}, u32[]{:S(2)}, u32[]{:S(2)}) %collective-permute-start.4) | collective-permute-done | bytes 229408 | tf_op jit(solution)/shard_map/ppermute | solution.py:224
  14.0 0.3 %select.1 = (f32[120,512]{1,0:T(8,128)S(1)}, bf16[120,512]{1,0:T(8,128)(2,1)S(1)}) custom-call(bf16[4,56,512]{2,1,0:T(8,128)(2,1)S(1)} %pad_maximum_fusion.args_0_, bf16[4,56,512]{2,1,0:T(8,128)(2,1)S(1)} %collective-permute-done.4.args_1_, s32[40,128]{1,0:T(8,128)S(1)} %get-tuple-element.30.args_2_, s32[40,128]{1,0:T(8,128)S(1)} %collective-permute-done.3.args_3_, ...), custom_call_target="tpu_custom_call" | custom-call | tf_op jit(solution)/shard_map/select/pallas_call | solution.py:313
  14.4 1.6 %collective-permute-start.5 = (bf16[120,512]{1,0:T(8,128)(2,1)S(1)}, bf16[120,512]{1,0:T(8,128)(2,1)S(1)}, u32[]{:S(2)}, u32[]{:S(2)}) collective-permute-start(bf16[120,512]{1,0:T(8,128)(2,1)S(1)} %get-tuple-element.34), channel_id=1, source_target_pairs={{0,2},{2,0},{1,3},{3,1},{4,6},{6,4},{5,7},{7,5},{8,10},{10,8},{9,1... | collective-permute-start | bytes 368648 | tf_op jit(solution)/shard_map/ppermute | solution.py:224
  15.9 2.5 %filters.3.args_3_ = bf16[20,384,256]{2,1,0:T(8,128)(2,1)S(1)} custom-call(bf16[10,3,4,300]{3,2,1,0:T(4,128)(2,1)S(1)} %get-tuple-element.25.waves), custom_call_target="tpu_custom_call" | custom-call | tf_op jit(solution)/shard_map/filters/pallas_call | solution.py:298
  18.4 1.4 %collective-permute-done.5.args_1_ = bf16[120,512]{1,0:T(8,128)(2,1)S(1)} collective-permute-done((bf16[120,512]{1,0:T(8,128)(2,1)S(1)}, bf16[120,512]{1,0:T(8,128)(2,1)S(1)}, u32[]{:S(2)}, u32[]{:S(2)}) %collective-permute-start.5) | collective-permute-done | bytes 122912 | tf_op jit(solution)/shard_map/ppermute | solution.py:224
  19.8 2.5 %correlate.1 = (f32[2,4,256]{2,1,0:T(4,128)S(1)}, f32[1,2,4,256]{3,2,1,0:T(4,128)S(1)}) custom-call(f32[120,512]{1,0:T(8,128)S(1)} %get-tuple-element.33.args_0_, bf16[120,512]{1,0:T(8,128)(2,1)S(1)} %collective-permute-done.5.args_1_, bf16[10,384,256]{2,1,0:T(8,128)(2,1)S(1)} %filters.2.args_2_, bf16[20,384,256]{2,1,0:T(8,128)(2,1)S(1)} %filters.3.args_3_, ...), custom_call_target="tpu_custom_call" | custom-call | tf_op jit(solution)/shard_map/correlate/pallas_call | solution.py:328
  22.3 0.1 collective-permute-start.6
  22.4 1.2 %collective-permute-done.6 = f32[2,4,256]{2,1,0:T(4,128)S(1)} collective-permute-done((f32[2,4,256]{2,1,0:T(4,128)S(1)}, f32[2,4,256]{2,1,0:T(4,128)S(1)}, u32[]{:S(2)}, u32[]{:S(2)}) %collective-permute-start.6) | collective-permute-done | bytes 8224 | tf_op jit(solution)/shard_map/ppermute | solution.py:224
  23.6 1.3 %collective-permute-start.7 = (f32[4,256]{1,0:T(4,128)S(1)}, f32[4,256]{1,0:T(4,128)S(1)}, u32[]{:S(2)}, u32[]{:S(2)}) collective-permute-start(f32[4,256]{1,0:T(4,128)S(1)} %slice_bitcast_fusion.1), channel_id=1, source_target_pairs={{0,3},{1,2},{2,1},{3,0},{4,7},{5,6},{6,5},{7,4},{8,11},{9,10},{10,... | collective-permute-start | bytes 12296 | tf_op jit(solution)/shard_map/ppermute | solution.py:224
  24.8 1.8 %collective-permute-done.7 = f32[4,256]{1,0:T(4,128)S(1)} collective-permute-done((f32[4,256]{1,0:T(4,128)S(1)}, f32[4,256]{1,0:T(4,128)S(1)}, u32[]{:S(2)}, u32[]{:S(2)}) %collective-permute-start.7) | collective-permute-done | bytes 4128 | tf_op jit(solution)/shard_map/ppermute | solution.py:224
  26.6 0.6 %pad_maximum_fusion.1 = f32[8,256]{1,0:T(8,128)} fusion(f32[4,256]{1,0:T(4,128)S(1)} %get-tuple-element.44, f32[4,256]{1,0:T(4,128)S(1)} %get-tuple-element.43), kind=kLoop, calls=%fused_computation.1 | loop fusion | flops 2048 | bytes 16384 | tf_op jit(solution)/shard_map/concatenate | solution.py:357
  (4 shorter events, 0.0 us)
Async XLA Ops:
  0.8 10.7 %collective-permute-start = (bf16[56,512]{1,0:T(8,128)(2,1)S(1)}, bf16[56,512]{1,0:T(8,128)(2,1)S(1)}, u32[]{:S(2)}, u32[]{:S(2)}) collective-permute-start(bf16[56,512]{1,0:T(8,128)(2,1)S(1)} %pack.1), channel_id=1, source_target_pairs={{0,4},{4,0},{8,12},{12,8},{1,5},{5,1},{9,13},{13,9},{2,6},{6,2},{1... | collective-permute-start | bytes 172040 | tf_op jit(solution)/shard_map/ppermute | solution.py:224
  3.9 7.6 %collective-permute-start.1 = (bf16[56,512]{1,0:T(8,128)(2,1)S(1)}, bf16[56,512]{1,0:T(8,128)(2,1)S(1)}, u32[]{:S(2)}, u32[]{:S(2)}) collective-permute-start(bf16[56,512]{1,0:T(8,128)(2,1)S(1)} %pack.1), channel_id=1, source_target_pairs={{0,8},{4,12},{8,0},{12,4},{1,9},{5,13},{9,1},{13,5},{2,10},{6,14},... | collective-permute-start | bytes 172040 | tf_op jit(solution)/shard_map/ppermute | solution.py:224
  6.5 6.0 %collective-permute-start.2 = (bf16[56,512]{1,0:T(8,128)(2,1)S(1)}, bf16[56,512]{1,0:T(8,128)(2,1)S(1)}, u32[]{:S(2)}, u32[]{:S(2)}) collective-permute-start(bf16[56,512]{1,0:T(8,128)(2,1)S(1)} %pack.1), channel_id=1, source_target_pairs={{0,12},{4,8},{8,4},{12,0},{1,13},{5,9},{9,5},{13,1},{2,14},{6,10},... | collective-permute-start | bytes 172040 | tf_op jit(solution)/shard_map/ppermute | solution.py:224
  7.7 3.8 %collective-permute-start.3 = (s32[40,128]{1,0:T(8,128)S(1)}, s32[40,128]{1,0:T(8,128)S(1)}, u32[]{:S(2)}, u32[]{:S(2)}) collective-permute-start(s32[40,128]{1,0:T(8,128)S(1)} %get-tuple-element.30.args_2_), channel_id=1, source_target_pairs={{0,2},{2,0},{1,3},{3,1},{4,6},{6,4},{5,7},{7,5},{8,10},{10,8},{9,1... | collective-permute-start | bytes 61448 | tf_op jit(solution)/shard_map/ppermute | solution.py:224
  12.5 1.6 %collective-permute-start.4 = (bf16[4,56,512]{2,1,0:T(8,128)(2,1)S(1)}, bf16[4,56,512]{2,1,0:T(8,128)(2,1)S(1)}, u32[]{:S(2)}, u32[]{:S(2)}) collective-permute-start(bf16[4,56,512]{2,1,0:T(8,128)(2,1)S(1)} %pad_maximum_fusion.args_0_), channel_id=1, source_target_pairs={{0,1},{1,0},{2,3},{3,2},{4,5},{5,4},{6,7},{7,6},{8,9},{9,8},{10,11... | collective-permute-start | bytes 688136 | tf_op jit(solution)/shard_map/ppermute | solution.py:224
  14.4 5.4 %collective-permute-start.5 = (bf16[120,512]{1,0:T(8,128)(2,1)S(1)}, bf16[120,512]{1,0:T(8,128)(2,1)S(1)}, u32[]{:S(2)}, u32[]{:S(2)}) collective-permute-start(bf16[120,512]{1,0:T(8,128)(2,1)S(1)} %get-tuple-element.34), channel_id=1, source_target_pairs={{0,2},{2,0},{1,3},{3,1},{4,6},{6,4},{5,7},{7,5},{8,10},{10,8},{9,1... | collective-permute-start | bytes 368648 | tf_op jit(solution)/shard_map/ppermute | solution.py:224
  22.3 1.2 %collective-permute-start.6 = (f32[2,4,256]{2,1,0:T(4,128)S(1)}, f32[2,4,256]{2,1,0:T(4,128)S(1)}, u32[]{:S(2)}, u32[]{:S(2)}) collective-permute-start(f32[2,4,256]{2,1,0:T(4,128)S(1)} %bitcast.18), channel_id=1, source_target_pairs={{0,1},{1,0},{2,3},{3,2},{4,5},{5,4},{6,7},{7,6},{8,9},{9,8},{10,11... | collective-permute-start | bytes 24584 | tf_op jit(solution)/shard_map/ppermute | solution.py:224
  23.6 3.0 %collective-permute-start.7 = (f32[4,256]{1,0:T(4,128)S(1)}, f32[4,256]{1,0:T(4,128)S(1)}, u32[]{:S(2)}, u32[]{:S(2)}) collective-permute-start(f32[4,256]{1,0:T(4,128)S(1)} %slice_bitcast_fusion.1), channel_id=1, source_target_pairs={{0,3},{1,2},{2,1},{3,0},{4,7},{5,6},{6,5},{7,4},{8,11},{9,10},{10,... | collective-permute-start | bytes 12296 | tf_op jit(solution)/shard_map/ppermute | solution.py:224

commit v7 on v6

--- a/solution.py
+++ b/solution.py
@@ -18,20 +18,21 @@
 
 def pack_kernel(owner_slots, records, block, owners, sems):
     comps, _, width = records.shape
-    half = (block.shape[0] - EXTRA) // comps
+    per = width // LANES
+    half = (block.shape[0] - EXTRA) // (comps * per)
     first = pl.multiple_of(lax.axis_index("sub") * half, half)
-    copies = [pltpu.make_async_copy(owner_slots, owners, sems.at[comps])]
-    for c in range(comps):
-        source, place = records.at[c, pl.ds(first, half), :], block.at[c * half : (c + 1) * half, :]
-        copies.append(pltpu.make_async_copy(source, place, sems.at[c]))
+    copies = [pltpu.make_async_copy(owner_slots, owners, sems.at[comps * per])]
+    for i in range(comps * per):
+        source = records.at[i // per, pl.ds(first, half), (i % per) * LANES : (i % per + 1) * LANES]
+        copies.append(pltpu.make_async_copy(source, block.at[i * half : (i + 1) * half, :], sems.at[i]))
     for copy in copies:
         copy.start()
     copies[0].wait()
-    lane = lax.rem(lax.broadcasted_iota(jnp.int32, (EXTRA, width), 1), half)
-    line = jnp.full((EXTRA, width), -1, jnp.int32)
+    lane = lax.rem(lax.broadcasted_iota(jnp.int32, (EXTRA, LANES), 1), half)
+    line = jnp.full((EXTRA, LANES), -1, jnp.int32)
     for i in range(half):
         line = jnp.where(lane == i, owners[first + i], line)
-    block[comps * half :, :] = line.astype(jnp.float32).astype(block.dtype)
+    block[comps * per * half :, :] = line.astype(jnp.float32).astype(block.dtype)
     for copy in copies[1:]:
         copy.wait()
 
@@ -93,27 +94,40 @@
     lax.fori_loop(0, groups, one_group, 0, unroll=5)
 
 
-def select_kernel(comps, rows_slab, nsub, *args):
+def select_kernel(comps, high, nsub, *args):
     heads, args = args[:nsub], args[nsub:]
     nslab = len(args) // 2
     sid_cols, mask, outs = args[:nslab], args[nslab], args[nslab + 1 :]
     refs = mask.shape[0]
-    ntmpl, _, width = heads[0].shape
+    ntmpl = heads[0].shape[0]
+    width = outs[0].shape[1]
+    per = width // LANES
     here = lax.axis_index("slab")
-    depth = nsub * ntmpl * rows_slab
+    rows_slab = comps * high
+    blocks = [(part, z) for part in heads for z in range(ntmpl)]
+    depth = len(blocks) * rows_slab
     owner = []
-    for q in range(round_up(depth, width) // width):
-        lane = lax.broadcasted_iota(jnp.int32, (1, width), 1) + q * width
-        line = jnp.full((1, width), -1.0, jnp.float32)
-        for b in range(nsub * ntmpl):
-            tail = heads[b // ntmpl][b % ntmpl, rows_slab : rows_slab + EXTRA, :].astype(jnp.float32)
-            inside = (lane >= b * rows_slab) & (lane < (b + 1) * rows_slab)
-            line = jnp.where(inside, tail[q : q + 1], line)
+    for q in range(0, depth, LANES):
+        lane = lax.broadcasted_iota(jnp.int32, (1, LANES), 1) + q
+        line = jnp.full((1, LANES), -1.0, jnp.float32)
+        for b, (part, z) in enumerate(blocks):
+            if b * rows_slab < q + LANES and (b + 1) * rows_slab > q:
+                tail = part[z, rows_slab * per : rows_slab * per + EXTRA, :].astype(jnp.float32)
+                inside = (lane >= b * rows_slab) & (lane < (b + 1) * rows_slab)
+                line = jnp.where(inside, tail[:1], line)
         owner.append(line)
     owner = jnp.concatenate(owner, axis=1)[:, :depth]
     row = lax.broadcasted_iota(jnp.int32, (1, depth), 1)
-    row = lax.rem(row, rows_slab) // (rows_slab // comps)
-    stack = jnp.concatenate([part[z, :rows_slab, :] for part in heads for z in range(ntmpl)], axis=0)
+    row = lax.rem(row, rows_slab) // high
+    columns = []
+    for q in range(per):
+        tiles = []
+        for part, z in blocks:
+            for c in range(comps):
+                first = (c * per + q) * high
+                tiles.append(part[z, first : first + high, :])
+        columns.append(jnp.concatenate(tiles, axis=0))
+    stack = jnp.concatenate(columns, axis=1)
     owners = [jnp.where(row == c, owner, -1.0) for c in range(comps)]
     for d, out in enumerate(outs):
         wanted = sid_cols[d][:, :1].astype(jnp.float32)
@@ -244,27 +258,30 @@
     hbm = pl.BlockSpec(memory_space=pltpu.HBM)
     half = nloc // nsub
     high = round_up(half, 16)
-    rows_slab = comps * high
+    per = width // LANES
     if high == half:
         block = pl.pallas_call(
             pack_kernel,
-            out_shape=jax.ShapeDtypeStruct((rows_slab + EXTRA, width), records.dtype),
+            out_shape=jax.ShapeDtypeStruct((comps * high * per + EXTRA, LANES), records.dtype),
             in_specs=[hbm, hbm],
             out_specs=vmem,
-            scratch_shapes=[pltpu.SMEM((nloc,), jnp.int32), pltpu.SemaphoreType.DMA((comps + 1,))],
+            scratch_shapes=[pltpu.SMEM((nloc,), jnp.int32), pltpu.SemaphoreType.DMA((comps * per + 1,))],
             compiler_params=params(4),
             name="pack",
         )(stays(owner_slots), stays(records.transpose(1, 0, 2)))
     else:
         mine = lax.dynamic_slice_in_dim(records.transpose(1, 0, 2), half * core, half, 1)
-        mine = jnp.pad(mine, ((0, 0), (0, high - half), (0, 0))).reshape(rows_slab, width)
+        mine = jnp.pad(mine, ((0, 0), (0, high - half), (0, 0))).reshape(comps, high, per, LANES)
+        mine = mine.transpose(0, 2, 1, 3).reshape(comps * per * high, LANES)
         own = lax.dynamic_slice_in_dim(owner_slots, half * core, half, 0)
-        index = jnp.arange(EXTRA * width, dtype=jnp.int32).reshape(1, EXTRA, width) % high
+        index = jnp.arange(EXTRA * LANES, dtype=jnp.int32).reshape(1, EXTRA, LANES) % high
         slots = jnp.arange(half, dtype=jnp.int32)[:, None, None]
         own = jnp.sum(jnp.where(index == slots, own[:, None, None] + 1, 0), axis=0) - 1
         block = jnp.concatenate([mine, own.astype(records.dtype)], axis=0)
+    column = [block]
     if ntmpl <= 8:
-        column = [block] + [swapped(block, "tmpl", d) for d in range(1, ntmpl)]
+        for d in range(1, ntmpl):
+            column.append(lax.ppermute(block, "tmpl", [(i, (i + d) % ntmpl) for i in range(ntmpl)]))
     else:
         column = list(lax.all_gather(block, "tmpl", axis=0))
     waves = templates.transpose(1, 2, 0, 3)
@@ -307,11 +324,12 @@
     groups = comps * js
     early = groups // 3
     bank_a = bank(0, early)
-    column, sid_cols, bank_a = lax.optimization_barrier((column, sid_cols, bank_a))
+    column, mask = lax.optimization_barrier((column, mask))
     head = jnp.stack(column)
     heads = [head] + [swapped(head, "sub", m) for m in range(1, nsub)]
+    heads, bank_a = lax.optimization_barrier((heads, bank_a))
     near, *fars = pl.pallas_call(
-        functools.partial(select_kernel, comps, rows_slab, nsub),
+        functools.partial(select_kernel, comps, high, nsub),
         out_shape=[jax.ShapeDtypeStruct((chans, width), jnp.float32)]
         + [jax.ShapeDtypeStruct((chans, width), records.dtype)] * (nslab - 1),
         in_specs=[vmem] * (nsub + nslab + 1),

time: 27.4 us -> 27.6 us (level)
  starting transfers between devices: 10.4 us -> 11.9 us
  waiting for transfers between devices: 7.53 us -> 6.11 us
    ppermute x0 -> x3, starting transfers between devices: none -> 7.01 us  [on_device(): lax.ppermute(block, 'tmpl', [(i, (i + d) % ntmpl) for i in range(ntmpl)])]
    ppermute x8 -> x5, starting transfers between devices: 10.4 us -> 4.89 us  [swapped(): lax.ppermute(value, axis, [(i, i ^ distance) for i in range(lax.axis_size...]
    ppermute x8 -> x5, waiting for transfers between devices: 7.53 us -> 4.48 us  [swapped(): lax.ppermute(value, axis, [(i, i ^ distance) for i in range(lax.axis_size...]
    ppermute x0 -> x3, waiting for transfers between devices: none -> 1.63 us  [on_device(): lax.ppermute(block, 'tmpl', [(i, (i + d) % ntmpl) for i in range(ntmpl)])]
where the time goes in v7:
time: 27.6 us; the launch traced here: 27.5 us
  starting transfers between devices  11.9 us (43%)
  Pallas kernels  8.72 us (32%)
  waiting for transfers between devices  6.11 us (22%)
  other arithmetic  0.65 us (2%)
    ppermute x3, starting transfers between devices, on_device(): lax.ppermute(block, 'tmpl', [(i, (i + d) % ntmpl) for i in range(ntmpl)])  7.01 us
    ppermute x5, starting transfers between devices, swapped(): lax.ppermute(value, axis, [(i, i ^ distance) for i in range(lax.axis_size...  4.89 us
    ppermute x5, waiting for transfers between devices, swapped(): lax.ppermute(value, axis, [(i, i ^ distance) for i in range(lax.axis_size...  4.48 us
    pallas_call x2, Pallas kernels, bank(): pl.pallas_call(functools.partial(filters_kernel, begin), out_shape=jax.Sh...  3.74 us
    pallas_call x1, Pallas kernels, on_device(): pl.pallas_call(functools.partial(correlate_kernel, nslab, nsub, taps, 2),...  2.5 us
    ppermute x3, waiting for transfers between devices, on_device(): lax.ppermute(block, 'tmpl', [(i, (i + d) % ntmpl) for i in range(ntmpl)])  1.63 us
    pallas_call x1, Pallas kernels, on_device(): pl.pallas_call(tables_kernel, out_shape=[jax.ShapeDtypeStruct((refs, LANE...  1.19 us
    pallas_call x1, Pallas kernels, on_device(): pl.pallas_call(pack_kernel, out_shape=jax.ShapeDtypeStruct((comps * high...  0.94 us
  transfers between devices with their start and end apart: 8, of which 6 were waited for; matrix products, arithmetic and copies ran while one was open for 0% of the time, Pallas kernels for 18%

profile of v7, /device:TPU:0, one launch (start us, length us, event | category | flops | bytes accessed | tf_op | source)
XLA Modules:
  0.0 27.5 jit_solution(8191224117297552526)
XLA Ops:
  0.0 0.9 %pack.1 = bf16[200,128]{1,0:T(8,128)(2,1)S(1)} custom-call(s32[32]{0:T(128)} %owner_slots.1, bf16[3,32,512]{2,1,0:T(8,128)(2,1)} %bitcast.19), custom_call_target="tpu_custom_call" | custom-call | tf_op jit(solution)/shard_map/pack/pallas_call | solution.py:263
  1.0 3.1 %collective-permute-start = (bf16[200,128]{1,0:T(8,128)(2,1)S(1)}, bf16[200,128]{1,0:T(8,128)(2,1)S(1)}, u32[]{:S(2)}, u32[]{:S(2)}) collective-permute-start(bf16[200,128]{1,0:T(8,128)(2,1)S(1)} %pack.1), channel_id=1, source_target_pairs={{0,4},{4,8},{8,12},{12,0},{1,5},{5,9},{9,13},{13,1},{2,6},{6,10},{... | collective-permute-start | bytes 153608 | tf_op jit(solution)/shard_map/ppermute | solution.py:284
  4.0 2.6 %collective-permute-start.1 = (bf16[200,128]{1,0:T(8,128)(2,1)S(1)}, bf16[200,128]{1,0:T(8,128)(2,1)S(1)}, u32[]{:S(2)}, u32[]{:S(2)}) collective-permute-start(bf16[200,128]{1,0:T(8,128)(2,1)S(1)} %pack.1), channel_id=1, source_target_pairs={{0,8},{4,12},{8,0},{12,4},{1,9},{5,13},{9,1},{13,5},{2,10},{6,14},... | collective-permute-start | bytes 153608 | tf_op jit(solution)/shard_map/ppermute | solution.py:284
  6.6 1.3 %collective-permute-start.2 = (bf16[200,128]{1,0:T(8,128)(2,1)S(1)}, bf16[200,128]{1,0:T(8,128)(2,1)S(1)}, u32[]{:S(2)}, u32[]{:S(2)}) collective-permute-start(bf16[200,128]{1,0:T(8,128)(2,1)S(1)} %pack.1), channel_id=1, source_target_pairs={{0,12},{4,0},{8,4},{12,8},{1,13},{5,1},{9,5},{13,9},{2,14},{6,2},{... | collective-permute-start | bytes 153608 | tf_op jit(solution)/shard_map/ppermute | solution.py:284
  8.0 1.2 %tables.1 = (s32[40,128]{1,0:T(8,128)S(1)}, s32[40,128]{1,0:T(8,128)S(1)}, f32[40,1024]{1,0:T(8,128)S(1)}, bf16[256,512]{1,0:T(8,128)(2,1)S(1)}, f32[120,128]{1,...) custom-call(s32[4,10]{1,0:T(4,128)} %sids_in.1, s32[4,10]{1,0:T(4,128)} %offs_in.1, s32[4,128]{1,0:T(4,128)} %bitcast.24, ...), custom_call_target="tpu_custom_call" | custom-call | tf_op jit(solution)/shard_map/tables/pallas_call | solution.py:289
  9.2 0.0 collective-permute-done
  9.2 1.2 %collective-permute-done.1 = bf16[200,128]{1,0:T(8,128)(2,1)S(1)} collective-permute-done((bf16[200,128]{1,0:T(8,128)(2,1)S(1)}, bf16[200,128]{1,0:T(8,128)(2,1)S(1)}, u32[]{:S(2)}, u32[]{:S(2)}) %collective-permute-start.1) | collective-permute-done | bytes 51232 | tf_op jit(solution)/shard_map/ppermute | solution.py:284
  10.3 0.5 %collective-permute-done.2 = bf16[200,128]{1,0:T(8,128)(2,1)S(1)} collective-permute-done((bf16[200,128]{1,0:T(8,128)(2,1)S(1)}, bf16[200,128]{1,0:T(8,128)(2,1)S(1)}, u32[]{:S(2)}, u32[]{:S(2)}) %collective-permute-start.2) | collective-permute-done | bytes 51232 | tf_op jit(solution)/shard_map/ppermute | solution.py:284
  10.8 0.1 collective-permute-start.3
  10.9 1.7 %collective-permute-start.4 = (s32[40,128]{1,0:T(8,128)S(1)}, s32[40,128]{1,0:T(8,128)S(1)}, u32[]{:S(2)}, u32[]{:S(2)}) collective-permute-start(s32[40,128]{1,0:T(8,128)S(1)} %get-tuple-element.33.args_2_), channel_id=1, source_target_pairs={{0,2},{2,0},{1,3},{3,1},{4,6},{6,4},{5,7},{7,5},{8,10},{10,8},{9,1... | collective-permute-start | bytes 61448 | tf_op jit(solution)/shard_map/ppermute | solution.py:238
  12.6 1.2 %filters.2.args_2_ = bf16[10,384,256]{2,1,0:T(8,128)(2,1)S(1)} custom-call(bf16[10,3,4,300]{3,2,1,0:T(4,128)(2,1)S(1)} %get-tuple-element.30.waves), custom_call_target="tpu_custom_call" | custom-call | tf_op jit(solution)/shard_map/filters/pallas_call | solution.py:315
  13.9 0.0 collective-permute-done.3.args_1_
  13.9 0.9 %collective-permute-done.4.args_3_ = s32[40,128]{1,0:T(8,128)S(1)} collective-permute-done((s32[40,128]{1,0:T(8,128)S(1)}, s32[40,128]{1,0:T(8,128)S(1)}, u32[]{:S(2)}, u32[]{:S(2)}) %collective-permute-start.4) | collective-permute-done | bytes 20512 | tf_op jit(solution)/shard_map/ppermute | solution.py:238
  14.8 0.3 %select.1 = (f32[120,512]{1,0:T(8,128)S(1)}, bf16[120,512]{1,0:T(8,128)(2,1)S(1)}) custom-call(bf16[4,200,128]{2,1,0:T(8,128)(2,1)S(1)} %pad_maximum_fusion.args_0_, bf16[4,200,128]{2,1,0:T(8,128)(2,1)S(1)} %collective-permute-done.3.args_1_, s32[40,128]{1,0:T(8,128)S(1)} %get-tuple-element.33.args_2_, s32[40,128]{1,0:T(8,128)S(1)} %collective-permute-done.4.args_3_, ...), custom_call_target="tpu_custom_call" | custom-call | tf_op jit(solution)/shard_map/select/pallas_call | solution.py:331
  15.1 1.7 %collective-permute-start.5 = (bf16[120,512]{1,0:T(8,128)(2,1)S(1)}, bf16[120,512]{1,0:T(8,128)(2,1)S(1)}, u32[]{:S(2)}, u32[]{:S(2)}) collective-permute-start(bf16[120,512]{1,0:T(8,128)(2,1)S(1)} %get-tuple-element.36), channel_id=1, source_target_pairs={{0,2},{2,0},{1,3},{3,1},{4,6},{6,4},{5,7},{7,5},{8,10},{10,8},{9,1... | collective-permute-start | bytes 368648 | tf_op jit(solution)/shard_map/ppermute | solution.py:238
  16.8 2.5 %filters.3.args_3_ = bf16[20,384,256]{2,1,0:T(8,128)(2,1)S(1)} custom-call(bf16[10,3,4,300]{3,2,1,0:T(4,128)(2,1)S(1)} %get-tuple-element.30.waves), custom_call_target="tpu_custom_call" | custom-call | tf_op jit(solution)/shard_map/filters/pallas_call | solution.py:315
  19.3 0.8 %collective-permute-done.5.args_1_ = bf16[120,512]{1,0:T(8,128)(2,1)S(1)} collective-permute-done((bf16[120,512]{1,0:T(8,128)(2,1)S(1)}, bf16[120,512]{1,0:T(8,128)(2,1)S(1)}, u32[]{:S(2)}, u32[]{:S(2)}) %collective-permute-start.5) | collective-permute-done | bytes 122912 | tf_op jit(solution)/shard_map/ppermute | solution.py:238
  20.1 2.5 %correlate.1 = (f32[2,4,256]{2,1,0:T(4,128)S(1)}, f32[1,2,4,256]{3,2,1,0:T(4,128)S(1)}) custom-call(f32[120,512]{1,0:T(8,128)S(1)} %get-tuple-element.35.args_0_, bf16[120,512]{1,0:T(8,128)(2,1)S(1)} %collective-permute-done.5.args_1_, bf16[10,384,256]{2,1,0:T(8,128)(2,1)S(1)} %filters.2.args_2_, bf16[20,384,256]{2,1,0:T(8,128)(2,1)S(1)} %filters.3.args_3_, ...), custom_call_target="tpu_custom_call" | custom-call | tf_op jit(solution)/shard_map/correlate/pallas_call | solution.py:346
  22.6 0.1 collective-permute-start.6
  22.6 1.2 %collective-permute-done.6 = f32[2,4,256]{2,1,0:T(4,128)S(1)} collective-permute-done((f32[2,4,256]{2,1,0:T(4,128)S(1)}, f32[2,4,256]{2,1,0:T(4,128)S(1)}, u32[]{:S(2)}, u32[]{:S(2)}) %collective-permute-start.6) | collective-permute-done | bytes 8224 | tf_op jit(solution)/shard_map/ppermute | solution.py:238
  23.8 1.4 %collective-permute-start.7 = (f32[4,256]{1,0:T(4,128)S(1)}, f32[4,256]{1,0:T(4,128)S(1)}, u32[]{:S(2)}, u32[]{:S(2)}) collective-permute-start(f32[4,256]{1,0:T(4,128)S(1)} %slice_bitcast_fusion.1), channel_id=1, source_target_pairs={{0,3},{1,2},{2,1},{3,0},{4,7},{5,6},{6,5},{7,4},{8,11},{9,10},{10,... | collective-permute-start | bytes 12296 | tf_op jit(solution)/shard_map/ppermute | solution.py:238
  25.2 1.7 %collective-permute-done.7 = f32[4,256]{1,0:T(4,128)S(1)} collective-permute-done((f32[4,256]{1,0:T(4,128)S(1)}, f32[4,256]{1,0:T(4,128)S(1)}, u32[]{:S(2)}, u32[]{:S(2)}) %collective-permute-start.7) | collective-permute-done | bytes 4128 | tf_op jit(solution)/shard_map/ppermute | solution.py:238
  26.9 0.6 %pad_maximum_fusion.1 = f32[8,256]{1,0:T(8,128)} fusion(f32[4,256]{1,0:T(4,128)S(1)} %get-tuple-element.46, f32[4,256]{1,0:T(4,128)S(1)} %get-tuple-element.45), kind=kLoop, calls=%fused_computation.1 | loop fusion | flops 2048 | bytes 16384 | tf_op jit(solution)/shard_map/concatenate | solution.py:375
  (4 shorter events, 0.0 us)
Async XLA Ops:
  1.0 8.2 %collective-permute-start = (bf16[200,128]{1,0:T(8,128)(2,1)S(1)}, bf16[200,128]{1,0:T(8,128)(2,1)S(1)}, u32[]{:S(2)}, u32[]{:S(2)}) collective-permute-start(bf16[200,128]{1,0:T(8,128)(2,1)S(1)} %pack.1), channel_id=1, source_target_pairs={{0,4},{4,8},{8,12},{12,0},{1,5},{5,9},{9,13},{13,1},{2,6},{6,10},{... | collective-permute-start | bytes 153608 | tf_op jit(solution)/shard_map/ppermute | solution.py:284
  4.0 6.3 %collective-permute-start.1 = (bf16[200,128]{1,0:T(8,128)(2,1)S(1)}, bf16[200,128]{1,0:T(8,128)(2,1)S(1)}, u32[]{:S(2)}, u32[]{:S(2)}) collective-permute-start(bf16[200,128]{1,0:T(8,128)(2,1)S(1)} %pack.1), channel_id=1, source_target_pairs={{0,8},{4,12},{8,0},{12,4},{1,9},{5,13},{9,1},{13,5},{2,10},{6,14},... | collective-permute-start | bytes 153608 | tf_op jit(solution)/shard_map/ppermute | solution.py:284
  6.6 4.2 %collective-permute-start.2 = (bf16[200,128]{1,0:T(8,128)(2,1)S(1)}, bf16[200,128]{1,0:T(8,128)(2,1)S(1)}, u32[]{:S(2)}, u32[]{:S(2)}) collective-permute-start(bf16[200,128]{1,0:T(8,128)(2,1)S(1)} %pack.1), channel_id=1, source_target_pairs={{0,12},{4,0},{8,4},{12,8},{1,13},{5,1},{9,5},{13,9},{2,14},{6,2},{... | collective-permute-start | bytes 153608 | tf_op jit(solution)/shard_map/ppermute | solution.py:284
  10.8 3.0 %collective-permute-start.3 = (bf16[4,200,128]{2,1,0:T(8,128)(2,1)S(1)}, bf16[4,200,128]{2,1,0:T(8,128)(2,1)S(1)}, u32[]{:S(2)}, u32[]{:S(2)}) collective-permute-start(bf16[4,200,128]{2,1,0:T(8,128)(2,1)S(1)} %pad_maximum_fusion.args_0_), channel_id=1, source_target_pairs={{0,1},{1,0},{2,3},{3,2},{4,5},{5,4},{6,7},{7,6},{8,9},{9,8},{10,11... | collective-permute-start | bytes 614408 | tf_op jit(solution)/shard_map/ppermute | solution.py:238
  10.9 3.8 %collective-permute-start.4 = (s32[40,128]{1,0:T(8,128)S(1)}, s32[40,128]{1,0:T(8,128)S(1)}, u32[]{:S(2)}, u32[]{:S(2)}) collective-permute-start(s32[40,128]{1,0:T(8,128)S(1)} %get-tuple-element.33.args_2_), channel_id=1, source_target_pairs={{0,2},{2,0},{1,3},{3,1},{4,6},{6,4},{5,7},{7,5},{8,10},{10,8},{9,1... | collective-permute-start | bytes 61448 | tf_op jit(solution)/shard_map/ppermute | solution.py:238
  15.1 4.9 %collective-permute-start.5 = (bf16[120,512]{1,0:T(8,128)(2,1)S(1)}, bf16[120,512]{1,0:T(8,128)(2,1)S(1)}, u32[]{:S(2)}, u32[]{:S(2)}) collective-permute-start(bf16[120,512]{1,0:T(8,128)(2,1)S(1)} %get-tuple-element.36), channel_id=1, source_target_pairs={{0,2},{2,0},{1,3},{3,1},{4,6},{6,4},{5,7},{7,5},{8,10},{10,8},{9,1... | collective-permute-start | bytes 368648 | tf_op jit(solution)/shard_map/ppermute | solution.py:238
  22.6 1.2 %collective-permute-start.6 = (f32[2,4,256]{2,1,0:T(4,128)S(1)}, f32[2,4,256]{2,1,0:T(4,128)S(1)}, u32[]{:S(2)}, u32[]{:S(2)}) collective-permute-start(f32[2,4,256]{2,1,0:T(4,128)S(1)} %bitcast.18), channel_id=1, source_target_pairs={{0,1},{1,0},{2,3},{3,2},{4,5},{5,4},{6,7},{7,6},{8,9},{9,8},{10,11... | collective-permute-start | bytes 24584 | tf_op jit(solution)/shard_map/ppermute | solution.py:238
  23.8 3.0 %collective-permute-start.7 = (f32[4,256]{1,0:T(4,128)S(1)}, f32[4,256]{1,0:T(4,128)S(1)}, u32[]{:S(2)}, u32[]{:S(2)}) collective-permute-start(f32[4,256]{1,0:T(4,128)S(1)} %slice_bitcast_fusion.1), channel_id=1, source_target_pairs={{0,3},{1,2},{2,1},{3,0},{4,7},{5,6},{6,5},{7,4},{8,11},{9,10},{10,... | collective-permute-start | bytes 12296 | tf_op jit(solution)/shard_map/ppermute | solution.py:238

commit v8 on v7

--- a/solution.py
+++ b/solution.py
@@ -10,6 +10,7 @@
 LANES = 128
 SPAN = 64
 EXTRA = 8
+UNROLL = 6
 
 
 def round_up(value, step):
@@ -37,7 +38,31 @@
         copy.wait()
 
 
-def tables_kernel(sids_in, offs_in, start_in, len_in, waves_in, sid_col, off_col, mask, band, scale, waves, *scratch):
+def build_filters(begin, waves, filters):
+    js, _, count, taps = waves.shape
+    groups, depth, _ = filters.shape
+
+    def one_group(i):
+        g = begin + i
+        wave = waves[lax.rem(g, js), g // js].astype(jnp.float32)
+        wave = jnp.concatenate([wave, jnp.zeros((count, depth - taps), jnp.float32)], axis=1)
+        rows = []
+        for k in range(count):
+            row = jnp.broadcast_to(wave[k : k + 1], (SPAN, depth))
+            rows.append(pltpu.roll(row, 0, 1, stride=1, stride_axis=0))
+        filters[i] = jnp.concatenate(rows, axis=0).T.astype(jnp.bfloat16)
+
+    def some_groups(t, carry):
+        for u in range(UNROLL):
+            one_group(t * UNROLL + u)
+        return carry
+
+    lax.fori_loop(0, groups // UNROLL, some_groups, 0)
+    for i in range(groups // UNROLL * UNROLL, groups):
+        one_group(i)
+
+
+def tables_kernel(sids_in, offs_in, start_in, len_in, waves_in, sid_col, off_col, mask, band, scale, waves, filters, *scratch):
     sids, offs, gap_start, gap_len, sems = scratch
     pairs = ((waves_in, waves), (sids_in, sids), (offs_in, offs), (start_in, gap_start), (len_in, gap_len))
     copies = [pltpu.make_async_copy(source, place, sems.at[i]) for i, (source, place) in enumerate(pairs)]
@@ -74,24 +99,21 @@
             factor = 1.0 / (taps * jnp.sqrt(power + 1e-06))
             first = (c * js + j) * count
             scale[first : first + count, :] = jnp.broadcast_to(factor, (count, LANES))
+    build_filters(0, waves, filters)
+
+
+def middle_kernel(begin, nfar, *args):
+    asked, waves, columns, filters = args[:nfar], args[nfar], args[nfar + 1 : -1], args[-1]
+    count, js = asked[0].shape
+    for source, column in zip(asked, columns):
+        for k in range(count):
+            for j in range(js):
+                column[j * count + k, :] = jnp.full((LANES,), source[k, j], jnp.int32)
+    build_filters(begin, waves, filters)
 
 
 def filters_kernel(begin, waves, filters):
-    js, _, count, taps = waves.shape
-    groups, depth, _ = filters.shape
-
-    def one_group(i, carry):
-        g = begin + i
-        wave = waves[lax.rem(g, js), g // js].astype(jnp.float32)
-        wave = jnp.concatenate([wave, jnp.zeros((count, depth - taps), jnp.float32)], axis=1)
-        rows = []
-        for k in range(count):
-            row = jnp.broadcast_to(wave[k : k + 1], (SPAN, depth))
-            rows.append(pltpu.roll(row, 0, 1, stride=1, stride_axis=0))
-        filters[i] = jnp.concatenate(rows, axis=0).T.astype(jnp.bfloat16)
-        return carry
-
-    lax.fori_loop(0, groups, one_group, 0, unroll=5)
+    build_filters(begin, waves, filters)
 
 
 def select_kernel(comps, high, nsub, *args):
@@ -238,6 +260,12 @@
     return lax.ppermute(value, axis, [(i, i ^ distance) for i in range(lax.axis_size(axis))])
 
 
+def crossed(value, distance):
+    nsub = lax.axis_size("sub")
+    count = lax.axis_size("slab") * nsub
+    return lax.ppermute(value, ("slab", "sub"), [(i, i ^ (distance * nsub + nsub - 1)) for i in range(count)])
+
+
 def stays(value):
     return pltpu.with_memory_space_constraint(value, pltpu.HBM)
 
@@ -284,20 +312,30 @@
             column.append(lax.ppermute(block, "tmpl", [(i, (i + d) % ntmpl) for i in range(ntmpl)]))
     else:
         column = list(lax.all_gather(block, "tmpl", axis=0))
+    asked = [crossed(station_ids, d) for d in range(1, nslab)]
     waves = templates.transpose(1, 2, 0, 3)
     reach = round_up(taps + LANES - 1, LANES)
-    sid_col, off_col, mask, band, scale, waves = pl.pallas_call(
+    depth = round_up(taps + SPAN - 1, LANES)
+    groups = comps * js
+    first, second = groups // 5, groups // 5
+
+    def bank(size):
+        return jax.ShapeDtypeStruct((size, depth, count * SPAN), jnp.bfloat16)
+
+    column_type = jax.ShapeDtypeStruct((refs, LANES), jnp.int32)
+    sid_col, off_col, mask, band, scale, waves, bank_a = pl.pallas_call(
         tables_kernel,
         out_shape=[
-            jax.ShapeDtypeStruct((refs, LANES), jnp.int32),
-            jax.ShapeDtypeStruct((refs, LANES), jnp.int32),
+            column_type,
+            column_type,
             jax.ShapeDtypeStruct((refs, time), jnp.float32),
             jax.ShapeDtypeStruct((2 * LANES, reach), jnp.bfloat16),
             jax.ShapeDtypeStruct((chans, LANES), jnp.float32),
             jax.ShapeDtypeStruct(waves.shape, waves.dtype),
+            bank(first),
         ],
         in_specs=[hbm] * 5,
-        out_specs=[vmem] * 6,
+        out_specs=[vmem] * 7,
         scratch_shapes=[
             pltpu.SMEM(station_ids.shape, jnp.int32),
             pltpu.SMEM(offsets.shape, jnp.int32),
@@ -305,29 +343,22 @@
             pltpu.VMEM(gap_len.T.shape, jnp.int32),
             pltpu.SemaphoreType.DMA((5,)),
         ],
-        compiler_params=params(8),
+        compiler_params=params(12),
         name="tables",
     )(*[stays(value) for value in (station_ids, offsets, gap_start.T, gap_len.T, waves)])
-    sid_cols = [sid_col] + [swapped(sid_col, "slab", d) for d in range(1, nslab)]
-    depth = round_up(taps + SPAN - 1, LANES)
-
-    def bank(begin, groups):
-        return pl.pallas_call(
-            functools.partial(filters_kernel, begin),
-            out_shape=jax.ShapeDtypeStruct((groups, depth, count * SPAN), jnp.bfloat16),
-            in_specs=[vmem],
-            out_specs=vmem,
-            compiler_params=params(16),
-            name="filters",
-        )(waves)
-
-    groups = comps * js
-    early = groups // 3
-    bank_a = bank(0, early)
-    column, mask = lax.optimization_barrier((column, mask))
+    column, asked, mask = lax.optimization_barrier((column, asked, mask))
     head = jnp.stack(column)
     heads = [head] + [swapped(head, "sub", m) for m in range(1, nsub)]
-    heads, bank_a = lax.optimization_barrier((heads, bank_a))
+    *sid_far, bank_b = pl.pallas_call(
+        functools.partial(middle_kernel, first, nslab - 1),
+        out_shape=[column_type] * (nslab - 1) + [bank(second)],
+        in_specs=[smem] * (nslab - 1) + [vmem],
+        out_specs=[vmem] * nslab,
+        compiler_params=params(12),
+        name="middle",
+    )(*asked, waves)
+    heads, sid_far, bank_b = lax.optimization_barrier((heads, sid_far, bank_b))
+    sid_cols = [sid_col] + list(sid_far)
     near, *fars = pl.pallas_call(
         functools.partial(select_kernel, comps, high, nsub),
         out_shape=[jax.ShapeDtypeStruct((chans, width), jnp.float32)]
@@ -337,19 +368,26 @@
         compiler_params=params(16),
         name="select",
     )(*heads, *sid_cols, mask)
-    fars = [swapped(far, "slab", d + 1) for d, far in enumerate(fars)]
-    bank_b = bank(early, groups - early)
-    fars, bank_b = lax.optimization_barrier((fars, bank_b))
+    fars = [crossed(far, d + 1) for d, far in enumerate(fars)]
+    bank_c = pl.pallas_call(
+        functools.partial(filters_kernel, first + second),
+        out_shape=bank(groups - first - second),
+        in_specs=[vmem],
+        out_specs=vmem,
+        compiler_params=params(16),
+        name="filters",
+    )(waves)
+    fars, bank_c = lax.optimization_barrier((fars, bank_c))
     chunks = time // LANES
     each = width // nsub
     tall = chunks + 8
     keep, send = pl.pallas_call(
-        functools.partial(correlate_kernel, nslab, nsub, taps, 2),
+        functools.partial(correlate_kernel, nslab, nsub, taps, 3),
         out_shape=[
             jax.ShapeDtypeStruct((nslab, count, each), jnp.float32),
             jax.ShapeDtypeStruct((nsub - 1, nslab, count, each), jnp.float32),
         ],
-        in_specs=[vmem] * (nslab + 6),
+        in_specs=[vmem] * (nslab + 7),
         out_specs=[vmem] * 2,
         scratch_shapes=[
             pltpu.VMEM((chans, time), jnp.float32),
@@ -360,12 +398,12 @@
         ],
         compiler_params=params(32),
         name="correlate",
-    )(near, *fars, bank_a, bank_b, off_col, mask, band, scale)
+    )(near, *fars, bank_a, bank_b, bank_c, off_col, mask, band, scale)
     for m in range(1, nsub):
         keep = keep + swapped(send[m - 1], "sub", m)
     lines = [keep[0]]
     for d in range(1, nslab):
-        lines.append(swapped(keep[d], ("slab", "sub"), d * nsub + nsub - 1))
+        lines.append(crossed(keep[d], d))
     result = []
     for s in range(nslab):
         line = lines[0]

time: 27.6 us -> 26.1 us (0.946)
  starting transfers between devices: 11.9 us -> 10.2 us
  Pallas kernels: 8.72 us -> 9.09 us
    ppermute x0 -> x3, waiting for transfers between devices: none -> 4.91 us  [crossed(): lax.ppermute(value, ('slab', 'sub'), [(i, i ^ distance * nsub + nsub - 1)...]
    ppermute x5 -> x2, starting transfers between devices: 4.89 us -> 0.54 us  [swapped(): lax.ppermute(value, axis, [(i, i ^ distance) for i in range(lax.axis_size...]
    ppermute x5 -> x2, waiting for transfers between devices: 4.48 us -> 1.03 us  [swapped(): lax.ppermute(value, axis, [(i, i ^ distance) for i in range(lax.axis_size...]
    ppermute x0 -> x3, starting transfers between devices: none -> 2.65 us  [crossed(): lax.ppermute(value, ('slab', 'sub'), [(i, i ^ distance * nsub + nsub - 1)...]
    ppermute x3, waiting for transfers between devices: 1.63 us -> 0.01 us  [on_device(): lax.ppermute(block, 'tmpl', [(i, (i + d) % ntmpl) for i in range(ntmpl)])]
    pallas_call x4, Pallas kernels: 7.43 us -> 7.8 us  [the longest x1 2.49 us: on_device(): pl.pallas_call(functools.partial(correlate_kernel, nslab, nsub, taps, 3),...]
  transfers between devices with their start and end apart: 8 -> 8, of which waited for: 6 -> 4; matrix products, arithmetic and copies ran while one was open for 0% -> 0% of each run, Pallas kernels for 18% -> 20%
where the time goes in v8:
time: 26.1 us; the launch traced here: 26 us
  starting transfers between devices  10.2 us (39%)
  Pallas kernels  9.09 us (35%)
  waiting for transfers between devices  5.95 us (23%)
  other arithmetic  0.65 us (2%)
    ppermute x3, starting transfers between devices, on_device(): lax.ppermute(block, 'tmpl', [(i, (i + d) % ntmpl) for i in range(ntmpl)])  7.01 us
    ppermute x3, waiting for transfers between devices, crossed(): lax.ppermute(value, ('slab', 'sub'), [(i, i ^ distance * nsub + nsub - 1)...  4.91 us
    ppermute x3, starting transfers between devices, crossed(): lax.ppermute(value, ('slab', 'sub'), [(i, i ^ distance * nsub + nsub - 1)...  2.65 us
    pallas_call x1, Pallas kernels, on_device(): pl.pallas_call(functools.partial(correlate_kernel, nslab, nsub, taps, 3),...  2.49 us
    pallas_call x1, Pallas kernels, on_device(): pl.pallas_call(functools.partial(filters_kernel, first + second), out_sha...  2.18 us
    pallas_call x1, Pallas kernels, on_device(): pl.pallas_call(tables_kernel, out_shape=[column_type, column_type, jax.Sh...  1.85 us
    pallas_call x1, Pallas kernels, on_device(): pl.pallas_call(functools.partial(middle_kernel, first, nslab - 1), out_sh...  1.28 us
    ppermute x2, waiting for transfers between devices, swapped(): lax.ppermute(value, axis, [(i, i ^ distance) for i in range(lax.axis_size...  1.03 us
  transfers between devices with their start and end apart: 8, of which 4 were waited for; matrix products, arithmetic and copies ran while one was open for 0% of the time, Pallas kernels for 20%

profile of v8, /device:TPU:0, one launch (start us, length us, event | category | flops | bytes accessed | tf_op | source)
XLA Modules:
  0.0 26.0 jit_solution(10779422299363174399)
XLA Ops:
  0.0 0.9 %pack.1 = bf16[200,128]{1,0:T(8,128)(2,1)S(1)} custom-call(s32[32]{0:T(128)} %owner_slots.1, bf16[3,32,512]{2,1,0:T(8,128)(2,1)} %bitcast.19), custom_call_target="tpu_custom_call" | custom-call | tf_op jit(solution)/shard_map/pack/pallas_call | solution.py:291
  1.0 3.1 %collective-permute-start = (bf16[200,128]{1,0:T(8,128)(2,1)S(1)}, bf16[200,128]{1,0:T(8,128)(2,1)S(1)}, u32[]{:S(2)}, u32[]{:S(2)}) collective-permute-start(bf16[200,128]{1,0:T(8,128)(2,1)S(1)} %pack.1), channel_id=1, source_target_pairs={{0,4},{4,8},{8,12},{12,0},{1,5},{5,9},{9,13},{13,1},{2,6},{6,10},{... | collective-permute-start | bytes 153608 | tf_op jit(solution)/shard_map/ppermute | solution.py:312
  4.0 2.6 %collective-permute-start.1 = (bf16[200,128]{1,0:T(8,128)(2,1)S(1)}, bf16[200,128]{1,0:T(8,128)(2,1)S(1)}, u32[]{:S(2)}, u32[]{:S(2)}) collective-permute-start(bf16[200,128]{1,0:T(8,128)(2,1)S(1)} %pack.1), channel_id=1, source_target_pairs={{0,8},{4,12},{8,0},{12,4},{1,9},{5,13},{9,1},{13,5},{2,10},{6,14},... | collective-permute-start | bytes 153608 | tf_op jit(solution)/shard_map/ppermute | solution.py:312
  6.6 1.3 %collective-permute-start.2 = (bf16[200,128]{1,0:T(8,128)(2,1)S(1)}, bf16[200,128]{1,0:T(8,128)(2,1)S(1)}, u32[]{:S(2)}, u32[]{:S(2)}) collective-permute-start(bf16[200,128]{1,0:T(8,128)(2,1)S(1)} %pack.1), channel_id=1, source_target_pairs={{0,12},{4,0},{8,4},{12,8},{1,13},{5,1},{9,5},{13,9},{2,14},{6,2},{... | collective-permute-start | bytes 153608 | tf_op jit(solution)/shard_map/ppermute | solution.py:312
  8.0 0.1 collective-permute-start.3
  8.1 1.8 %tables.1 = (s32[40,128]{1,0:T(8,128)S(1)}, s32[40,128]{1,0:T(8,128)S(1)}, f32[40,1024]{1,0:T(8,128)S(1)}, bf16[256,512]{1,0:T(8,128)(2,1)S(1)}, f32[120,128]{1,...) custom-call(s32[4,10]{1,0:T(4,128)} %sids_in.1, s32[4,10]{1,0:T(4,128)} %offs_in.1, ...), custom_call_target="tpu_custom_call" | custom-call | tf_op jit(solution)/shard_map/tables/pallas_call | solution.py:326
  9.9 1.3 %collective-permute-done.3.args_0_ = s32[4,10]{1,0:T(4,128)S(1)} collective-permute-done((s32[4,10]{1,0:T(4,128)}, s32[4,10]{1,0:T(4,128)S(1)}, u32[]{:S(2)}, u32[]{:S(2)}) %collective-permute-start.3) | collective-permute-done | bytes 192 | tf_op jit(solution)/shard_map/ppermute | solution.py:266
  11.2 0.0 collective-permute-done
  11.2 0.0 collective-permute-done.1
  11.2 0.0 collective-permute-done.2
  11.2 0.3 %collective-permute-start.4 = (bf16[4,200,128]{2,1,0:T(8,128)(2,1)S(1)}, bf16[4,200,128]{2,1,0:T(8,128)(2,1)S(1)}, u32[]{:S(2)}, u32[]{:S(2)}) collective-permute-start(bf16[4,200,128]{2,1,0:T(8,128)(2,1)S(1)} %pad_maximum_fusion.args_0_), channel_id=1, source_target_pairs={{0,1},{1,0},{2,3},{3,2},{4,5},{5,4},{6,7},{7,6},{8,9},{9,8},{10,11... | collective-permute-start | bytes 614408 | tf_op jit(solution)/shard_map/ppermute | solution.py:260
  11.6 1.3 %middle.1 = (s32[40,128]{1,0:T(8,128)S(1)}, bf16[6,384,256]{2,1,0:T(8,128)(2,1)S(1)}) custom-call(s32[4,10]{1,0:T(4,128)S(1)} %collective-permute-done.3.args_0_, bf16[10,3,4,300]{3,2,1,0:T(4,128)(2,1)S(1)} %get-tuple-element.36.args_1_.waves), custom_call_target="tpu_custom_call" | custom-call | tf_op jit(solution)/shard_map/middle/pallas_call | solution.py:352
  12.9 0.0 collective-permute-done.4.args_1_
  12.9 0.3 %select.1 = (f32[120,512]{1,0:T(8,128)S(1)}, bf16[120,512]{1,0:T(8,128)(2,1)S(1)}) custom-call(bf16[4,200,128]{2,1,0:T(8,128)(2,1)S(1)} %pad_maximum_fusion.args_0_, bf16[4,200,128]{2,1,0:T(8,128)(2,1)S(1)} %collective-permute-done.4.args_1_, s32[40,128]{1,0:T(8,128)S(1)} %get-tuple-element.41.args_2_, s32[40,128]{1,0:T(8,128)S(1)} %get-tuple-element.42.args_3_, ...), custom_call_target="tpu_custom_call" | custom-call | tf_op jit(solution)/shard_map/select/pallas_call | solution.py:362
  13.2 1.4 %collective-permute-start.5 = (bf16[120,512]{1,0:T(8,128)(2,1)S(1)}, bf16[120,512]{1,0:T(8,128)(2,1)S(1)}, u32[]{:S(2)}, u32[]{:S(2)}) collective-permute-start(bf16[120,512]{1,0:T(8,128)(2,1)S(1)} %get-tuple-element.45), channel_id=1, source_target_pairs={{0,3},{1,2},{2,1},{3,0},{4,7},{5,6},{6,5},{7,4},{8,11},{9,10},{10,... | collective-permute-start | bytes 368648 | tf_op jit(solution)/shard_map/ppermute | solution.py:266
  14.6 2.2 %filters.1.args_4_ = bf16[18,384,256]{2,1,0:T(8,128)(2,1)S(1)} custom-call(bf16[10,3,4,300]{3,2,1,0:T(4,128)(2,1)S(1)} %get-tuple-element.36.args_1_.waves), custom_call_target="tpu_custom_call" | custom-call | tf_op jit(solution)/shard_map/filters/pallas_call | solution.py:372
  16.8 1.7 %collective-permute-done.5.args_1_ = bf16[120,512]{1,0:T(8,128)(2,1)S(1)} collective-permute-done((bf16[120,512]{1,0:T(8,128)(2,1)S(1)}, bf16[120,512]{1,0:T(8,128)(2,1)S(1)}, u32[]{:S(2)}, u32[]{:S(2)}) %collective-permute-start.5) | collective-permute-done | bytes 122912 | tf_op jit(solution)/shard_map/ppermute | solution.py:266
  18.6 2.5 %correlate.1 = (f32[2,4,256]{2,1,0:T(4,128)S(1)}, f32[1,2,4,256]{3,2,1,0:T(4,128)S(1)}) custom-call(f32[120,512]{1,0:T(8,128)S(1)} %get-tuple-element.44.args_0_, bf16[120,512]{1,0:T(8,128)(2,1)S(1)} %collective-permute-done.5.args_1_, bf16[6,384,256]{2,1,0:T(8,128)(2,1)S(1)} %get-tuple-element.47.args_2_, ...), custom_call_target="tpu_custom_call" | custom-call | tf_op jit(solution)/shard_map/correlate/pallas_call | solution.py:384
  21.1 0.2 collective-permute-start.6
  21.3 1.0 %collective-permute-done.6 = f32[2,4,256]{2,1,0:T(4,128)S(1)} collective-permute-done((f32[2,4,256]{2,1,0:T(4,128)S(1)}, f32[2,4,256]{2,1,0:T(4,128)S(1)}, u32[]{:S(2)}, u32[]{:S(2)}) %collective-permute-start.6) | collective-permute-done | bytes 8224 | tf_op jit(solution)/shard_map/ppermute | solution.py:260
  22.3 1.1 %collective-permute-start.7 = (f32[4,256]{1,0:T(4,128)S(1)}, f32[4,256]{1,0:T(4,128)S(1)}, u32[]{:S(2)}, u32[]{:S(2)}) collective-permute-start(f32[4,256]{1,0:T(4,128)S(1)} %slice_bitcast_fusion.1), channel_id=1, source_target_pairs={{0,3},{1,2},{2,1},{3,0},{4,7},{5,6},{6,5},{7,4},{8,11},{9,10},{10,... | collective-permute-start | bytes 12296 | tf_op jit(solution)/shard_map/ppermute | solution.py:266
  23.5 1.9 %collective-permute-done.7 = f32[4,256]{1,0:T(4,128)S(1)} collective-permute-done((f32[4,256]{1,0:T(4,128)S(1)}, f32[4,256]{1,0:T(4,128)S(1)}, u32[]{:S(2)}, u32[]{:S(2)}) %collective-permute-start.7) | collective-permute-done | bytes 4128 | tf_op jit(solution)/shard_map/ppermute | solution.py:266
  25.4 0.6 %pad_maximum_fusion.1 = f32[8,256]{1,0:T(8,128)} fusion(f32[4,256]{1,0:T(4,128)S(1)} %get-tuple-element.56, f32[4,256]{1,0:T(4,128)S(1)} %get-tuple-element.55), kind=kLoop, calls=%fused_computation.1 | loop fusion | flops 2048 | bytes 16384 | tf_op jit(solution)/shard_map/concatenate | solution.py:413
  (4 shorter events, 0.0 us)
Async XLA Ops:
  1.0 10.2 %collective-permute-start = (bf16[200,128]{1,0:T(8,128)(2,1)S(1)}, bf16[200,128]{1,0:T(8,128)(2,1)S(1)}, u32[]{:S(2)}, u32[]{:S(2)}) collective-permute-start(bf16[200,128]{1,0:T(8,128)(2,1)S(1)} %pack.1), channel_id=1, source_target_pairs={{0,4},{4,8},{8,12},{12,0},{1,5},{5,9},{9,13},{13,1},{2,6},{6,10},{... | collective-permute-start | bytes 153608 | tf_op jit(solution)/shard_map/ppermute | solution.py:312
  4.0 7.2 %collective-permute-start.1 = (bf16[200,128]{1,0:T(8,128)(2,1)S(1)}, bf16[200,128]{1,0:T(8,128)(2,1)S(1)}, u32[]{:S(2)}, u32[]{:S(2)}) collective-permute-start(bf16[200,128]{1,0:T(8,128)(2,1)S(1)} %pack.1), channel_id=1, source_target_pairs={{0,8},{4,12},{8,0},{12,4},{1,9},{5,13},{9,1},{13,5},{2,10},{6,14},... | collective-permute-start | bytes 153608 | tf_op jit(solution)/shard_map/ppermute | solution.py:312
  6.6 4.6 %collective-permute-start.2 = (bf16[200,128]{1,0:T(8,128)(2,1)S(1)}, bf16[200,128]{1,0:T(8,128)(2,1)S(1)}, u32[]{:S(2)}, u32[]{:S(2)}) collective-permute-start(bf16[200,128]{1,0:T(8,128)(2,1)S(1)} %pack.1), channel_id=1, source_target_pairs={{0,12},{4,0},{8,4},{12,8},{1,13},{5,1},{9,5},{13,9},{2,14},{6,2},{... | collective-permute-start | bytes 153608 | tf_op jit(solution)/shard_map/ppermute | solution.py:312
  8.0 3.2 %collective-permute-start.3 = (s32[4,10]{1,0:T(4,128)}, s32[4,10]{1,0:T(4,128)S(1)}, u32[]{:S(2)}, u32[]{:S(2)}) collective-permute-start(s32[4,10]{1,0:T(4,128)} %sids_in.1), channel_id=1, source_target_pairs={{0,3},{1,2},{2,1},{3,0},{4,7},{5,6},{6,5},{7,4},{8,11},{9,10},{10,... | collective-permute-start | bytes 488 | tf_op jit(solution)/shard_map/ppermute | solution.py:266
  11.2 1.6 %collective-permute-start.4 = (bf16[4,200,128]{2,1,0:T(8,128)(2,1)S(1)}, bf16[4,200,128]{2,1,0:T(8,128)(2,1)S(1)}, u32[]{:S(2)}, u32[]{:S(2)}) collective-permute-start(bf16[4,200,128]{2,1,0:T(8,128)(2,1)S(1)} %pad_maximum_fusion.args_0_), channel_id=1, source_target_pairs={{0,1},{1,0},{2,3},{3,2},{4,5},{5,4},{6,7},{7,6},{8,9},{9,8},{10,11... | collective-permute-start | bytes 614408 | tf_op jit(solution)/shard_map/ppermute | solution.py:260
  13.2 5.3 %collective-permute-start.5 = (bf16[120,512]{1,0:T(8,128)(2,1)S(1)}, bf16[120,512]{1,0:T(8,128)(2,1)S(1)}, u32[]{:S(2)}, u32[]{:S(2)}) collective-permute-start(bf16[120,512]{1,0:T(8,128)(2,1)S(1)} %get-tuple-element.45), channel_id=1, source_target_pairs={{0,3},{1,2},{2,1},{3,0},{4,7},{5,6},{6,5},{7,4},{8,11},{9,10},{10,... | collective-permute-start | bytes 368648 | tf_op jit(solution)/shard_map/ppermute | solution.py:266
  21.1 1.2 %collective-permute-start.6 = (f32[2,4,256]{2,1,0:T(4,128)S(1)}, f32[2,4,256]{2,1,0:T(4,128)S(1)}, u32[]{:S(2)}, u32[]{:S(2)}) collective-permute-start(f32[2,4,256]{2,1,0:T(4,128)S(1)} %bitcast.18), channel_id=1, source_target_pairs={{0,1},{1,0},{2,3},{3,2},{4,5},{5,4},{6,7},{7,6},{8,9},{9,8},{10,11... | collective-permute-start | bytes 24584 | tf_op jit(solution)/shard_map/ppermute | solution.py:260
  22.3 3.0 %collective-permute-start.7 = (f32[4,256]{1,0:T(4,128)S(1)}, f32[4,256]{1,0:T(4,128)S(1)}, u32[]{:S(2)}, u32[]{:S(2)}) collective-permute-start(f32[4,256]{1,0:T(4,128)S(1)} %slice_bitcast_fusion.1), channel_id=1, source_target_pairs={{0,3},{1,2},{2,1},{3,0},{4,7},{5,6},{6,5},{7,4},{8,11},{9,10},{10,... | collective-permute-start | bytes 12296 | tf_op jit(solution)/shard_map/ppermute | solution.py:266

commit v9 on v8

--- a/solution.py
+++ b/solution.py
@@ -172,7 +172,6 @@
     comps = chans // refs
     chunks = time // LANES
     count = keep.shape[1]
-    tall = low.shape[1]
     here, core = lax.axis_index("slab"), lax.axis_index("sub")
     for d in range(nslab):
         spot = pl.ds(pl.multiple_of(lax.bitwise_xor(here, d) * width, LANES), width)
@@ -183,6 +182,7 @@
             for c in range(comps):
                 got = fars[d - 1][c * refs : (c + 1) * refs, :].astype(jnp.float32)
                 segs[c * refs : (c + 1) * refs, spot] = got * live
+    span = banks[0].shape[1] // LANES
     lane = lax.broadcasted_iota(jnp.int32, (8, LANES), 1)
     zero = jnp.zeros((8, LANES), jnp.float32)
     for i in range(chans // 8):
@@ -198,50 +198,60 @@
         ]
         turned += [zero, zero]
         moved = [jnp.where(close, turned[r], turned[r + 1]) for r in range(chunks + 1)]
-        mine = [jnp.where(far, moved[r + 1], moved[r]) for r in range(chunks)] + [zero]
+        mine = [jnp.where(far, moved[r + 1], moved[r]) for r in range(chunks)]
+        swung = [pltpu.roll(part, SPAN, 1) for part in mine] + [zero]
         for r in range(chunks):
             segs[i * 8 : i * 8 + 8, r * LANES : (r + 1) * LANES] = mine[r]
             low[pl.ds(i * 8, 8), r, :] = mine[r]
-            half = jnp.where(lane < LANES - SPAN, pltpu.roll(mine[r], SPAN, 1), pltpu.roll(mine[r + 1], SPAN, 1))
-            high[pl.ds(i * 8, 8), r, :] = half
-        for r in range(chunks, tall):
+            high[pl.ds(i * 8, 8), r, :] = jnp.where(lane < LANES - SPAN, swung[r], swung[r + 1])
+        for r in range(chunks, chunks + span - 1):
             low[pl.ds(i * 8, 8), r, :] = zero
             high[pl.ds(i * 8, 8), r, :] = zero
     reach = band.shape[1] // LANES
     sums = {}
-    for r in reversed(range(chunks)):
-        part = segs[:, r * LANES : (r + 1) * LANES]
-        power = part * part
+    for first in range(0, chunks, 2):
+        batch = range(first, first + 2)
+        power = jnp.concatenate([segs[:, r * LANES : (r + 1) * LANES] for r in batch], axis=0)
+        power = power * power
         lead = power.astype(jnp.bfloat16)
         rest = (power - lead.astype(jnp.float32)).astype(jnp.bfloat16)
-        sums[r] = jnp.dot(jnp.concatenate([lead, rest], axis=1), band[...], preferred_element_type=jnp.float32)
+        both = jnp.concatenate([lead, rest], axis=1)
+        got = jnp.dot(both, band[...], preferred_element_type=jnp.float32)
+        for r in batch:
+            sums[r] = got[(r - first) * chans : (r - first + 1) * chans]
+    for r in range(chunks):
         window = sums[r][:, :LANES]
         for p in range(1, min(reach, chunks - r)):
             window = window + sums[r + p][:, p * LANES : (p + 1) * LANES]
         factor = scale[...] * lax.rsqrt(window / taps + 1e-06)
         for i in range(chans // 8):
             norm[pl.ds(i * 8, 8), r, :] = factor[i * 8 : i * 8 + 8]
-    span = banks[0].shape[1] // LANES
     accs = [jnp.zeros((chunks, LANES), jnp.float32) for _ in range(count)]
     side = lax.broadcasted_iota(jnp.int32, (chunks, LANES), 1) < SPAN
     weights = [(bank, i) for bank in banks for i in range(bank.shape[0])]
-    for g, (bank, i) in enumerate(weights):
-        base = g * count
+    def operand(g):
         rows = []
-        for ch in range(base, base + count):
+        for ch in range(g * count, (g + 1) * count):
             for source in (low, high):
                 rows.append(jnp.concatenate([source[ch, p : p + chunks, :] for p in range(span)], axis=1))
-        both = jnp.concatenate(rows, axis=0).astype(jnp.bfloat16)
-        res = jnp.dot(both, bank[i], preferred_element_type=jnp.float32)
+        return jnp.concatenate(rows, axis=0).astype(jnp.bfloat16)
+
+    def gather_sums(g, res):
+        base = g * count
         for k in range(count):
             left = (k // 2) * LANES
             tile = res[2 * k * chunks : 2 * (k + 1) * chunks, left : left + LANES]
             early, late = tile[:chunks], tile[chunks:]
             if k % 2 == 0:
-                wide = jnp.where(side, early, pltpu.roll(late, SPAN, 1))
+                first, turned = early, late
             else:
-                wide = jnp.where(side, pltpu.roll(early, SPAN, 1), late)
-            accs[k] = accs[k] + wide * norm[base + k]
+                turned = pltpu.roll(jnp.where(side, turned, early), SPAN, 1)
+                even, odd = jnp.where(side, first, turned), jnp.where(side, turned, late)
+                accs[k - 1] = accs[k - 1] + even * norm[base + k - 1]
+                accs[k] = accs[k] + odd * norm[base + k]
+
+    for g, (bank, i) in enumerate(weights):
+        gather_sums(g, jnp.dot(operand(g), bank[i], preferred_element_type=jnp.float32))
     for k in range(count):
         total[k] = accs[k]
     each = chunks // (nslab * nsub)

time: 26.1 us -> 25.9 us (level)
  transfers between devices with their start and end apart: 8 -> 8, of which waited for: 4 -> 4; matrix products, arithmetic and copies ran while one was open for 0% -> 0% of each run, Pallas kernels for 20% -> 21%
where the time goes in v9:
time: 25.9 us; the launch traced here: 25.8 us
  starting transfers between devices  10.2 us (39%)
  Pallas kernels  8.89 us (34%)
  waiting for transfers between devices  5.92 us (23%)
  other arithmetic  0.65 us (3%)
    ppermute x3, starting transfers between devices, on_device(): lax.ppermute(block, 'tmpl', [(i, (i + d) % ntmpl) for i in range(ntmpl)])  7.01 us
    ppermute x3, waiting for transfers between devices, crossed(): lax.ppermute(value, ('slab', 'sub'), [(i, i ^ distance * nsub + nsub - 1)...  4.9 us
    ppermute x3, starting transfers between devices, crossed(): lax.ppermute(value, ('slab', 'sub'), [(i, i ^ distance * nsub + nsub - 1)...  2.66 us
    pallas_call x1, Pallas kernels, on_device(): pl.pallas_call(functools.partial(correlate_kernel, nslab, nsub, taps, 3),...  2.29 us
    pallas_call x1, Pallas kernels, on_device(): pl.pallas_call(functools.partial(filters_kernel, first + second), out_sha...  2.18 us
    pallas_call x1, Pallas kernels, on_device(): pl.pallas_call(tables_kernel, out_shape=[column_type, column_type, jax.Sh...  1.85 us
    pallas_call x1, Pallas kernels, on_device(): pl.pallas_call(functools.partial(middle_kernel, first, nslab - 1), out_sh...  1.28 us
    ppermute x2, waiting for transfers between devices, swapped(): lax.ppermute(value, axis, [(i, i ^ distance) for i in range(lax.axis_size...  1.01 us
  transfers between devices with their start and end apart: 8, of which 4 were waited for; matrix products, arithmetic and copies ran while one was open for 0% of the time, Pallas kernels for 21%

profile of v9, /device:TPU:0, one launch (start us, length us, event | category | flops | bytes accessed | tf_op | source)
XLA Modules:
  0.0 25.8 jit_solution(6632602294514160307)
XLA Ops:
  0.0 0.9 %pack.1 = bf16[200,128]{1,0:T(8,128)(2,1)S(1)} custom-call(s32[32]{0:T(128)} %owner_slots.1, bf16[3,32,512]{2,1,0:T(8,128)(2,1)} %bitcast.19), custom_call_target="tpu_custom_call" | custom-call | tf_op jit(solution)/shard_map/pack/pallas_call | solution.py:301
  1.0 3.1 %collective-permute-start = (bf16[200,128]{1,0:T(8,128)(2,1)S(1)}, bf16[200,128]{1,0:T(8,128)(2,1)S(1)}, u32[]{:S(2)}, u32[]{:S(2)}) collective-permute-start(bf16[200,128]{1,0:T(8,128)(2,1)S(1)} %pack.1), channel_id=1, source_target_pairs={{0,4},{4,8},{8,12},{12,0},{1,5},{5,9},{9,13},{13,1},{2,6},{6,10},{... | collective-permute-start | bytes 153608 | tf_op jit(solution)/shard_map/ppermute | solution.py:322
  4.0 2.6 %collective-permute-start.1 = (bf16[200,128]{1,0:T(8,128)(2,1)S(1)}, bf16[200,128]{1,0:T(8,128)(2,1)S(1)}, u32[]{:S(2)}, u32[]{:S(2)}) collective-permute-start(bf16[200,128]{1,0:T(8,128)(2,1)S(1)} %pack.1), channel_id=1, source_target_pairs={{0,8},{4,12},{8,0},{12,4},{1,9},{5,13},{9,1},{13,5},{2,10},{6,14},... | collective-permute-start | bytes 153608 | tf_op jit(solution)/shard_map/ppermute | solution.py:322
  6.6 1.3 %collective-permute-start.2 = (bf16[200,128]{1,0:T(8,128)(2,1)S(1)}, bf16[200,128]{1,0:T(8,128)(2,1)S(1)}, u32[]{:S(2)}, u32[]{:S(2)}) collective-permute-start(bf16[200,128]{1,0:T(8,128)(2,1)S(1)} %pack.1), channel_id=1, source_target_pairs={{0,12},{4,0},{8,4},{12,8},{1,13},{5,1},{9,5},{13,9},{2,14},{6,2},{... | collective-permute-start | bytes 153608 | tf_op jit(solution)/shard_map/ppermute | solution.py:322
  8.0 0.1 collective-permute-start.3
  8.1 1.8 %tables.1 = (s32[40,128]{1,0:T(8,128)S(1)}, s32[40,128]{1,0:T(8,128)S(1)}, f32[40,1024]{1,0:T(8,128)S(1)}, bf16[256,512]{1,0:T(8,128)(2,1)S(1)}, f32[120,128]{1,...) custom-call(s32[4,10]{1,0:T(4,128)} %sids_in.1, s32[4,10]{1,0:T(4,128)} %offs_in.1, ...), custom_call_target="tpu_custom_call" | custom-call | tf_op jit(solution)/shard_map/tables/pallas_call | solution.py:336
  9.9 1.3 %collective-permute-done.3.args_0_ = s32[4,10]{1,0:T(4,128)S(1)} collective-permute-done((s32[4,10]{1,0:T(4,128)}, s32[4,10]{1,0:T(4,128)S(1)}, u32[]{:S(2)}, u32[]{:S(2)}) %collective-permute-start.3) | collective-permute-done | bytes 192 | tf_op jit(solution)/shard_map/ppermute | solution.py:276
  11.2 0.0 collective-permute-done
  11.2 0.0 collective-permute-done.1
  11.2 0.0 collective-permute-done.2
  11.2 0.3 %collective-permute-start.4 = (bf16[4,200,128]{2,1,0:T(8,128)(2,1)S(1)}, bf16[4,200,128]{2,1,0:T(8,128)(2,1)S(1)}, u32[]{:S(2)}, u32[]{:S(2)}) collective-permute-start(bf16[4,200,128]{2,1,0:T(8,128)(2,1)S(1)} %pad_maximum_fusion.args_0_), channel_id=1, source_target_pairs={{0,1},{1,0},{2,3},{3,2},{4,5},{5,4},{6,7},{7,6},{8,9},{9,8},{10,11... | collective-permute-start | bytes 614408 | tf_op jit(solution)/shard_map/ppermute | solution.py:270
  11.6 1.3 %middle.1 = (s32[40,128]{1,0:T(8,128)S(1)}, bf16[6,384,256]{2,1,0:T(8,128)(2,1)S(1)}) custom-call(s32[4,10]{1,0:T(4,128)S(1)} %collective-permute-done.3.args_0_, bf16[10,3,4,300]{3,2,1,0:T(4,128)(2,1)S(1)} %get-tuple-element.36.args_1_.waves), custom_call_target="tpu_custom_call" | custom-call | tf_op jit(solution)/shard_map/middle/pallas_call | solution.py:362
  12.9 0.0 collective-permute-done.4.args_1_
  12.9 0.3 %select.1 = (f32[120,512]{1,0:T(8,128)S(1)}, bf16[120,512]{1,0:T(8,128)(2,1)S(1)}) custom-call(bf16[4,200,128]{2,1,0:T(8,128)(2,1)S(1)} %pad_maximum_fusion.args_0_, bf16[4,200,128]{2,1,0:T(8,128)(2,1)S(1)} %collective-permute-done.4.args_1_, s32[40,128]{1,0:T(8,128)S(1)} %get-tuple-element.41.args_2_, s32[40,128]{1,0:T(8,128)S(1)} %get-tuple-element.42.args_3_, ...), custom_call_target="tpu_custom_call" | custom-call | tf_op jit(solution)/shard_map/select/pallas_call | solution.py:372
  13.2 1.4 %collective-permute-start.5 = (bf16[120,512]{1,0:T(8,128)(2,1)S(1)}, bf16[120,512]{1,0:T(8,128)(2,1)S(1)}, u32[]{:S(2)}, u32[]{:S(2)}) collective-permute-start(bf16[120,512]{1,0:T(8,128)(2,1)S(1)} %get-tuple-element.45), channel_id=1, source_target_pairs={{0,3},{1,2},{2,1},{3,0},{4,7},{5,6},{6,5},{7,4},{8,11},{9,10},{10,... | collective-permute-start | bytes 368648 | tf_op jit(solution)/shard_map/ppermute | solution.py:276
  14.6 2.2 %filters.1.args_4_ = bf16[18,384,256]{2,1,0:T(8,128)(2,1)S(1)} custom-call(bf16[10,3,4,300]{3,2,1,0:T(4,128)(2,1)S(1)} %get-tuple-element.36.args_1_.waves), custom_call_target="tpu_custom_call" | custom-call | tf_op jit(solution)/shard_map/filters/pallas_call | solution.py:382
  16.8 1.7 %collective-permute-done.5.args_1_ = bf16[120,512]{1,0:T(8,128)(2,1)S(1)} collective-permute-done((bf16[120,512]{1,0:T(8,128)(2,1)S(1)}, bf16[120,512]{1,0:T(8,128)(2,1)S(1)}, u32[]{:S(2)}, u32[]{:S(2)}) %collective-permute-start.5) | collective-permute-done | bytes 122912 | tf_op jit(solution)/shard_map/ppermute | solution.py:276
  18.6 2.3 %correlate.1 = (f32[2,4,256]{2,1,0:T(4,128)S(1)}, f32[1,2,4,256]{3,2,1,0:T(4,128)S(1)}) custom-call(f32[120,512]{1,0:T(8,128)S(1)} %get-tuple-element.44.args_0_, bf16[120,512]{1,0:T(8,128)(2,1)S(1)} %collective-permute-done.5.args_1_, bf16[6,384,256]{2,1,0:T(8,128)(2,1)S(1)} %get-tuple-element.47.args_2_, ...), custom_call_target="tpu_custom_call" | custom-call | tf_op jit(solution)/shard_map/correlate/pallas_call | solution.py:394
  20.9 0.2 collective-permute-start.6
  21.1 1.0 %collective-permute-done.6 = f32[2,4,256]{2,1,0:T(4,128)S(1)} collective-permute-done((f32[2,4,256]{2,1,0:T(4,128)S(1)}, f32[2,4,256]{2,1,0:T(4,128)S(1)}, u32[]{:S(2)}, u32[]{:S(2)}) %collective-permute-start.6) | collective-permute-done | bytes 8224 | tf_op jit(solution)/shard_map/ppermute | solution.py:270
  22.1 1.2 %collective-permute-start.7 = (f32[4,256]{1,0:T(4,128)S(1)}, f32[4,256]{1,0:T(4,128)S(1)}, u32[]{:S(2)}, u32[]{:S(2)}) collective-permute-start(f32[4,256]{1,0:T(4,128)S(1)} %slice_bitcast_fusion.1), channel_id=1, source_target_pairs={{0,3},{1,2},{2,1},{3,0},{4,7},{5,6},{6,5},{7,4},{8,11},{9,10},{10,... | collective-permute-start | bytes 12296 | tf_op jit(solution)/shard_map/ppermute | solution.py:276
  23.3 1.9 %collective-permute-done.7 = f32[4,256]{1,0:T(4,128)S(1)} collective-permute-done((f32[4,256]{1,0:T(4,128)S(1)}, f32[4,256]{1,0:T(4,128)S(1)}, u32[]{:S(2)}, u32[]{:S(2)}) %collective-permute-start.7) | collective-permute-done | bytes 4128 | tf_op jit(solution)/shard_map/ppermute | solution.py:276
  25.2 0.6 %pad_maximum_fusion.1 = f32[8,256]{1,0:T(8,128)} fusion(f32[4,256]{1,0:T(4,128)S(1)} %get-tuple-element.56, f32[4,256]{1,0:T(4,128)S(1)} %get-tuple-element.55), kind=kLoop, calls=%fused_computation.1 | loop fusion | flops 2048 | bytes 16384 | tf_op jit(solution)/shard_map/concatenate | solution.py:423
  (4 shorter events, 0.0 us)
Async XLA Ops:
  1.0 10.2 %collective-permute-start = (bf16[200,128]{1,0:T(8,128)(2,1)S(1)}, bf16[200,128]{1,0:T(8,128)(2,1)S(1)}, u32[]{:S(2)}, u32[]{:S(2)}) collective-permute-start(bf16[200,128]{1,0:T(8,128)(2,1)S(1)} %pack.1), channel_id=1, source_target_pairs={{0,4},{4,8},{8,12},{12,0},{1,5},{5,9},{9,13},{13,1},{2,6},{6,10},{... | collective-permute-start | bytes 153608 | tf_op jit(solution)/shard_map/ppermute | solution.py:322
  4.0 7.2 %collective-permute-start.1 = (bf16[200,128]{1,0:T(8,128)(2,1)S(1)}, bf16[200,128]{1,0:T(8,128)(2,1)S(1)}, u32[]{:S(2)}, u32[]{:S(2)}) collective-permute-start(bf16[200,128]{1,0:T(8,128)(2,1)S(1)} %pack.1), channel_id=1, source_target_pairs={{0,8},{4,12},{8,0},{12,4},{1,9},{5,13},{9,1},{13,5},{2,10},{6,14},... | collective-permute-start | bytes 153608 | tf_op jit(solution)/shard_map/ppermute | solution.py:322
  6.6 4.6 %collective-permute-start.2 = (bf16[200,128]{1,0:T(8,128)(2,1)S(1)}, bf16[200,128]{1,0:T(8,128)(2,1)S(1)}, u32[]{:S(2)}, u32[]{:S(2)}) collective-permute-start(bf16[200,128]{1,0:T(8,128)(2,1)S(1)} %pack.1), channel_id=1, source_target_pairs={{0,12},{4,0},{8,4},{12,8},{1,13},{5,1},{9,5},{13,9},{2,14},{6,2},{... | collective-permute-start | bytes 153608 | tf_op jit(solution)/shard_map/ppermute | solution.py:322
  8.0 3.2 %collective-permute-start.3 = (s32[4,10]{1,0:T(4,128)}, s32[4,10]{1,0:T(4,128)S(1)}, u32[]{:S(2)}, u32[]{:S(2)}) collective-permute-start(s32[4,10]{1,0:T(4,128)} %sids_in.1), channel_id=1, source_target_pairs={{0,3},{1,2},{2,1},{3,0},{4,7},{5,6},{6,5},{7,4},{8,11},{9,10},{10,... | collective-permute-start | bytes 488 | tf_op jit(solution)/shard_map/ppermute | solution.py:276
  11.2 1.6 %collective-permute-start.4 = (bf16[4,200,128]{2,1,0:T(8,128)(2,1)S(1)}, bf16[4,200,128]{2,1,0:T(8,128)(2,1)S(1)}, u32[]{:S(2)}, u32[]{:S(2)}) collective-permute-start(bf16[4,200,128]{2,1,0:T(8,128)(2,1)S(1)} %pad_maximum_fusion.args_0_), channel_id=1, source_target_pairs={{0,1},{1,0},{2,3},{3,2},{4,5},{5,4},{6,7},{7,6},{8,9},{9,8},{10,11... | collective-permute-start | bytes 614408 | tf_op jit(solution)/shard_map/ppermute | solution.py:270
  13.2 5.3 %collective-permute-start.5 = (bf16[120,512]{1,0:T(8,128)(2,1)S(1)}, bf16[120,512]{1,0:T(8,128)(2,1)S(1)}, u32[]{:S(2)}, u32[]{:S(2)}) collective-permute-start(bf16[120,512]{1,0:T(8,128)(2,1)S(1)} %get-tuple-element.45), channel_id=1, source_target_pairs={{0,3},{1,2},{2,1},{3,0},{4,7},{5,6},{6,5},{7,4},{8,11},{9,10},{10,... | collective-permute-start | bytes 368648 | tf_op jit(solution)/shard_map/ppermute | solution.py:276
  20.9 1.2 %collective-permute-start.6 = (f32[2,4,256]{2,1,0:T(4,128)S(1)}, f32[2,4,256]{2,1,0:T(4,128)S(1)}, u32[]{:S(2)}, u32[]{:S(2)}) collective-permute-start(f32[2,4,256]{2,1,0:T(4,128)S(1)} %bitcast.18), channel_id=1, source_target_pairs={{0,1},{1,0},{2,3},{3,2},{4,5},{5,4},{6,7},{7,6},{8,9},{9,8},{10,11... | collective-permute-start | bytes 24584 | tf_op jit(solution)/shard_map/ppermute | solution.py:270
  22.1 3.0 %collective-permute-start.7 = (f32[4,256]{1,0:T(4,128)S(1)}, f32[4,256]{1,0:T(4,128)S(1)}, u32[]{:S(2)}, u32[]{:S(2)}) collective-permute-start(f32[4,256]{1,0:T(4,128)S(1)} %slice_bitcast_fusion.1), channel_id=1, source_target_pairs={{0,3},{1,2},{2,1},{3,0},{4,7},{5,6},{6,5},{7,4},{8,11},{9,10},{10,... | collective-permute-start | bytes 12296 | tf_op jit(solution)/shard_map/ppermute | solution.py:276

commit v10 on v9

--- a/solution.py
+++ b/solution.py
@@ -118,9 +118,10 @@
 
 def select_kernel(comps, high, nsub, *args):
     heads, args = args[:nsub], args[nsub:]
-    nslab = len(args) // 2
-    sid_cols, mask, outs = args[:nslab], args[nslab], args[nslab + 1 :]
-    refs = mask.shape[0]
+    asks = len(args) // 2
+    sid_cols, outs = args[:asks], args[-asks:]
+    masks = args[asks:-asks]
+    refs = sid_cols[0].shape[0]
     ntmpl = heads[0].shape[0]
     width = outs[0].shape[1]
     per = width // LANES
@@ -151,14 +152,14 @@
         columns.append(jnp.concatenate(tiles, axis=0))
     stack = jnp.concatenate(columns, axis=1)
     owners = [jnp.where(row == c, owner, -1.0) for c in range(comps)]
-    for d, out in enumerate(outs):
-        wanted = sid_cols[d][:, :1].astype(jnp.float32)
+    for sid_col, out in zip(sid_cols, outs):
+        wanted = sid_col[:, :1].astype(jnp.float32)
         pick = [jnp.where(owners[c] == wanted, 1.0, 0.0).astype(jnp.bfloat16) for c in range(comps)]
         got = jnp.dot(jnp.concatenate(pick, axis=0), stack, preferred_element_type=jnp.float32)
-        if d:
+        if not masks:
             out[...] = got.astype(out.dtype)
         else:
-            live = mask[:, pl.ds(pl.multiple_of(here * width, LANES), width)]
+            live = masks[0][:, pl.ds(pl.multiple_of(here * width, LANES), width)]
             for c in range(comps):
                 out[c * refs : (c + 1) * refs, :] = got[c * refs : (c + 1) * refs] * live
 
@@ -327,7 +328,7 @@
     reach = round_up(taps + LANES - 1, LANES)
     depth = round_up(taps + SPAN - 1, LANES)
     groups = comps * js
-    first, second = groups // 5, groups // 5
+    first, second = max(groups // 15, 1), groups // 5
 
     def bank(size):
         return jax.ShapeDtypeStruct((size, depth, count * SPAN), jnp.bfloat16)
@@ -368,16 +369,18 @@
         name="middle",
     )(*asked, waves)
     heads, sid_far, bank_b = lax.optimization_barrier((heads, sid_far, bank_b))
-    sid_cols = [sid_col] + list(sid_far)
-    near, *fars = pl.pallas_call(
-        functools.partial(select_kernel, comps, high, nsub),
-        out_shape=[jax.ShapeDtypeStruct((chans, width), jnp.float32)]
-        + [jax.ShapeDtypeStruct((chans, width), records.dtype)] * (nslab - 1),
-        in_specs=[vmem] * (nsub + nslab + 1),
-        out_specs=[vmem] * nslab,
-        compiler_params=params(16),
-        name="select",
-    )(*heads, *sid_cols, mask)
+
+    def select(columns, masks, dtype):
+        return pl.pallas_call(
+            functools.partial(select_kernel, comps, high, nsub),
+            out_shape=[jax.ShapeDtypeStruct((chans, width), dtype)] * len(columns),
+            in_specs=[vmem] * (nsub + len(columns) + len(masks)),
+            out_specs=[vmem] * len(columns),
+            compiler_params=params(16),
+            name="select",
+        )(*heads, *columns, *masks)
+
+    fars = select(sid_far, [], records.dtype)
     fars = [crossed(far, d + 1) for d, far in enumerate(fars)]
     bank_c = pl.pallas_call(
         functools.partial(filters_kernel, first + second),
@@ -387,7 +390,8 @@
         compiler_params=params(16),
         name="filters",
     )(waves)
-    fars, bank_c = lax.optimization_barrier((fars, bank_c))
+    (near,) = select([sid_col], [mask], jnp.float32)
+    fars, bank_c, near = lax.optimization_barrier((fars, bank_c, near))
     chunks = time // LANES
     each = width // nsub
     tall = chunks + 8

time: 25.9 us -> 25.6 us (0.988)
  waiting for transfers between devices: 5.92 us -> 5.04 us
  starting transfers between devices: 10.2 us -> 10.5 us
  Pallas kernels: 8.89 us -> 9.15 us
    ppermute x3, waiting for transfers between devices: 4.9 us -> 4.09 us  [crossed(): lax.ppermute(value, ('slab', 'sub'), [(i, i ^ distance * nsub + nsub - 1)...]
    pallas_call x1, Pallas kernels: 2.18 us -> 2.68 us  [on_device(): pl.pallas_call(functools.partial(filters_kernel, first + second), out_sha...]
    pallas_call x1, Pallas kernels: 1.85 us -> 1.44 us  [on_device(): pl.pallas_call(tables_kernel, out_shape=[column_type, column_type, jax.Sh...]
    ppermute x3, starting transfers between devices: 2.66 us -> 2.98 us  [crossed(): lax.ppermute(value, ('slab', 'sub'), [(i, i ^ distance * nsub + nsub - 1)...]
    pallas_call x1 -> x2, Pallas kernels: 0.34 us -> 0.53 us  [select(): pl.pallas_call(functools.partial(select_kernel, comps, high, nsub), out_s...]
  transfers between devices with their start and end apart: 8 -> 8, of which waited for: 4 -> 5; matrix products, arithmetic and copies ran while one was open for 0% -> 0% of each run, Pallas kernels for 21% -> 22%
where the time goes in v10:
time: 25.6 us; the launch traced here: 25.4 us
  starting transfers between devices  10.5 us (41%)
  Pallas kernels  9.15 us (36%)
  waiting for transfers between devices  5.04 us (20%)
  other arithmetic  0.65 us (3%)
    ppermute x3, starting transfers between devices, on_device(): lax.ppermute(block, 'tmpl', [(i, (i + d) % ntmpl) for i in range(ntmpl)])  7.01 us
    ppermute x3, waiting for transfers between devices, crossed(): lax.ppermute(value, ('slab', 'sub'), [(i, i ^ distance * nsub + nsub - 1)...  4.09 us
    ppermute x3, starting transfers between devices, crossed(): lax.ppermute(value, ('slab', 'sub'), [(i, i ^ distance * nsub + nsub - 1)...  2.98 us
    pallas_call x1, Pallas kernels, on_device(): pl.pallas_call(functools.partial(filters_kernel, first + second), out_sha...  2.68 us
    pallas_call x1, Pallas kernels, on_device(): pl.pallas_call(functools.partial(correlate_kernel, nslab, nsub, taps, 3),...  2.28 us
    pallas_call x1, Pallas kernels, on_device(): pl.pallas_call(tables_kernel, out_shape=[column_type, column_type, jax.Sh...  1.44 us
    pallas_call x1, Pallas kernels, on_device(): pl.pallas_call(functools.partial(middle_kernel, first, nslab - 1), out_sh...  1.28 us
    pallas_call x1, Pallas kernels, on_device(): pl.pallas_call(pack_kernel, out_shape=jax.ShapeDtypeStruct((comps * high...  0.94 us
  transfers between devices with their start and end apart: 8, of which 5 were waited for; matrix products, arithmetic and copies ran while one was open for 0% of the time, Pallas kernels for 22%

profile of v10, /device:TPU:0, one launch (start us, length us, event | category | flops | bytes accessed | tf_op | source)
XLA Modules:
  0.0 25.4 jit_solution(18106226121170435725)
XLA Ops:
  0.0 0.9 %pack.1 = bf16[200,128]{1,0:T(8,128)(2,1)S(1)} custom-call(s32[32]{0:T(128)} %owner_slots.1, bf16[3,32,512]{2,1,0:T(8,128)(2,1)} %bitcast.19), custom_call_target="tpu_custom_call" | custom-call | tf_op jit(solution)/shard_map/pack/pallas_call | solution.py:302
  1.0 3.1 %collective-permute-start = (bf16[200,128]{1,0:T(8,128)(2,1)S(1)}, bf16[200,128]{1,0:T(8,128)(2,1)S(1)}, u32[]{:S(2)}, u32[]{:S(2)}) collective-permute-start(bf16[200,128]{1,0:T(8,128)(2,1)S(1)} %pack.1), channel_id=1, source_target_pairs={{0,4},{4,8},{8,12},{12,0},{1,5},{5,9},{9,13},{13,1},{2,6},{6,10},{... | collective-permute-start | bytes 153608 | tf_op jit(solution)/shard_map/ppermute | solution.py:323
  4.0 2.6 %collective-permute-start.1 = (bf16[200,128]{1,0:T(8,128)(2,1)S(1)}, bf16[200,128]{1,0:T(8,128)(2,1)S(1)}, u32[]{:S(2)}, u32[]{:S(2)}) collective-permute-start(bf16[200,128]{1,0:T(8,128)(2,1)S(1)} %pack.1), channel_id=1, source_target_pairs={{0,8},{4,12},{8,0},{12,4},{1,9},{5,13},{9,1},{13,5},{2,10},{6,14},... | collective-permute-start | bytes 153608 | tf_op jit(solution)/shard_map/ppermute | solution.py:323
  6.6 1.3 %collective-permute-start.2 = (bf16[200,128]{1,0:T(8,128)(2,1)S(1)}, bf16[200,128]{1,0:T(8,128)(2,1)S(1)}, u32[]{:S(2)}, u32[]{:S(2)}) collective-permute-start(bf16[200,128]{1,0:T(8,128)(2,1)S(1)} %pack.1), channel_id=1, source_target_pairs={{0,12},{4,0},{8,4},{12,8},{1,13},{5,1},{9,5},{13,9},{2,14},{6,2},{... | collective-permute-start | bytes 153608 | tf_op jit(solution)/shard_map/ppermute | solution.py:323
  8.0 0.1 collective-permute-start.3
  8.1 1.4 %tables.1 = (s32[40,128]{1,0:T(8,128)S(1)}, s32[40,128]{1,0:T(8,128)S(1)}, f32[40,1024]{1,0:T(8,128)S(1)}, bf16[256,512]{1,0:T(8,128)(2,1)S(1)}, f32[120,128]{1,...) custom-call(s32[4,10]{1,0:T(4,128)} %sids_in.1, s32[4,10]{1,0:T(4,128)} %offs_in.1, ...), custom_call_target="tpu_custom_call" | custom-call | tf_op jit(solution)/shard_map/tables/pallas_call | solution.py:337
  9.5 1.7 %collective-permute-done.3.args_0_ = s32[4,10]{1,0:T(4,128)S(1)} collective-permute-done((s32[4,10]{1,0:T(4,128)}, s32[4,10]{1,0:T(4,128)S(1)}, u32[]{:S(2)}, u32[]{:S(2)}) %collective-permute-start.3) | collective-permute-done | bytes 192 | tf_op jit(solution)/shard_map/ppermute | solution.py:277
  11.2 0.0 collective-permute-done
  11.2 0.0 collective-permute-done.1
  11.2 0.0 collective-permute-done.2
  11.2 0.2 collective-permute-start.4
  11.4 1.3 %middle.1 = (s32[40,128]{1,0:T(8,128)S(1)}, bf16[6,384,256]{2,1,0:T(8,128)(2,1)S(1)}) custom-call(s32[4,10]{1,0:T(4,128)S(1)} %collective-permute-done.3.args_0_, bf16[10,3,4,300]{3,2,1,0:T(4,128)(2,1)S(1)} %get-tuple-element.35.args_1_.waves), custom_call_target="tpu_custom_call" | custom-call | tf_op jit(solution)/shard_map/middle/pallas_call | solution.py:363
  12.7 0.1 collective-permute-done.4.args_1_
  12.8 0.3 %select.2 = bf16[120,512]{1,0:T(8,128)(2,1)S(1)} custom-call(bf16[4,200,128]{2,1,0:T(8,128)(2,1)S(1)} %pad_maximum_fusion.args_0_, bf16[4,200,128]{2,1,0:T(8,128)(2,1)S(1)} %collective-permute-done.4.args_1_, s32[40,128]{1,0:T(8,128)S(1)} %get-tuple-element.40.args_2_), custom_call_target="tpu_custom_call" | custom-call | tf_op jit(solution)/shard_map/select/pallas_call | solution.py:374
  13.0 1.5 %collective-permute-start.5 = (bf16[120,512]{1,0:T(8,128)(2,1)S(1)}, bf16[120,512]{1,0:T(8,128)(2,1)S(1)}, u32[]{:S(2)}, u32[]{:S(2)}) collective-permute-start(bf16[120,512]{1,0:T(8,128)(2,1)S(1)} %select.2), channel_id=1, source_target_pairs={{0,3},{1,2},{2,1},{3,0},{4,7},{5,6},{6,5},{7,4},{8,11},{9,10},{10,... | collective-permute-start | bytes 368648 | tf_op jit(solution)/shard_map/ppermute | solution.py:277
  14.5 2.7 %filters.1.args_4_ = bf16[22,384,256]{2,1,0:T(8,128)(2,1)S(1)} custom-call(bf16[10,3,4,300]{3,2,1,0:T(4,128)(2,1)S(1)} %get-tuple-element.35.args_1_.waves), custom_call_target="tpu_custom_call" | custom-call | tf_op jit(solution)/shard_map/filters/pallas_call | solution.py:385
  17.2 0.3 %select.3.args_0_ = f32[120,512]{1,0:T(8,128)S(1)} custom-call(bf16[4,200,128]{2,1,0:T(8,128)(2,1)S(1)} %pad_maximum_fusion.args_0_, bf16[4,200,128]{2,1,0:T(8,128)(2,1)S(1)} %collective-permute-done.4.args_1_, s32[40,128]{1,0:T(8,128)S(1)} %get-tuple-element.41.args_2_, f32[40,1024]{1,0:T(8,128)S(1)} %get-tuple-element.42.args_3_.args_6_), custom_call_target="tpu_custom_call" | custom-call | tf_op jit(solution)/shard_map/select/pallas_call | solution.py:374
  17.5 0.8 %collective-permute-done.5.args_1_ = bf16[120,512]{1,0:T(8,128)(2,1)S(1)} collective-permute-done((bf16[120,512]{1,0:T(8,128)(2,1)S(1)}, bf16[120,512]{1,0:T(8,128)(2,1)S(1)}, u32[]{:S(2)}, u32[]{:S(2)}) %collective-permute-start.5) | collective-permute-done | bytes 122912 | tf_op jit(solution)/shard_map/ppermute | solution.py:277
  18.3 2.3 %correlate.1 = (f32[2,4,256]{2,1,0:T(4,128)S(1)}, f32[1,2,4,256]{3,2,1,0:T(4,128)S(1)}) custom-call(f32[120,512]{1,0:T(8,128)S(1)} %select.3.args_0_, bf16[120,512]{1,0:T(8,128)(2,1)S(1)} %collective-permute-done.5.args_1_, bf16[2,384,256]{2,1,0:T(8,128)(2,1)S(1)} %get-tuple-element.45.args_2_, bf16[6,384,256]{2,1,0:T(8,128)(2,1)S(1)} %get-tuple-element.46.args_3_, ...), custom_call_target="tpu_custom_call" | custom-call | tf_op jit(solution)/shard_map/correlate/pallas_call | solution.py:398
  20.5 0.4 %collective-permute-start.6 = (f32[2,4,256]{2,1,0:T(4,128)S(1)}, f32[2,4,256]{2,1,0:T(4,128)S(1)}, u32[]{:S(2)}, u32[]{:S(2)}) collective-permute-start(f32[2,4,256]{2,1,0:T(4,128)S(1)} %bitcast.18), channel_id=1, source_target_pairs={{0,1},{1,0},{2,3},{3,2},{4,5},{5,4},{6,7},{7,6},{8,9},{9,8},{10,11... | collective-permute-start | bytes 24584 | tf_op jit(solution)/shard_map/ppermute | solution.py:271
  20.9 0.9 %collective-permute-done.6 = f32[2,4,256]{2,1,0:T(4,128)S(1)} collective-permute-done((f32[2,4,256]{2,1,0:T(4,128)S(1)}, f32[2,4,256]{2,1,0:T(4,128)S(1)}, u32[]{:S(2)}, u32[]{:S(2)}) %collective-permute-start.6) | collective-permute-done | bytes 8224 | tf_op jit(solution)/shard_map/ppermute | solution.py:271
  21.8 1.4 %collective-permute-start.7 = (f32[4,256]{1,0:T(4,128)S(1)}, f32[4,256]{1,0:T(4,128)S(1)}, u32[]{:S(2)}, u32[]{:S(2)}) collective-permute-start(f32[4,256]{1,0:T(4,128)S(1)} %slice_bitcast_fusion.1), channel_id=1, source_target_pairs={{0,3},{1,2},{2,1},{3,0},{4,7},{5,6},{6,5},{7,4},{8,11},{9,10},{10,... | collective-permute-start | bytes 12296 | tf_op jit(solution)/shard_map/ppermute | solution.py:277
  23.2 1.7 %collective-permute-done.7 = f32[4,256]{1,0:T(4,128)S(1)} collective-permute-done((f32[4,256]{1,0:T(4,128)S(1)}, f32[4,256]{1,0:T(4,128)S(1)}, u32[]{:S(2)}, u32[]{:S(2)}) %collective-permute-start.7) | collective-permute-done | bytes 4128 | tf_op jit(solution)/shard_map/ppermute | solution.py:277
  24.8 0.6 %pad_maximum_fusion.1 = f32[8,256]{1,0:T(8,128)} fusion(f32[4,256]{1,0:T(4,128)S(1)} %get-tuple-element.54, f32[4,256]{1,0:T(4,128)S(1)} %get-tuple-element.53), kind=kLoop, calls=%fused_computation.1 | loop fusion | flops 2048 | bytes 16384 | tf_op jit(solution)/shard_map/concatenate | solution.py:427
  (4 shorter events, 0.0 us)
Async XLA Ops:
  1.0 10.2 %collective-permute-start = (bf16[200,128]{1,0:T(8,128)(2,1)S(1)}, bf16[200,128]{1,0:T(8,128)(2,1)S(1)}, u32[]{:S(2)}, u32[]{:S(2)}) collective-permute-start(bf16[200,128]{1,0:T(8,128)(2,1)S(1)} %pack.1), channel_id=1, source_target_pairs={{0,4},{4,8},{8,12},{12,0},{1,5},{5,9},{9,13},{13,1},{2,6},{6,10},{... | collective-permute-start | bytes 153608 | tf_op jit(solution)/shard_map/ppermute | solution.py:323
  4.0 7.2 %collective-permute-start.1 = (bf16[200,128]{1,0:T(8,128)(2,1)S(1)}, bf16[200,128]{1,0:T(8,128)(2,1)S(1)}, u32[]{:S(2)}, u32[]{:S(2)}) collective-permute-start(bf16[200,128]{1,0:T(8,128)(2,1)S(1)} %pack.1), channel_id=1, source_target_pairs={{0,8},{4,12},{8,0},{12,4},{1,9},{5,13},{9,1},{13,5},{2,10},{6,14},... | collective-permute-start | bytes 153608 | tf_op jit(solution)/shard_map/ppermute | solution.py:323
  6.6 4.6 %collective-permute-start.2 = (bf16[200,128]{1,0:T(8,128)(2,1)S(1)}, bf16[200,128]{1,0:T(8,128)(2,1)S(1)}, u32[]{:S(2)}, u32[]{:S(2)}) collective-permute-start(bf16[200,128]{1,0:T(8,128)(2,1)S(1)} %pack.1), channel_id=1, source_target_pairs={{0,12},{4,0},{8,4},{12,8},{1,13},{5,1},{9,5},{13,9},{2,14},{6,2},{... | collective-permute-start | bytes 153608 | tf_op jit(solution)/shard_map/ppermute | solution.py:323
  8.0 3.2 %collective-permute-start.3 = (s32[4,10]{1,0:T(4,128)}, s32[4,10]{1,0:T(4,128)S(1)}, u32[]{:S(2)}, u32[]{:S(2)}) collective-permute-start(s32[4,10]{1,0:T(4,128)} %sids_in.1), channel_id=1, source_target_pairs={{0,3},{1,2},{2,1},{3,0},{4,7},{5,6},{6,5},{7,4},{8,11},{9,10},{10,... | collective-permute-start | bytes 488 | tf_op jit(solution)/shard_map/ppermute | solution.py:277
  11.2 1.5 %collective-permute-start.4 = (bf16[4,200,128]{2,1,0:T(8,128)(2,1)S(1)}, bf16[4,200,128]{2,1,0:T(8,128)(2,1)S(1)}, u32[]{:S(2)}, u32[]{:S(2)}) collective-permute-start(bf16[4,200,128]{2,1,0:T(8,128)(2,1)S(1)} %pad_maximum_fusion.args_0_), channel_id=1, source_target_pairs={{0,1},{1,0},{2,3},{3,2},{4,5},{5,4},{6,7},{7,6},{8,9},{9,8},{10,11... | collective-permute-start | bytes 614408 | tf_op jit(solution)/shard_map/ppermute | solution.py:271
  13.0 5.2 %collective-permute-start.5 = (bf16[120,512]{1,0:T(8,128)(2,1)S(1)}, bf16[120,512]{1,0:T(8,128)(2,1)S(1)}, u32[]{:S(2)}, u32[]{:S(2)}) collective-permute-start(bf16[120,512]{1,0:T(8,128)(2,1)S(1)} %select.2), channel_id=1, source_target_pairs={{0,3},{1,2},{2,1},{3,0},{4,7},{5,6},{6,5},{7,4},{8,11},{9,10},{10,... | collective-permute-start | bytes 368648 | tf_op jit(solution)/shard_map/ppermute | solution.py:277
  20.5 1.2 %collective-permute-start.6 = (f32[2,4,256]{2,1,0:T(4,128)S(1)}, f32[2,4,256]{2,1,0:T(4,128)S(1)}, u32[]{:S(2)}, u32[]{:S(2)}) collective-permute-start(f32[2,4,256]{2,1,0:T(4,128)S(1)} %bitcast.18), channel_id=1, source_target_pairs={{0,1},{1,0},{2,3},{3,2},{4,5},{5,4},{6,7},{7,6},{8,9},{9,8},{10,11... | collective-permute-start | bytes 24584 | tf_op jit(solution)/shard_map/ppermute | solution.py:271
  21.8 3.0 %collective-permute-start.7 = (f32[4,256]{1,0:T(4,128)S(1)}, f32[4,256]{1,0:T(4,128)S(1)}, u32[]{:S(2)}, u32[]{:S(2)}) collective-permute-start(f32[4,256]{1,0:T(4,128)S(1)} %slice_bitcast_fusion.1), channel_id=1, source_target_pairs={{0,3},{1,2},{2,1},{3,0},{4,7},{5,6},{6,5},{7,4},{8,11},{9,10},{10,... | collective-permute-start | bytes 12296 | tf_op jit(solution)/shard_map/ppermute | solution.py:277

commit v11 on v10

--- a/solution.py
+++ b/solution.py
@@ -116,11 +116,9 @@
     build_filters(begin, waves, filters)
 
 
-def select_kernel(comps, high, nsub, *args):
+def select_kernel(comps, high, nsub, asks, nmask, *args):
     heads, args = args[:nsub], args[nsub:]
-    asks = len(args) // 2
-    sid_cols, outs = args[:asks], args[-asks:]
-    masks = args[asks:-asks]
+    sid_cols, masks, outs = args[:asks], args[asks : asks + nmask], args[asks + nmask :]
     refs = sid_cols[0].shape[0]
     ntmpl = heads[0].shape[0]
     width = outs[0].shape[1]
@@ -152,40 +150,49 @@
         columns.append(jnp.concatenate(tiles, axis=0))
     stack = jnp.concatenate(columns, axis=1)
     owners = [jnp.where(row == c, owner, -1.0) for c in range(comps)]
-    for sid_col, out in zip(sid_cols, outs):
+    for d, (sid_col, out) in enumerate(zip(sid_cols, outs)):
         wanted = sid_col[:, :1].astype(jnp.float32)
         pick = [jnp.where(owners[c] == wanted, 1.0, 0.0).astype(jnp.bfloat16) for c in range(comps)]
         got = jnp.dot(jnp.concatenate(pick, axis=0), stack, preferred_element_type=jnp.float32)
         if not masks:
-            out[...] = got.astype(out.dtype)
+            split = out.shape[0]
+            out[...] = got[:split].astype(out.dtype)
+            outs[asks + d][...] = got[split:].astype(out.dtype)
         else:
             live = masks[0][:, pl.ds(pl.multiple_of(here * width, LANES), width)]
             for c in range(comps):
                 out[c * refs : (c + 1) * refs, :] = got[c * refs : (c + 1) * refs] * live
 
 
-def correlate_kernel(nslab, nsub, taps, nbank, *args):
+def correlate_kernel(nslab, nsub, taps, nbank, start, last, *args):
     near, fars, args = args[0], args[1:nslab], args[nslab:]
     banks, args = args[:nbank], args[nbank:]
-    off_col, mask, band, scale, keep, send, segs, low, high, norm, total = args
+    if start:
+        before, args = args[0], args[1:]
+    off_col, mask, band, scale, args = *args[:4], args[4:]
+    if last:
+        keep, send, segs, low, high, norm, total = args
+    else:
+        total, segs, low, high, norm = args
     refs, time = mask.shape
-    chans, width = near.shape
+    chans, width = fars[0].shape
     comps = chans // refs
     chunks = time // LANES
-    count = keep.shape[1]
+    count = total.shape[0]
+    js = refs // count
     here, core = lax.axis_index("slab"), lax.axis_index("sub")
     for d in range(nslab):
         spot = pl.ds(pl.multiple_of(lax.bitwise_xor(here, d) * width, LANES), width)
         if d == 0:
-            segs[:, spot] = near[...]
+            segs[:, spot] = near[start * refs : start * refs + chans, :]
         else:
             live = mask[:, spot]
             for c in range(comps):
                 got = fars[d - 1][c * refs : (c + 1) * refs, :].astype(jnp.float32)
                 segs[c * refs : (c + 1) * refs, spot] = got * live
-    span = banks[0].shape[1] // LANES
     lane = lax.broadcasted_iota(jnp.int32, (8, LANES), 1)
     zero = jnp.zeros((8, LANES), jnp.float32)
+    span = banks[0].shape[1] // LANES
     for i in range(chans // 8):
         ref_row = (i * 8) % refs
         off = off_col[ref_row : ref_row + 8, :]
@@ -224,12 +231,13 @@
         window = sums[r][:, :LANES]
         for p in range(1, min(reach, chunks - r)):
             window = window + sums[r + p][:, p * LANES : (p + 1) * LANES]
-        factor = scale[...] * lax.rsqrt(window / taps + 1e-06)
+        factor = scale[start * refs : start * refs + chans, :] * lax.rsqrt(window / taps + 1e-06)
         for i in range(chans // 8):
             norm[pl.ds(i * 8, 8), r, :] = factor[i * 8 : i * 8 + 8]
-    accs = [jnp.zeros((chunks, LANES), jnp.float32) for _ in range(count)]
+    accs = [before[k] if start else jnp.zeros((chunks, LANES), jnp.float32) for k in range(count)]
     side = lax.broadcasted_iota(jnp.int32, (chunks, LANES), 1) < SPAN
     weights = [(bank, i) for bank in banks for i in range(bank.shape[0])]
+    weights = weights[start * js : (start + comps) * js]
     def operand(g):
         rows = []
         for ch in range(g * count, (g + 1) * count):
@@ -255,6 +263,8 @@
         gather_sums(g, jnp.dot(operand(g), bank[i], preferred_element_type=jnp.float32))
     for k in range(count):
         total[k] = accs[k]
+    if not last:
+        return
     each = chunks // (nslab * nsub)
     for d in range(nslab):
         for e in range(each):
@@ -370,18 +380,21 @@
     )(*asked, waves)
     heads, sid_far, bank_b = lax.optimization_barrier((heads, sid_far, bank_b))
 
-    def select(columns, masks, dtype):
+    def select(columns, masks, heights, dtype):
+        sizes = [size for size in heights for _ in columns]
         return pl.pallas_call(
-            functools.partial(select_kernel, comps, high, nsub),
-            out_shape=[jax.ShapeDtypeStruct((chans, width), dtype)] * len(columns),
+            functools.partial(select_kernel, comps, high, nsub, len(columns), len(masks)),
+            out_shape=[jax.ShapeDtypeStruct((size, width), dtype) for size in sizes],
             in_specs=[vmem] * (nsub + len(columns) + len(masks)),
-            out_specs=[vmem] * len(columns),
+            out_specs=[vmem] * len(sizes),
             compiler_params=params(16),
             name="select",
         )(*heads, *columns, *masks)
 
-    fars = select(sid_far, [], records.dtype)
-    fars = [crossed(far, d + 1) for d, far in enumerate(fars)]
+    ahead = comps - 1
+    fars = select(sid_far, [], [ahead * refs, chans - ahead * refs], records.dtype)
+    early = [crossed(far, d + 1) for d, far in enumerate(fars[: nslab - 1])]
+    late = [crossed(far, d + 1) for d, far in enumerate(fars[nslab - 1 :])]
     bank_c = pl.pallas_call(
         functools.partial(filters_kernel, first + second),
         out_shape=bank(groups - first - second),
@@ -390,29 +403,41 @@
         compiler_params=params(16),
         name="filters",
     )(waves)
-    (near,) = select([sid_col], [mask], jnp.float32)
-    fars, bank_c, near = lax.optimization_barrier((fars, bank_c, near))
+    (near,) = select([sid_col], [mask], [chans], jnp.float32)
+    early, bank_c, near = lax.optimization_barrier((early, bank_c, near))
     chunks = time // LANES
     each = width // nsub
     tall = chunks + 8
-    keep, send = pl.pallas_call(
-        functools.partial(correlate_kernel, nslab, nsub, taps, 3),
-        out_shape=[
-            jax.ShapeDtypeStruct((nslab, count, each), jnp.float32),
-            jax.ShapeDtypeStruct((nsub - 1, nslab, count, each), jnp.float32),
-        ],
-        in_specs=[vmem] * (nslab + 7),
-        out_specs=[vmem] * 2,
-        scratch_shapes=[
-            pltpu.VMEM((chans, time), jnp.float32),
-            pltpu.VMEM((chans, tall, LANES), jnp.float32),
-            pltpu.VMEM((chans, tall, LANES), jnp.float32),
-            pltpu.VMEM((chans, chunks, LANES), jnp.float32),
-            pltpu.VMEM((count, chunks, LANES), jnp.float32),
-        ],
-        compiler_params=params(32),
-        name="correlate",
-    )(near, *fars, bank_a, bank_b, bank_c, off_col, mask, band, scale)
+    stack_type = jax.ShapeDtypeStruct((count, chunks, LANES), jnp.float32)
+
+    def correlate(start, far, before, last):
+        size = far[0].shape[0]
+        scratch = [
+            pltpu.VMEM((size, time), jnp.float32),
+            pltpu.VMEM((size, tall, LANES), jnp.float32),
+            pltpu.VMEM((size, tall, LANES), jnp.float32),
+            pltpu.VMEM((size, chunks, LANES), jnp.float32),
+        ]
+        shapes = [stack_type]
+        if last:
+            scratch.append(pltpu.VMEM(stack_type.shape, jnp.float32))
+            shapes = [
+                jax.ShapeDtypeStruct((nslab, count, each), jnp.float32),
+                jax.ShapeDtypeStruct((nsub - 1, nslab, count, each), jnp.float32),
+            ]
+        operands = [near, *far, bank_a, bank_b, bank_c, *before, off_col, mask, band, scale]
+        return pl.pallas_call(
+            functools.partial(correlate_kernel, nslab, nsub, taps, 3, start, last),
+            out_shape=shapes,
+            in_specs=[vmem] * len(operands),
+            out_specs=[vmem] * len(shapes),
+            scratch_shapes=scratch,
+            compiler_params=params(24),
+            name="correlate",
+        )(*operands)
+
+    before = correlate(0, early, [], False)
+    keep, send = correlate(ahead, late, before, True)
     for m in range(1, nsub):
         keep = keep + swapped(send[m - 1], "sub", m)
     lines = [keep[0]]

time: 25.6 us -> 25.5 us (level)
  waiting for transfers between devices: 5.04 us -> 4.09 us
  starting transfers between devices: 10.5 us -> 11.2 us
    ppermute x3 -> x4, waiting for transfers between devices: 4.09 us -> 3.2 us  [crossed(): lax.ppermute(value, ('slab', 'sub'), [(i, i ^ distance * nsub + nsub - 1)...]
    ppermute x3 -> x4, starting transfers between devices: 2.98 us -> 3.43 us  [crossed(): lax.ppermute(value, ('slab', 'sub'), [(i, i ^ distance * nsub + nsub - 1)...]
    pallas_call x3 -> x4, Pallas kernels: 2.81 us -> 3.02 us  [the longest x2 2.49 us: correlate(): pl.pallas_call(functools.partial(correlate_kernel, nslab, nsub, taps, 3,...]
  transfers between devices with their start and end apart: 8 -> 9, of which waited for: 5 -> 4; matrix products, arithmetic and copies ran while one was open for 0% -> 0% of each run, Pallas kernels for 22% -> 29%
where the time goes in v11:
time: 25.5 us; the launch traced here: 25.3 us
  starting transfers between devices  11.2 us (44%)
  Pallas kernels  9.35 us (37%)
  waiting for transfers between devices  4.09 us (16%)
  other arithmetic  0.65 us (3%)
    ppermute x3, starting transfers between devices, on_device(): lax.ppermute(block, 'tmpl', [(i, (i + d) % ntmpl) for i in range(ntmpl)])  7.01 us
    ppermute x4, starting transfers between devices, crossed(): lax.ppermute(value, ('slab', 'sub'), [(i, i ^ distance * nsub + nsub - 1)...  3.43 us
    ppermute x4, waiting for transfers between devices, crossed(): lax.ppermute(value, ('slab', 'sub'), [(i, i ^ distance * nsub + nsub - 1)...  3.2 us
    pallas_call x1, Pallas kernels, on_device(): pl.pallas_call(functools.partial(filters_kernel, first + second), out_sha...  2.68 us
    pallas_call x2, Pallas kernels, correlate(): pl.pallas_call(functools.partial(correlate_kernel, nslab, nsub, taps, 3,...  2.49 us
    pallas_call x1, Pallas kernels, on_device(): pl.pallas_call(tables_kernel, out_shape=[column_type, column_type, jax.Sh...  1.43 us
    pallas_call x1, Pallas kernels, on_device(): pl.pallas_call(functools.partial(middle_kernel, first, nslab - 1), out_sh...  1.28 us
    pallas_call x1, Pallas kernels, on_device(): pl.pallas_call(pack_kernel, out_shape=jax.ShapeDtypeStruct((comps * high...  0.94 us
  transfers between devices with their start and end apart: 9, of which 4 were waited for; matrix products, arithmetic and copies ran while one was open for 0% of the time, Pallas kernels for 29%

profile of v11, /device:TPU:0, one launch (start us, length us, event | category | flops | bytes accessed | tf_op | source)
XLA Modules:
  0.0 25.3 jit_solution(12170125297783049840)
XLA Ops:
  0.0 0.9 %pack.1 = bf16[200,128]{1,0:T(8,128)(2,1)S(1)} custom-call(s32[32]{0:T(128)} %owner_slots.1, bf16[3,32,512]{2,1,0:T(8,128)(2,1)} %bitcast.19), custom_call_target="tpu_custom_call" | custom-call | tf_op jit(solution)/shard_map/pack/pallas_call | solution.py:312
  1.0 3.1 %collective-permute-start = (bf16[200,128]{1,0:T(8,128)(2,1)S(1)}, bf16[200,128]{1,0:T(8,128)(2,1)S(1)}, u32[]{:S(2)}, u32[]{:S(2)}) collective-permute-start(bf16[200,128]{1,0:T(8,128)(2,1)S(1)} %pack.1), channel_id=1, source_target_pairs={{0,4},{4,8},{8,12},{12,0},{1,5},{5,9},{9,13},{13,1},{2,6},{6,10},{... | collective-permute-start | bytes 153608 | tf_op jit(solution)/shard_map/ppermute | solution.py:333
  4.0 2.6 %collective-permute-start.1 = (bf16[200,128]{1,0:T(8,128)(2,1)S(1)}, bf16[200,128]{1,0:T(8,128)(2,1)S(1)}, u32[]{:S(2)}, u32[]{:S(2)}) collective-permute-start(bf16[200,128]{1,0:T(8,128)(2,1)S(1)} %pack.1), channel_id=1, source_target_pairs={{0,8},{4,12},{8,0},{12,4},{1,9},{5,13},{9,1},{13,5},{2,10},{6,14},... | collective-permute-start | bytes 153608 | tf_op jit(solution)/shard_map/ppermute | solution.py:333
  6.6 1.3 %collective-permute-start.2 = (bf16[200,128]{1,0:T(8,128)(2,1)S(1)}, bf16[200,128]{1,0:T(8,128)(2,1)S(1)}, u32[]{:S(2)}, u32[]{:S(2)}) collective-permute-start(bf16[200,128]{1,0:T(8,128)(2,1)S(1)} %pack.1), channel_id=1, source_target_pairs={{0,12},{4,0},{8,4},{12,8},{1,13},{5,1},{9,5},{13,9},{2,14},{6,2},{... | collective-permute-start | bytes 153608 | tf_op jit(solution)/shard_map/ppermute | solution.py:333
  8.0 0.1 collective-permute-start.3
  8.1 1.4 %tables.1 = (s32[40,128]{1,0:T(8,128)S(1)}, s32[40,128]{1,0:T(8,128)S(1)}, f32[40,1024]{1,0:T(8,128)S(1)}, bf16[256,512]{1,0:T(8,128)(2,1)S(1)}, f32[120,128]{1,...) custom-call(s32[4,10]{1,0:T(4,128)} %sids_in.1, s32[4,10]{1,0:T(4,128)} %offs_in.1, ...), custom_call_target="tpu_custom_call" | custom-call | tf_op jit(solution)/shard_map/tables/pallas_call | solution.py:347
  9.5 1.7 %collective-permute-done.3.args_0_ = s32[4,10]{1,0:T(4,128)S(1)} collective-permute-done((s32[4,10]{1,0:T(4,128)}, s32[4,10]{1,0:T(4,128)S(1)}, u32[]{:S(2)}, u32[]{:S(2)}) %collective-permute-start.3) | collective-permute-done | bytes 192 | tf_op jit(solution)/shard_map/ppermute | solution.py:287
  11.2 0.0 collective-permute-done
  11.2 0.0 collective-permute-done.1
  11.2 0.0 collective-permute-done.2
  11.2 0.2 collective-permute-start.4
  11.4 1.3 %middle.1 = (s32[40,128]{1,0:T(8,128)S(1)}, bf16[6,384,256]{2,1,0:T(8,128)(2,1)S(1)}) custom-call(s32[4,10]{1,0:T(4,128)S(1)} %collective-permute-done.3.args_0_, bf16[10,3,4,300]{3,2,1,0:T(4,128)(2,1)S(1)} %get-tuple-element.37.args_1_.waves), custom_call_target="tpu_custom_call" | custom-call | tf_op jit(solution)/shard_map/middle/pallas_call | solution.py:373
  12.7 0.1 collective-permute-done.4.args_1_
  12.8 0.3 %select.2 = (bf16[80,512]{1,0:T(8,128)(2,1)S(1)}, bf16[40,512]{1,0:T(8,128)(2,1)S(1)}) custom-call(bf16[4,200,128]{2,1,0:T(8,128)(2,1)S(1)} %pad_maximum_fusion.args_0_, bf16[4,200,128]{2,1,0:T(8,128)(2,1)S(1)} %collective-permute-done.4.args_1_, s32[40,128]{1,0:T(8,128)S(1)} %get-tuple-element.42.args_2_), custom_call_target="tpu_custom_call" | custom-call | tf_op jit(solution)/shard_map/select/pallas_call | solution.py:385
  13.0 1.5 %collective-permute-start.5 = (bf16[80,512]{1,0:T(8,128)(2,1)S(1)}, bf16[80,512]{1,0:T(8,128)(2,1)S(1)}, u32[]{:S(2)}, u32[]{:S(2)}) collective-permute-start(bf16[80,512]{1,0:T(8,128)(2,1)S(1)} %get-tuple-element.43), channel_id=1, source_target_pairs={{0,3},{1,2},{2,1},{3,0},{4,7},{5,6},{6,5},{7,4},{8,11},{9,10},{10,... | collective-permute-start | bytes 245768 | tf_op jit(solution)/shard_map/ppermute | solution.py:287
  14.5 0.3 %collective-permute-start.6 = (bf16[40,512]{1,0:T(8,128)(2,1)S(1)}, bf16[40,512]{1,0:T(8,128)(2,1)S(1)}, u32[]{:S(2)}, u32[]{:S(2)}) collective-permute-start(bf16[40,512]{1,0:T(8,128)(2,1)S(1)} %get-tuple-element.47), channel_id=1, source_target_pairs={{0,3},{1,2},{2,1},{3,0},{4,7},{5,6},{6,5},{7,4},{8,11},{9,10},{10,... | collective-permute-start | bytes 122888 | tf_op jit(solution)/shard_map/ppermute | solution.py:287
  14.8 2.7 %filters.1.args_4_ = bf16[22,384,256]{2,1,0:T(8,128)(2,1)S(1)} custom-call(bf16[10,3,4,300]{3,2,1,0:T(4,128)(2,1)S(1)} %get-tuple-element.37.args_1_.waves), custom_call_target="tpu_custom_call" | custom-call | tf_op jit(solution)/shard_map/filters/pallas_call | solution.py:398
  17.5 0.3 %select.3.args_0_ = f32[120,512]{1,0:T(8,128)S(1)} custom-call(bf16[4,200,128]{2,1,0:T(8,128)(2,1)S(1)} %pad_maximum_fusion.args_0_, bf16[4,200,128]{2,1,0:T(8,128)(2,1)S(1)} %collective-permute-done.4.args_1_, s32[40,128]{1,0:T(8,128)S(1)} %get-tuple-element.44.args_2_, f32[40,1024]{1,0:T(8,128)S(1)} %get-tuple-element.45.args_3_.args_6_.args_7_), custom_call_target="tpu_custom_call" | custom-call | tf_op jit(solution)/shard_map/select/pallas_call | solution.py:385
  17.8 0.0 collective-permute-done.5.args_1_
  17.8 1.6 %correlate.2.args_5_ = f32[4,8,128]{2,1,0:T(8,128)S(1)} custom-call(f32[120,512]{1,0:T(8,128)S(1)} %select.3.args_0_, bf16[80,512]{1,0:T(8,128)(2,1)S(1)} %collective-permute-done.5.args_1_, bf16[2,384,256]{2,1,0:T(8,128)(2,1)S(1)} %get-tuple-element.48.args_2_, bf16[6,384,256]{2,1,0:T(8,128)(2,1)S(1)} %get-tuple-element.49.args_3_, ...), custom_call_target="tpu_custom_call" | custom-call | tf_op jit(solution)/shard_map/correlate/pallas_call | solution.py:429
  19.4 0.0 collective-permute-done.6.args_1_
  19.4 0.9 %correlate.3 = (f32[2,4,256]{2,1,0:T(4,128)S(1)}, f32[1,2,4,256]{3,2,1,0:T(4,128)S(1)}) custom-call(f32[120,512]{1,0:T(8,128)S(1)} %select.3.args_0_, bf16[40,512]{1,0:T(8,128)(2,1)S(1)} %collective-permute-done.6.args_1_, bf16[2,384,256]{2,1,0:T(8,128)(2,1)S(1)} %get-tuple-element.48.args_2_, bf16[6,384,256]{2,1,0:T(8,128)(2,1)S(1)} %get-tuple-element.49.args_3_, ...), custom_call_target="tpu_custom_call" | custom-call | tf_op jit(solution)/shard_map/correlate/pallas_call | solution.py:429
  20.3 0.5 %collective-permute-start.7 = (f32[2,4,256]{2,1,0:T(4,128)S(1)}, f32[2,4,256]{2,1,0:T(4,128)S(1)}, u32[]{:S(2)}, u32[]{:S(2)}) collective-permute-start(f32[2,4,256]{2,1,0:T(4,128)S(1)} %bitcast.18), channel_id=1, source_target_pairs={{0,1},{1,0},{2,3},{3,2},{4,5},{5,4},{6,7},{7,6},{8,9},{9,8},{10,11... | collective-permute-start | bytes 24584 | tf_op jit(solution)/shard_map/ppermute | solution.py:281
  20.9 0.8 %collective-permute-done.7 = f32[2,4,256]{2,1,0:T(4,128)S(1)} collective-permute-done((f32[2,4,256]{2,1,0:T(4,128)S(1)}, f32[2,4,256]{2,1,0:T(4,128)S(1)}, u32[]{:S(2)}, u32[]{:S(2)}) %collective-permute-start.7) | collective-permute-done | bytes 8224 | tf_op jit(solution)/shard_map/ppermute | solution.py:281
  21.7 1.5 %collective-permute-start.8 = (f32[4,256]{1,0:T(4,128)S(1)}, f32[4,256]{1,0:T(4,128)S(1)}, u32[]{:S(2)}, u32[]{:S(2)}) collective-permute-start(f32[4,256]{1,0:T(4,128)S(1)} %slice_bitcast_fusion.1), channel_id=1, source_target_pairs={{0,3},{1,2},{2,1},{3,0},{4,7},{5,6},{6,5},{7,4},{8,11},{9,10},{10,... | collective-permute-start | bytes 12296 | tf_op jit(solution)/shard_map/ppermute | solution.py:287
  23.2 1.5 %collective-permute-done.8 = f32[4,256]{1,0:T(4,128)S(1)} collective-permute-done((f32[4,256]{1,0:T(4,128)S(1)}, f32[4,256]{1,0:T(4,128)S(1)}, u32[]{:S(2)}, u32[]{:S(2)}) %collective-permute-start.8) | collective-permute-done | bytes 4128 | tf_op jit(solution)/shard_map/ppermute | solution.py:287
  24.7 0.6 %pad_maximum_fusion.1 = f32[8,256]{1,0:T(8,128)} fusion(f32[4,256]{1,0:T(4,128)S(1)} %get-tuple-element.58, f32[4,256]{1,0:T(4,128)S(1)} %get-tuple-element.57), kind=kLoop, calls=%fused_computation.1 | loop fusion | flops 2048 | bytes 16384 | tf_op jit(solution)/shard_map/concatenate | solution.py:452
  (4 shorter events, 0.0 us)
Async XLA Ops:
  1.0 10.2 %collective-permute-start = (bf16[200,128]{1,0:T(8,128)(2,1)S(1)}, bf16[200,128]{1,0:T(8,128)(2,1)S(1)}, u32[]{:S(2)}, u32[]{:S(2)}) collective-permute-start(bf16[200,128]{1,0:T(8,128)(2,1)S(1)} %pack.1), channel_id=1, source_target_pairs={{0,4},{4,8},{8,12},{12,0},{1,5},{5,9},{9,13},{13,1},{2,6},{6,10},{... | collective-permute-start | bytes 153608 | tf_op jit(solution)/shard_map/ppermute | solution.py:333
  4.0 7.2 %collective-permute-start.1 = (bf16[200,128]{1,0:T(8,128)(2,1)S(1)}, bf16[200,128]{1,0:T(8,128)(2,1)S(1)}, u32[]{:S(2)}, u32[]{:S(2)}) collective-permute-start(bf16[200,128]{1,0:T(8,128)(2,1)S(1)} %pack.1), channel_id=1, source_target_pairs={{0,8},{4,12},{8,0},{12,4},{1,9},{5,13},{9,1},{13,5},{2,10},{6,14},... | collective-permute-start | bytes 153608 | tf_op jit(solution)/shard_map/ppermute | solution.py:333
  6.6 4.6 %collective-permute-start.2 = (bf16[200,128]{1,0:T(8,128)(2,1)S(1)}, bf16[200,128]{1,0:T(8,128)(2,1)S(1)}, u32[]{:S(2)}, u32[]{:S(2)}) collective-permute-start(bf16[200,128]{1,0:T(8,128)(2,1)S(1)} %pack.1), channel_id=1, source_target_pairs={{0,12},{4,0},{8,4},{12,8},{1,13},{5,1},{9,5},{13,9},{2,14},{6,2},{... | collective-permute-start | bytes 153608 | tf_op jit(solution)/shard_map/ppermute | solution.py:333
  8.0 3.2 %collective-permute-start.3 = (s32[4,10]{1,0:T(4,128)}, s32[4,10]{1,0:T(4,128)S(1)}, u32[]{:S(2)}, u32[]{:S(2)}) collective-permute-start(s32[4,10]{1,0:T(4,128)} %sids_in.1), channel_id=1, source_target_pairs={{0,3},{1,2},{2,1},{3,0},{4,7},{5,6},{6,5},{7,4},{8,11},{9,10},{10,... | collective-permute-start | bytes 488 | tf_op jit(solution)/shard_map/ppermute | solution.py:287
  11.2 1.5 %collective-permute-start.4 = (bf16[4,200,128]{2,1,0:T(8,128)(2,1)S(1)}, bf16[4,200,128]{2,1,0:T(8,128)(2,1)S(1)}, u32[]{:S(2)}, u32[]{:S(2)}) collective-permute-start(bf16[4,200,128]{2,1,0:T(8,128)(2,1)S(1)} %pad_maximum_fusion.args_0_), channel_id=1, source_target_pairs={{0,1},{1,0},{2,3},{3,2},{4,5},{5,4},{6,7},{7,6},{8,9},{9,8},{10,11... | collective-permute-start | bytes 614408 | tf_op jit(solution)/shard_map/ppermute | solution.py:281
  13.0 4.8 %collective-permute-start.5 = (bf16[80,512]{1,0:T(8,128)(2,1)S(1)}, bf16[80,512]{1,0:T(8,128)(2,1)S(1)}, u32[]{:S(2)}, u32[]{:S(2)}) collective-permute-start(bf16[80,512]{1,0:T(8,128)(2,1)S(1)} %get-tuple-element.43), channel_id=1, source_target_pairs={{0,3},{1,2},{2,1},{3,0},{4,7},{5,6},{6,5},{7,4},{8,11},{9,10},{10,... | collective-permute-start | bytes 245768 | tf_op jit(solution)/shard_map/ppermute | solution.py:287
  14.5 4.8 %collective-permute-start.6 = (bf16[40,512]{1,0:T(8,128)(2,1)S(1)}, bf16[40,512]{1,0:T(8,128)(2,1)S(1)}, u32[]{:S(2)}, u32[]{:S(2)}) collective-permute-start(bf16[40,512]{1,0:T(8,128)(2,1)S(1)} %get-tuple-element.47), channel_id=1, source_target_pairs={{0,3},{1,2},{2,1},{3,0},{4,7},{5,6},{6,5},{7,4},{8,11},{9,10},{10,... | collective-permute-start | bytes 122888 | tf_op jit(solution)/shard_map/ppermute | solution.py:287
  20.3 1.4 %collective-permute-start.7 = (f32[2,4,256]{2,1,0:T(4,128)S(1)}, f32[2,4,256]{2,1,0:T(4,128)S(1)}, u32[]{:S(2)}, u32[]{:S(2)}) collective-permute-start(f32[2,4,256]{2,1,0:T(4,128)S(1)} %bitcast.18), channel_id=1, source_target_pairs={{0,1},{1,0},{2,3},{3,2},{4,5},{5,4},{6,7},{7,6},{8,9},{9,8},{10,11... | collective-permute-start | bytes 24584 | tf_op jit(solution)/shard_map/ppermute | solution.py:281
  21.7 3.0 %collective-permute-start.8 = (f32[4,256]{1,0:T(4,128)S(1)}, f32[4,256]{1,0:T(4,128)S(1)}, u32[]{:S(2)}, u32[]{:S(2)}) collective-permute-start(f32[4,256]{1,0:T(4,128)S(1)} %slice_bitcast_fusion.1), channel_id=1, source_target_pairs={{0,3},{1,2},{2,1},{3,0},{4,7},{5,6},{6,5},{7,4},{8,11},{9,10},{10,... | collective-permute-start | bytes 12296 | tf_op jit(solution)/shard_map/ppermute | solution.py:287

commit v12 on v11

--- a/solution.py
+++ b/solution.py
@@ -338,7 +338,7 @@
     reach = round_up(taps + LANES - 1, LANES)
     depth = round_up(taps + SPAN - 1, LANES)
     groups = comps * js
-    first, second = max(groups // 15, 1), groups // 5
+    first, second = groups * 4 // 15, groups // 5
 
     def bank(size):
         return jax.ShapeDtypeStruct((size, depth, count * SPAN), jnp.bfloat16)

time: 25.5 us -> 25.8 us (1.012)
  starting transfers between devices: 11.2 us -> 11.5 us
    pallas_call x1, Pallas kernels: 2.68 us -> 1.95 us  [on_device(): pl.pallas_call(functools.partial(filters_kernel, first + second), out_sha...]
    ppermute x2, starting transfers between devices: 0.72 us -> 1.4 us  [swapped(): lax.ppermute(value, axis, [(i, i ^ distance) for i in range(lax.axis_size...]
    pallas_call x1, Pallas kernels: 1.43 us -> 2.05 us  [on_device(): pl.pallas_call(tables_kernel, out_shape=[column_type, column_type, jax.Sh...]
    ppermute x4, starting transfers between devices: 3.43 us -> 3.1 us  [crossed(): lax.ppermute(value, ('slab', 'sub'), [(i, i ^ distance * nsub + nsub - 1)...]
  transfers between devices with their start and end apart: 9 -> 9, of which waited for: 4 -> 4; matrix products, arithmetic and copies ran while one was open for 0% -> 0% of each run, Pallas kernels for 29% -> 28%
where the time goes in v12:
time: 25.8 us; the launch traced here: 25.6 us
  starting transfers between devices  11.5 us (45%)
  Pallas kernels  9.21 us (36%)
  waiting for transfers between devices  4.18 us (16%)
  other arithmetic  0.65 us (3%)
    ppermute x3, starting transfers between devices, on_device(): lax.ppermute(block, 'tmpl', [(i, (i + d) % ntmpl) for i in range(ntmpl)])  7.01 us
    ppermute x4, waiting for transfers between devices, crossed(): lax.ppermute(value, ('slab', 'sub'), [(i, i ^ distance * nsub + nsub - 1)...  3.34 us
    ppermute x4, starting transfers between devices, crossed(): lax.ppermute(value, ('slab', 'sub'), [(i, i ^ distance * nsub + nsub - 1)...  3.1 us
    pallas_call x2, Pallas kernels, correlate(): pl.pallas_call(functools.partial(correlate_kernel, nslab, nsub, taps, 3,...  2.47 us
    pallas_call x1, Pallas kernels, on_device(): pl.pallas_call(tables_kernel, out_shape=[column_type, column_type, jax.Sh...  2.05 us
    pallas_call x1, Pallas kernels, on_device(): pl.pallas_call(functools.partial(filters_kernel, first + second), out_sha...  1.95 us
    ppermute x2, starting transfers between devices, swapped(): lax.ppermute(value, axis, [(i, i ^ distance) for i in range(lax.axis_size...  1.4 us
    pallas_call x1, Pallas kernels, on_device(): pl.pallas_call(functools.partial(middle_kernel, first, nslab - 1), out_sh...  1.28 us
  transfers between devices with their start and end apart: 9, of which 4 were waited for; matrix products, arithmetic and copies ran while one was open for 0% of the time, Pallas kernels for 28%

profile of v12, /device:TPU:0, one launch (start us, length us, event | category | flops | bytes accessed | tf_op | source)
XLA Modules:
  0.0 25.6 jit_solution(5288090048037610411)
XLA Ops:
  0.0 0.9 %pack.1 = bf16[200,128]{1,0:T(8,128)(2,1)S(1)} custom-call(s32[32]{0:T(128)} %owner_slots.1, bf16[3,32,512]{2,1,0:T(8,128)(2,1)} %bitcast.19), custom_call_target="tpu_custom_call" | custom-call | tf_op jit(solution)/shard_map/pack/pallas_call | solution.py:312
  1.0 3.1 %collective-permute-start = (bf16[200,128]{1,0:T(8,128)(2,1)S(1)}, bf16[200,128]{1,0:T(8,128)(2,1)S(1)}, u32[]{:S(2)}, u32[]{:S(2)}) collective-permute-start(bf16[200,128]{1,0:T(8,128)(2,1)S(1)} %pack.1), channel_id=1, source_target_pairs={{0,4},{4,8},{8,12},{12,0},{1,5},{5,9},{9,13},{13,1},{2,6},{6,10},{... | collective-permute-start | bytes 153608 | tf_op jit(solution)/shard_map/ppermute | solution.py:333
  4.0 2.6 %collective-permute-start.1 = (bf16[200,128]{1,0:T(8,128)(2,1)S(1)}, bf16[200,128]{1,0:T(8,128)(2,1)S(1)}, u32[]{:S(2)}, u32[]{:S(2)}) collective-permute-start(bf16[200,128]{1,0:T(8,128)(2,1)S(1)} %pack.1), channel_id=1, source_target_pairs={{0,8},{4,12},{8,0},{12,4},{1,9},{5,13},{9,1},{13,5},{2,10},{6,14},... | collective-permute-start | bytes 153608 | tf_op jit(solution)/shard_map/ppermute | solution.py:333
  6.6 1.3 %collective-permute-start.2 = (bf16[200,128]{1,0:T(8,128)(2,1)S(1)}, bf16[200,128]{1,0:T(8,128)(2,1)S(1)}, u32[]{:S(2)}, u32[]{:S(2)}) collective-permute-start(bf16[200,128]{1,0:T(8,128)(2,1)S(1)} %pack.1), channel_id=1, source_target_pairs={{0,12},{4,0},{8,4},{12,8},{1,13},{5,1},{9,5},{13,9},{2,14},{6,2},{... | collective-permute-start | bytes 153608 | tf_op jit(solution)/shard_map/ppermute | solution.py:333
  8.0 0.1 collective-permute-start.3
  8.1 2.1 %tables.1 = (s32[40,128]{1,0:T(8,128)S(1)}, s32[40,128]{1,0:T(8,128)S(1)}, f32[40,1024]{1,0:T(8,128)S(1)}, bf16[256,512]{1,0:T(8,128)(2,1)S(1)}, f32[120,128]{1,...) custom-call(s32[4,10]{1,0:T(4,128)} %sids_in.1, s32[4,10]{1,0:T(4,128)} %offs_in.1, ...), custom_call_target="tpu_custom_call" | custom-call | tf_op jit(solution)/shard_map/tables/pallas_call | solution.py:347
  10.1 1.1 %collective-permute-done.3.args_0_ = s32[4,10]{1,0:T(4,128)S(1)} collective-permute-done((s32[4,10]{1,0:T(4,128)}, s32[4,10]{1,0:T(4,128)S(1)}, u32[]{:S(2)}, u32[]{:S(2)}) %collective-permute-start.3) | collective-permute-done | bytes 192 | tf_op jit(solution)/shard_map/ppermute | solution.py:287
  11.2 0.0 collective-permute-done
  11.2 0.0 collective-permute-done.1
  11.2 0.0 collective-permute-done.2
  11.2 0.5 %collective-permute-start.4 = (bf16[4,200,128]{2,1,0:T(8,128)(2,1)S(1)}, bf16[4,200,128]{2,1,0:T(8,128)(2,1)S(1)}, u32[]{:S(2)}, u32[]{:S(2)}) collective-permute-start(bf16[4,200,128]{2,1,0:T(8,128)(2,1)S(1)} %pad_maximum_fusion.args_0_), channel_id=1, source_target_pairs={{0,1},{1,0},{2,3},{3,2},{4,5},{5,4},{6,7},{7,6},{8,9},{9,8},{10,11... | collective-permute-start | bytes 614408 | tf_op jit(solution)/shard_map/ppermute | solution.py:281
  11.8 1.3 %middle.1 = (s32[40,128]{1,0:T(8,128)S(1)}, bf16[6,384,256]{2,1,0:T(8,128)(2,1)S(1)}) custom-call(s32[4,10]{1,0:T(4,128)S(1)} %collective-permute-done.3.args_0_, bf16[10,3,4,300]{3,2,1,0:T(4,128)(2,1)S(1)} %get-tuple-element.37.args_1_.waves), custom_call_target="tpu_custom_call" | custom-call | tf_op jit(solution)/shard_map/middle/pallas_call | solution.py:373
  13.1 0.0 collective-permute-done.4.args_1_
  13.1 0.3 %select.2 = (bf16[80,512]{1,0:T(8,128)(2,1)S(1)}, bf16[40,512]{1,0:T(8,128)(2,1)S(1)}) custom-call(bf16[4,200,128]{2,1,0:T(8,128)(2,1)S(1)} %pad_maximum_fusion.args_0_, bf16[4,200,128]{2,1,0:T(8,128)(2,1)S(1)} %collective-permute-done.4.args_1_, s32[40,128]{1,0:T(8,128)S(1)} %get-tuple-element.42.args_2_), custom_call_target="tpu_custom_call" | custom-call | tf_op jit(solution)/shard_map/select/pallas_call | solution.py:385
  13.3 1.2 %collective-permute-start.5 = (bf16[80,512]{1,0:T(8,128)(2,1)S(1)}, bf16[80,512]{1,0:T(8,128)(2,1)S(1)}, u32[]{:S(2)}, u32[]{:S(2)}) collective-permute-start(bf16[80,512]{1,0:T(8,128)(2,1)S(1)} %get-tuple-element.43), channel_id=1, source_target_pairs={{0,3},{1,2},{2,1},{3,0},{4,7},{5,6},{6,5},{7,4},{8,11},{9,10},{10,... | collective-permute-start | bytes 245768 | tf_op jit(solution)/shard_map/ppermute | solution.py:287
  14.5 0.6 %collective-permute-start.6 = (bf16[40,512]{1,0:T(8,128)(2,1)S(1)}, bf16[40,512]{1,0:T(8,128)(2,1)S(1)}, u32[]{:S(2)}, u32[]{:S(2)}) collective-permute-start(bf16[40,512]{1,0:T(8,128)(2,1)S(1)} %get-tuple-element.47), channel_id=1, source_target_pairs={{0,3},{1,2},{2,1},{3,0},{4,7},{5,6},{6,5},{7,4},{8,11},{9,10},{10,... | collective-permute-start | bytes 122888 | tf_op jit(solution)/shard_map/ppermute | solution.py:287
  15.2 1.9 %filters.1.args_4_ = bf16[16,384,256]{2,1,0:T(8,128)(2,1)S(1)} custom-call(bf16[10,3,4,300]{3,2,1,0:T(4,128)(2,1)S(1)} %get-tuple-element.37.args_1_.waves), custom_call_target="tpu_custom_call" | custom-call | tf_op jit(solution)/shard_map/filters/pallas_call | solution.py:398
  17.1 0.3 %select.3.args_0_ = f32[120,512]{1,0:T(8,128)S(1)} custom-call(bf16[4,200,128]{2,1,0:T(8,128)(2,1)S(1)} %pad_maximum_fusion.args_0_, bf16[4,200,128]{2,1,0:T(8,128)(2,1)S(1)} %collective-permute-done.4.args_1_, s32[40,128]{1,0:T(8,128)S(1)} %get-tuple-element.44.args_2_, f32[40,1024]{1,0:T(8,128)S(1)} %get-tuple-element.45.args_3_.args_6_.args_7_), custom_call_target="tpu_custom_call" | custom-call | tf_op jit(solution)/shard_map/select/pallas_call | solution.py:385
  17.4 0.4 %collective-permute-done.5.args_1_ = bf16[80,512]{1,0:T(8,128)(2,1)S(1)} collective-permute-done((bf16[80,512]{1,0:T(8,128)(2,1)S(1)}, bf16[80,512]{1,0:T(8,128)(2,1)S(1)}, u32[]{:S(2)}, u32[]{:S(2)}) %collective-permute-start.5) | collective-permute-done | bytes 81952 | tf_op jit(solution)/shard_map/ppermute | solution.py:287
  17.8 1.5 %correlate.2.args_5_ = f32[4,8,128]{2,1,0:T(8,128)S(1)} custom-call(f32[120,512]{1,0:T(8,128)S(1)} %select.3.args_0_, bf16[80,512]{1,0:T(8,128)(2,1)S(1)} %collective-permute-done.5.args_1_, bf16[8,384,256]{2,1,0:T(8,128)(2,1)S(1)} %get-tuple-element.48.args_2_, bf16[6,384,256]{2,1,0:T(8,128)(2,1)S(1)} %get-tuple-element.49.args_3_, ...), custom_call_target="tpu_custom_call" | custom-call | tf_op jit(solution)/shard_map/correlate/pallas_call | solution.py:429
  19.4 0.0 collective-permute-done.6.args_1_
  19.4 0.9 %correlate.3 = (f32[2,4,256]{2,1,0:T(4,128)S(1)}, f32[1,2,4,256]{3,2,1,0:T(4,128)S(1)}) custom-call(f32[120,512]{1,0:T(8,128)S(1)} %select.3.args_0_, bf16[40,512]{1,0:T(8,128)(2,1)S(1)} %collective-permute-done.6.args_1_, bf16[8,384,256]{2,1,0:T(8,128)(2,1)S(1)} %get-tuple-element.48.args_2_, bf16[6,384,256]{2,1,0:T(8,128)(2,1)S(1)} %get-tuple-element.49.args_3_, ...), custom_call_target="tpu_custom_call" | custom-call | tf_op jit(solution)/shard_map/correlate/pallas_call | solution.py:429
  20.3 0.9 %collective-permute-start.7 = (f32[2,4,256]{2,1,0:T(4,128)S(1)}, f32[2,4,256]{2,1,0:T(4,128)S(1)}, u32[]{:S(2)}, u32[]{:S(2)}) collective-permute-start(f32[2,4,256]{2,1,0:T(4,128)S(1)} %bitcast.18), channel_id=1, source_target_pairs={{0,1},{1,0},{2,3},{3,2},{4,5},{5,4},{6,7},{7,6},{8,9},{9,8},{10,11... | collective-permute-start | bytes 24584 | tf_op jit(solution)/shard_map/ppermute | solution.py:281
  21.2 0.8 %collective-permute-done.7 = f32[2,4,256]{2,1,0:T(4,128)S(1)} collective-permute-done((f32[2,4,256]{2,1,0:T(4,128)S(1)}, f32[2,4,256]{2,1,0:T(4,128)S(1)}, u32[]{:S(2)}, u32[]{:S(2)}) %collective-permute-start.7) | collective-permute-done | bytes 8224 | tf_op jit(solution)/shard_map/ppermute | solution.py:281
  22.0 1.2 %collective-permute-start.8 = (f32[4,256]{1,0:T(4,128)S(1)}, f32[4,256]{1,0:T(4,128)S(1)}, u32[]{:S(2)}, u32[]{:S(2)}) collective-permute-start(f32[4,256]{1,0:T(4,128)S(1)} %slice_bitcast_fusion.1), channel_id=1, source_target_pairs={{0,3},{1,2},{2,1},{3,0},{4,7},{5,6},{6,5},{7,4},{8,11},{9,10},{10,... | collective-permute-start | bytes 12296 | tf_op jit(solution)/shard_map/ppermute | solution.py:287
  23.2 1.8 %collective-permute-done.8 = f32[4,256]{1,0:T(4,128)S(1)} collective-permute-done((f32[4,256]{1,0:T(4,128)S(1)}, f32[4,256]{1,0:T(4,128)S(1)}, u32[]{:S(2)}, u32[]{:S(2)}) %collective-permute-start.8) | collective-permute-done | bytes 4128 | tf_op jit(solution)/shard_map/ppermute | solution.py:287
  25.0 0.6 %pad_maximum_fusion.1 = f32[8,256]{1,0:T(8,128)} fusion(f32[4,256]{1,0:T(4,128)S(1)} %get-tuple-element.58, f32[4,256]{1,0:T(4,128)S(1)} %get-tuple-element.57), kind=kLoop, calls=%fused_computation.1 | loop fusion | flops 2048 | bytes 16384 | tf_op jit(solution)/shard_map/concatenate | solution.py:452
  (4 shorter events, 0.0 us)
Async XLA Ops:
  1.0 10.2 %collective-permute-start = (bf16[200,128]{1,0:T(8,128)(2,1)S(1)}, bf16[200,128]{1,0:T(8,128)(2,1)S(1)}, u32[]{:S(2)}, u32[]{:S(2)}) collective-permute-start(bf16[200,128]{1,0:T(8,128)(2,1)S(1)} %pack.1), channel_id=1, source_target_pairs={{0,4},{4,8},{8,12},{12,0},{1,5},{5,9},{9,13},{13,1},{2,6},{6,10},{... | collective-permute-start | bytes 153608 | tf_op jit(solution)/shard_map/ppermute | solution.py:333
  4.0 7.2 %collective-permute-start.1 = (bf16[200,128]{1,0:T(8,128)(2,1)S(1)}, bf16[200,128]{1,0:T(8,128)(2,1)S(1)}, u32[]{:S(2)}, u32[]{:S(2)}) collective-permute-start(bf16[200,128]{1,0:T(8,128)(2,1)S(1)} %pack.1), channel_id=1, source_target_pairs={{0,8},{4,12},{8,0},{12,4},{1,9},{5,13},{9,1},{13,5},{2,10},{6,14},... | collective-permute-start | bytes 153608 | tf_op jit(solution)/shard_map/ppermute | solution.py:333
  6.6 4.6 %collective-permute-start.2 = (bf16[200,128]{1,0:T(8,128)(2,1)S(1)}, bf16[200,128]{1,0:T(8,128)(2,1)S(1)}, u32[]{:S(2)}, u32[]{:S(2)}) collective-permute-start(bf16[200,128]{1,0:T(8,128)(2,1)S(1)} %pack.1), channel_id=1, source_target_pairs={{0,12},{4,0},{8,4},{12,8},{1,13},{5,1},{9,5},{13,9},{2,14},{6,2},{... | collective-permute-start | bytes 153608 | tf_op jit(solution)/shard_map/ppermute | solution.py:333
  8.0 3.2 %collective-permute-start.3 = (s32[4,10]{1,0:T(4,128)}, s32[4,10]{1,0:T(4,128)S(1)}, u32[]{:S(2)}, u32[]{:S(2)}) collective-permute-start(s32[4,10]{1,0:T(4,128)} %sids_in.1), channel_id=1, source_target_pairs={{0,3},{1,2},{2,1},{3,0},{4,7},{5,6},{6,5},{7,4},{8,11},{9,10},{10,... | collective-permute-start | bytes 488 | tf_op jit(solution)/shard_map/ppermute | solution.py:287
  11.2 1.8 %collective-permute-start.4 = (bf16[4,200,128]{2,1,0:T(8,128)(2,1)S(1)}, bf16[4,200,128]{2,1,0:T(8,128)(2,1)S(1)}, u32[]{:S(2)}, u32[]{:S(2)}) collective-permute-start(bf16[4,200,128]{2,1,0:T(8,128)(2,1)S(1)} %pad_maximum_fusion.args_0_), channel_id=1, source_target_pairs={{0,1},{1,0},{2,3},{3,2},{4,5},{5,4},{6,7},{7,6},{8,9},{9,8},{10,11... | collective-permute-start | bytes 614408 | tf_op jit(solution)/shard_map/ppermute | solution.py:281
  13.3 4.5 %collective-permute-start.5 = (bf16[80,512]{1,0:T(8,128)(2,1)S(1)}, bf16[80,512]{1,0:T(8,128)(2,1)S(1)}, u32[]{:S(2)}, u32[]{:S(2)}) collective-permute-start(bf16[80,512]{1,0:T(8,128)(2,1)S(1)} %get-tuple-element.43), channel_id=1, source_target_pairs={{0,3},{1,2},{2,1},{3,0},{4,7},{5,6},{6,5},{7,4},{8,11},{9,10},{10,... | collective-permute-start | bytes 245768 | tf_op jit(solution)/shard_map/ppermute | solution.py:287
  14.5 4.8 %collective-permute-start.6 = (bf16[40,512]{1,0:T(8,128)(2,1)S(1)}, bf16[40,512]{1,0:T(8,128)(2,1)S(1)}, u32[]{:S(2)}, u32[]{:S(2)}) collective-permute-start(bf16[40,512]{1,0:T(8,128)(2,1)S(1)} %get-tuple-element.47), channel_id=1, source_target_pairs={{0,3},{1,2},{2,1},{3,0},{4,7},{5,6},{6,5},{7,4},{8,11},{9,10},{10,... | collective-permute-start | bytes 122888 | tf_op jit(solution)/shard_map/ppermute | solution.py:287
  20.3 1.7 %collective-permute-start.7 = (f32[2,4,256]{2,1,0:T(4,128)S(1)}, f32[2,4,256]{2,1,0:T(4,128)S(1)}, u32[]{:S(2)}, u32[]{:S(2)}) collective-permute-start(f32[2,4,256]{2,1,0:T(4,128)S(1)} %bitcast.18), channel_id=1, source_target_pairs={{0,1},{1,0},{2,3},{3,2},{4,5},{5,4},{6,7},{7,6},{8,9},{9,8},{10,11... | collective-permute-start | bytes 24584 | tf_op jit(solution)/shard_map/ppermute | solution.py:281
  22.0 3.0 %collective-permute-start.8 = (f32[4,256]{1,0:T(4,128)S(1)}, f32[4,256]{1,0:T(4,128)S(1)}, u32[]{:S(2)}, u32[]{:S(2)}) collective-permute-start(f32[4,256]{1,0:T(4,128)S(1)} %slice_bitcast_fusion.1), channel_id=1, source_target_pairs={{0,3},{1,2},{2,1},{3,0},{4,7},{5,6},{6,5},{7,4},{8,11},{9,10},{10,... | collective-permute-start | bytes 12296 | tf_op jit(solution)/shard_map/ppermute | solution.py:287

commit v13 on v12

--- a/solution.py
+++ b/solution.py
@@ -338,7 +338,7 @@
     reach = round_up(taps + LANES - 1, LANES)
     depth = round_up(taps + SPAN - 1, LANES)
     groups = comps * js
-    first, second = groups * 4 // 15, groups // 5
+    first, second = max(groups // 6, 1), groups // 5
 
     def bank(size):
         return jax.ShapeDtypeStruct((size, depth, count * SPAN), jnp.bfloat16)

time: 25.8 us -> 25.5 us (0.988)
  waiting for transfers between devices: 4.18 us -> 3.74 us
    ppermute x4, waiting for transfers between devices: 3.34 us -> 2.9 us  [crossed(): lax.ppermute(value, ('slab', 'sub'), [(i, i ^ distance * nsub + nsub - 1)...]
    pallas_call x1, Pallas kernels: 1.95 us -> 2.37 us  [on_device(): pl.pallas_call(functools.partial(filters_kernel, first + second), out_sha...]
    ppermute x2, starting transfers between devices: 1.4 us -> 1.08 us  [swapped(): lax.ppermute(value, axis, [(i, i ^ distance) for i in range(lax.axis_size...]
    ppermute x4, starting transfers between devices: 3.1 us -> 3.41 us  [crossed(): lax.ppermute(value, ('slab', 'sub'), [(i, i ^ distance * nsub + nsub - 1)...]
    pallas_call x1, Pallas kernels: 2.05 us -> 1.75 us  [on_device(): pl.pallas_call(tables_kernel, out_shape=[column_type, column_type, jax.Sh...]
  transfers between devices with their start and end apart: 9 -> 9, of which waited for: 4 -> 3; matrix products, arithmetic and copies ran while one was open for 0% -> 0% of each run, Pallas kernels for 28% -> 29%
where the time goes in v13:
time: 25.5 us; the launch traced here: 25.3 us
  starting transfers between devices  11.5 us (45%)
  Pallas kernels  9.35 us (37%)
  waiting for transfers between devices  3.74 us (15%)
  other arithmetic  0.65 us (3%)
    ppermute x3, starting transfers between devices, on_device(): lax.ppermute(block, 'tmpl', [(i, (i + d) % ntmpl) for i in range(ntmpl)])  7.01 us
    ppermute x4, starting transfers between devices, crossed(): lax.ppermute(value, ('slab', 'sub'), [(i, i ^ distance * nsub + nsub - 1)...  3.41 us
    ppermute x4, waiting for transfers between devices, crossed(): lax.ppermute(value, ('slab', 'sub'), [(i, i ^ distance * nsub + nsub - 1)...  2.9 us
    pallas_call x2, Pallas kernels, correlate(): pl.pallas_call(functools.partial(correlate_kernel, nslab, nsub, taps, 3,...  2.48 us
    pallas_call x1, Pallas kernels, on_device(): pl.pallas_call(functools.partial(filters_kernel, first + second), out_sha...  2.37 us
    pallas_call x1, Pallas kernels, on_device(): pl.pallas_call(tables_kernel, out_shape=[column_type, column_type, jax.Sh...  1.75 us
    pallas_call x1, Pallas kernels, on_device(): pl.pallas_call(functools.partial(middle_kernel, first, nslab - 1), out_sh...  1.28 us
    ppermute x2, starting transfers between devices, swapped(): lax.ppermute(value, axis, [(i, i ^ distance) for i in range(lax.axis_size...  1.08 us
  transfers between devices with their start and end apart: 9, of which 3 were waited for; matrix products, arithmetic and copies ran while one was open for 0% of the time, Pallas kernels for 29%

profile of v13, /device:TPU:0, one launch (start us, length us, event | category | flops | bytes accessed | tf_op | source)
XLA Modules:
  0.0 25.3 jit_solution(7530445550608363724)
XLA Ops:
  0.0 0.9 %pack.1 = bf16[200,128]{1,0:T(8,128)(2,1)S(1)} custom-call(s32[32]{0:T(128)} %owner_slots.1, bf16[3,32,512]{2,1,0:T(8,128)(2,1)} %bitcast.19), custom_call_target="tpu_custom_call" | custom-call | tf_op jit(solution)/shard_map/pack/pallas_call | solution.py:312
  1.0 3.1 %collective-permute-start = (bf16[200,128]{1,0:T(8,128)(2,1)S(1)}, bf16[200,128]{1,0:T(8,128)(2,1)S(1)}, u32[]{:S(2)}, u32[]{:S(2)}) collective-permute-start(bf16[200,128]{1,0:T(8,128)(2,1)S(1)} %pack.1), channel_id=1, source_target_pairs={{0,4},{4,8},{8,12},{12,0},{1,5},{5,9},{9,13},{13,1},{2,6},{6,10},{... | collective-permute-start | bytes 153608 | tf_op jit(solution)/shard_map/ppermute | solution.py:333
  4.0 2.6 %collective-permute-start.1 = (bf16[200,128]{1,0:T(8,128)(2,1)S(1)}, bf16[200,128]{1,0:T(8,128)(2,1)S(1)}, u32[]{:S(2)}, u32[]{:S(2)}) collective-permute-start(bf16[200,128]{1,0:T(8,128)(2,1)S(1)} %pack.1), channel_id=1, source_target_pairs={{0,8},{4,12},{8,0},{12,4},{1,9},{5,13},{9,1},{13,5},{2,10},{6,14},... | collective-permute-start | bytes 153608 | tf_op jit(solution)/shard_map/ppermute | solution.py:333
  6.6 1.3 %collective-permute-start.2 = (bf16[200,128]{1,0:T(8,128)(2,1)S(1)}, bf16[200,128]{1,0:T(8,128)(2,1)S(1)}, u32[]{:S(2)}, u32[]{:S(2)}) collective-permute-start(bf16[200,128]{1,0:T(8,128)(2,1)S(1)} %pack.1), channel_id=1, source_target_pairs={{0,12},{4,0},{8,4},{12,8},{1,13},{5,1},{9,5},{13,9},{2,14},{6,2},{... | collective-permute-start | bytes 153608 | tf_op jit(solution)/shard_map/ppermute | solution.py:333
  8.0 0.1 collective-permute-start.3
  8.1 1.7 %tables.1 = (s32[40,128]{1,0:T(8,128)S(1)}, s32[40,128]{1,0:T(8,128)S(1)}, f32[40,1024]{1,0:T(8,128)S(1)}, bf16[256,512]{1,0:T(8,128)(2,1)S(1)}, f32[120,128]{1,...) custom-call(s32[4,10]{1,0:T(4,128)} %sids_in.1, s32[4,10]{1,0:T(4,128)} %offs_in.1, ...), custom_call_target="tpu_custom_call" | custom-call | tf_op jit(solution)/shard_map/tables/pallas_call | solution.py:347
  9.8 1.4 %collective-permute-done.3.args_0_ = s32[4,10]{1,0:T(4,128)S(1)} collective-permute-done((s32[4,10]{1,0:T(4,128)}, s32[4,10]{1,0:T(4,128)S(1)}, u32[]{:S(2)}, u32[]{:S(2)}) %collective-permute-start.3) | collective-permute-done | bytes 192 | tf_op jit(solution)/shard_map/ppermute | solution.py:287
  11.2 0.0 collective-permute-done
  11.2 0.0 collective-permute-done.1
  11.2 0.0 collective-permute-done.2
  11.2 0.2 collective-permute-start.4
  11.5 1.3 %middle.1 = (s32[40,128]{1,0:T(8,128)S(1)}, bf16[6,384,256]{2,1,0:T(8,128)(2,1)S(1)}) custom-call(s32[4,10]{1,0:T(4,128)S(1)} %collective-permute-done.3.args_0_, bf16[10,3,4,300]{3,2,1,0:T(4,128)(2,1)S(1)} %get-tuple-element.37.args_1_.waves), custom_call_target="tpu_custom_call" | custom-call | tf_op jit(solution)/shard_map/middle/pallas_call | solution.py:373
  12.8 0.0 collective-permute-done.4.args_1_
  12.8 0.3 %select.2 = (bf16[80,512]{1,0:T(8,128)(2,1)S(1)}, bf16[40,512]{1,0:T(8,128)(2,1)S(1)}) custom-call(bf16[4,200,128]{2,1,0:T(8,128)(2,1)S(1)} %pad_maximum_fusion.args_0_, bf16[4,200,128]{2,1,0:T(8,128)(2,1)S(1)} %collective-permute-done.4.args_1_, s32[40,128]{1,0:T(8,128)S(1)} %get-tuple-element.42.args_2_), custom_call_target="tpu_custom_call" | custom-call | tf_op jit(solution)/shard_map/select/pallas_call | solution.py:385
  13.0 1.5 %collective-permute-start.5 = (bf16[80,512]{1,0:T(8,128)(2,1)S(1)}, bf16[80,512]{1,0:T(8,128)(2,1)S(1)}, u32[]{:S(2)}, u32[]{:S(2)}) collective-permute-start(bf16[80,512]{1,0:T(8,128)(2,1)S(1)} %get-tuple-element.43), channel_id=1, source_target_pairs={{0,3},{1,2},{2,1},{3,0},{4,7},{5,6},{6,5},{7,4},{8,11},{9,10},{10,... | collective-permute-start | bytes 245768 | tf_op jit(solution)/shard_map/ppermute | solution.py:287
  14.5 0.3 %collective-permute-start.6 = (bf16[40,512]{1,0:T(8,128)(2,1)S(1)}, bf16[40,512]{1,0:T(8,128)(2,1)S(1)}, u32[]{:S(2)}, u32[]{:S(2)}) collective-permute-start(bf16[40,512]{1,0:T(8,128)(2,1)S(1)} %get-tuple-element.47), channel_id=1, source_target_pairs={{0,3},{1,2},{2,1},{3,0},{4,7},{5,6},{6,5},{7,4},{8,11},{9,10},{10,... | collective-permute-start | bytes 122888 | tf_op jit(solution)/shard_map/ppermute | solution.py:287
  14.9 2.4 %filters.1.args_4_ = bf16[19,384,256]{2,1,0:T(8,128)(2,1)S(1)} custom-call(bf16[10,3,4,300]{3,2,1,0:T(4,128)(2,1)S(1)} %get-tuple-element.37.args_1_.waves), custom_call_target="tpu_custom_call" | custom-call | tf_op jit(solution)/shard_map/filters/pallas_call | solution.py:398
  17.2 0.3 %select.3.args_0_ = f32[120,512]{1,0:T(8,128)S(1)} custom-call(bf16[4,200,128]{2,1,0:T(8,128)(2,1)S(1)} %pad_maximum_fusion.args_0_, bf16[4,200,128]{2,1,0:T(8,128)(2,1)S(1)} %collective-permute-done.4.args_1_, s32[40,128]{1,0:T(8,128)S(1)} %get-tuple-element.44.args_2_, f32[40,1024]{1,0:T(8,128)S(1)} %get-tuple-element.45.args_3_.args_6_.args_7_), custom_call_target="tpu_custom_call" | custom-call | tf_op jit(solution)/shard_map/select/pallas_call | solution.py:385
  17.5 0.0 collective-permute-done.5.args_1_
  17.5 1.5 %correlate.2.args_5_ = f32[4,8,128]{2,1,0:T(8,128)S(1)} custom-call(f32[120,512]{1,0:T(8,128)S(1)} %select.3.args_0_, bf16[80,512]{1,0:T(8,128)(2,1)S(1)} %collective-permute-done.5.args_1_, bf16[5,384,256]{2,1,0:T(8,128)(2,1)S(1)} %get-tuple-element.48.args_2_, bf16[6,384,256]{2,1,0:T(8,128)(2,1)S(1)} %get-tuple-element.49.args_3_, ...), custom_call_target="tpu_custom_call" | custom-call | tf_op jit(solution)/shard_map/correlate/pallas_call | solution.py:429
  19.1 0.0 collective-permute-done.6.args_1_
  19.1 0.9 %correlate.3 = (f32[2,4,256]{2,1,0:T(4,128)S(1)}, f32[1,2,4,256]{3,2,1,0:T(4,128)S(1)}) custom-call(f32[120,512]{1,0:T(8,128)S(1)} %select.3.args_0_, bf16[40,512]{1,0:T(8,128)(2,1)S(1)} %collective-permute-done.6.args_1_, bf16[5,384,256]{2,1,0:T(8,128)(2,1)S(1)} %get-tuple-element.48.args_2_, bf16[6,384,256]{2,1,0:T(8,128)(2,1)S(1)} %get-tuple-element.49.args_3_, ...), custom_call_target="tpu_custom_call" | custom-call | tf_op jit(solution)/shard_map/correlate/pallas_call | solution.py:429
  20.0 0.8 %collective-permute-start.7 = (f32[2,4,256]{2,1,0:T(4,128)S(1)}, f32[2,4,256]{2,1,0:T(4,128)S(1)}, u32[]{:S(2)}, u32[]{:S(2)}) collective-permute-start(f32[2,4,256]{2,1,0:T(4,128)S(1)} %bitcast.18), channel_id=1, source_target_pairs={{0,1},{1,0},{2,3},{3,2},{4,5},{5,4},{6,7},{7,6},{8,9},{9,8},{10,11... | collective-permute-start | bytes 24584 | tf_op jit(solution)/shard_map/ppermute | solution.py:281
  20.9 0.8 %collective-permute-done.7 = f32[2,4,256]{2,1,0:T(4,128)S(1)} collective-permute-done((f32[2,4,256]{2,1,0:T(4,128)S(1)}, f32[2,4,256]{2,1,0:T(4,128)S(1)}, u32[]{:S(2)}, u32[]{:S(2)}) %collective-permute-start.7) | collective-permute-done | bytes 8224 | tf_op jit(solution)/shard_map/ppermute | solution.py:281
  21.7 1.5 %collective-permute-start.8 = (f32[4,256]{1,0:T(4,128)S(1)}, f32[4,256]{1,0:T(4,128)S(1)}, u32[]{:S(2)}, u32[]{:S(2)}) collective-permute-start(f32[4,256]{1,0:T(4,128)S(1)} %slice_bitcast_fusion.1), channel_id=1, source_target_pairs={{0,3},{1,2},{2,1},{3,0},{4,7},{5,6},{6,5},{7,4},{8,11},{9,10},{10,... | collective-permute-start | bytes 12296 | tf_op jit(solution)/shard_map/ppermute | solution.py:287
  23.2 1.5 %collective-permute-done.8 = f32[4,256]{1,0:T(4,128)S(1)} collective-permute-done((f32[4,256]{1,0:T(4,128)S(1)}, f32[4,256]{1,0:T(4,128)S(1)}, u32[]{:S(2)}, u32[]{:S(2)}) %collective-permute-start.8) | collective-permute-done | bytes 4128 | tf_op jit(solution)/shard_map/ppermute | solution.py:287
  24.7 0.6 %pad_maximum_fusion.1 = f32[8,256]{1,0:T(8,128)} fusion(f32[4,256]{1,0:T(4,128)S(1)} %get-tuple-element.58, f32[4,256]{1,0:T(4,128)S(1)} %get-tuple-element.57), kind=kLoop, calls=%fused_computation.1 | loop fusion | flops 2048 | bytes 16384 | tf_op jit(solution)/shard_map/concatenate | solution.py:452
  (4 shorter events, 0.0 us)
Async XLA Ops:
  1.0 10.2 %collective-permute-start = (bf16[200,128]{1,0:T(8,128)(2,1)S(1)}, bf16[200,128]{1,0:T(8,128)(2,1)S(1)}, u32[]{:S(2)}, u32[]{:S(2)}) collective-permute-start(bf16[200,128]{1,0:T(8,128)(2,1)S(1)} %pack.1), channel_id=1, source_target_pairs={{0,4},{4,8},{8,12},{12,0},{1,5},{5,9},{9,13},{13,1},{2,6},{6,10},{... | collective-permute-start | bytes 153608 | tf_op jit(solution)/shard_map/ppermute | solution.py:333
  4.0 7.2 %collective-permute-start.1 = (bf16[200,128]{1,0:T(8,128)(2,1)S(1)}, bf16[200,128]{1,0:T(8,128)(2,1)S(1)}, u32[]{:S(2)}, u32[]{:S(2)}) collective-permute-start(bf16[200,128]{1,0:T(8,128)(2,1)S(1)} %pack.1), channel_id=1, source_target_pairs={{0,8},{4,12},{8,0},{12,4},{1,9},{5,13},{9,1},{13,5},{2,10},{6,14},... | collective-permute-start | bytes 153608 | tf_op jit(solution)/shard_map/ppermute | solution.py:333
  6.6 4.6 %collective-permute-start.2 = (bf16[200,128]{1,0:T(8,128)(2,1)S(1)}, bf16[200,128]{1,0:T(8,128)(2,1)S(1)}, u32[]{:S(2)}, u32[]{:S(2)}) collective-permute-start(bf16[200,128]{1,0:T(8,128)(2,1)S(1)} %pack.1), channel_id=1, source_target_pairs={{0,12},{4,0},{8,4},{12,8},{1,13},{5,1},{9,5},{13,9},{2,14},{6,2},{... | collective-permute-start | bytes 153608 | tf_op jit(solution)/shard_map/ppermute | solution.py:333
  8.0 3.2 %collective-permute-start.3 = (s32[4,10]{1,0:T(4,128)}, s32[4,10]{1,0:T(4,128)S(1)}, u32[]{:S(2)}, u32[]{:S(2)}) collective-permute-start(s32[4,10]{1,0:T(4,128)} %sids_in.1), channel_id=1, source_target_pairs={{0,3},{1,2},{2,1},{3,0},{4,7},{5,6},{6,5},{7,4},{8,11},{9,10},{10,... | collective-permute-start | bytes 488 | tf_op jit(solution)/shard_map/ppermute | solution.py:287
  11.2 1.5 %collective-permute-start.4 = (bf16[4,200,128]{2,1,0:T(8,128)(2,1)S(1)}, bf16[4,200,128]{2,1,0:T(8,128)(2,1)S(1)}, u32[]{:S(2)}, u32[]{:S(2)}) collective-permute-start(bf16[4,200,128]{2,1,0:T(8,128)(2,1)S(1)} %pad_maximum_fusion.args_0_), channel_id=1, source_target_pairs={{0,1},{1,0},{2,3},{3,2},{4,5},{5,4},{6,7},{7,6},{8,9},{9,8},{10,11... | collective-permute-start | bytes 614408 | tf_op jit(solution)/shard_map/ppermute | solution.py:281
  13.0 4.5 %collective-permute-start.5 = (bf16[80,512]{1,0:T(8,128)(2,1)S(1)}, bf16[80,512]{1,0:T(8,128)(2,1)S(1)}, u32[]{:S(2)}, u32[]{:S(2)}) collective-permute-start(bf16[80,512]{1,0:T(8,128)(2,1)S(1)} %get-tuple-element.43), channel_id=1, source_target_pairs={{0,3},{1,2},{2,1},{3,0},{4,7},{5,6},{6,5},{7,4},{8,11},{9,10},{10,... | collective-permute-start | bytes 245768 | tf_op jit(solution)/shard_map/ppermute | solution.py:287
  14.5 4.5 %collective-permute-start.6 = (bf16[40,512]{1,0:T(8,128)(2,1)S(1)}, bf16[40,512]{1,0:T(8,128)(2,1)S(1)}, u32[]{:S(2)}, u32[]{:S(2)}) collective-permute-start(bf16[40,512]{1,0:T(8,128)(2,1)S(1)} %get-tuple-element.47), channel_id=1, source_target_pairs={{0,3},{1,2},{2,1},{3,0},{4,7},{5,6},{6,5},{7,4},{8,11},{9,10},{10,... | collective-permute-start | bytes 122888 | tf_op jit(solution)/shard_map/ppermute | solution.py:287
  20.0 1.7 %collective-permute-start.7 = (f32[2,4,256]{2,1,0:T(4,128)S(1)}, f32[2,4,256]{2,1,0:T(4,128)S(1)}, u32[]{:S(2)}, u32[]{:S(2)}) collective-permute-start(f32[2,4,256]{2,1,0:T(4,128)S(1)} %bitcast.18), channel_id=1, source_target_pairs={{0,1},{1,0},{2,3},{3,2},{4,5},{5,4},{6,7},{7,6},{8,9},{9,8},{10,11... | collective-permute-start | bytes 24584 | tf_op jit(solution)/shard_map/ppermute | solution.py:281
  21.7 3.0 %collective-permute-start.8 = (f32[4,256]{1,0:T(4,128)S(1)}, f32[4,256]{1,0:T(4,128)S(1)}, u32[]{:S(2)}, u32[]{:S(2)}) collective-permute-start(f32[4,256]{1,0:T(4,128)S(1)} %slice_bitcast_fusion.1), channel_id=1, source_target_pairs={{0,3},{1,2},{2,1},{3,0},{4,7},{5,6},{6,5},{7,4},{8,11},{9,10},{10,... | collective-permute-start | bytes 12296 | tf_op jit(solution)/shard_map/ppermute | solution.py:287
